TPU v7x, 256 devices: a whole 4x4x8 slice. The times are simulated.
256 devices in a mesh: blk: 256 (over z, x, y, core).
Axes of the slice: x: 4, y: 4, z: 8, core: 2. Of those that a mesh axis runs over, the one named last changes fastest.
Arguments:
- embeddings: float32 [196608, 1024], P('blk')
- labels: int32 [196608], P('blk'), may hold values from 0 to 999
Outputs:
- agreement: float32 [196608], P('blk')
- log_weight: float32 [196608], P('blk')
All inputs are finite; a program needn't handle non-finite values.
Results may differ from a plain program's by a relative error of at most 0.00087.
Values may be sent and summed in bfloat16 or wider, within the bound.
No kernel may reach another device: no remote copies, remote signals or barrier semaphores. Data moves between devices by JAX's collectives and lax.ppermute only.
A program may use at most 64 MiB of HBM per device.

v0:
```python
import jax
import jax.numpy as jnp
from jax import lax
from jax.sharding import PartitionSpec as P

STEPS = 4


tau_value = 0.1


def passed_along(block, axis, distance):
    devices = range(lax.axis_size(axis))
    route = [((i - distance) % len(devices), i) for i in devices]
    return lax.ppermute(block, axis, route)


def tile_weights(mine, other):
    score = jnp.dot(mine, other.T, preferred_element_type=jnp.float32)
    return jnp.exp((score - 1.0) / tau_value)


def on_device(embeddings, labels):
    unit = (
        embeddings / jnp.sqrt(jnp.sum(embeddings * embeddings, axis=1, keepdims=True) + 1e-06)
    ).astype(jnp.bfloat16)
    rows = unit.shape[0]
    row_index = lax.broadcasted_iota(jnp.int32, (rows, rows), 0)
    col_index = lax.broadcasted_iota(jnp.int32, (rows, rows), 1)
    own_weight = jnp.where(row_index == col_index, 0.0, tile_weights(unit, unit))
    own_match = (labels[:, None] == labels[None, :]).astype(jnp.float32)
    same_sum = jnp.sum(own_weight * own_match, axis=1)
    total = jnp.sum(own_weight, axis=1)
    for offset in range(1, STEPS + 1):
        lower, lower_ids = passed_along((unit, labels), "blk", offset)
        upper, upper_ids = passed_along((unit, labels), "blk", -offset)
        for other, other_ids in ((lower, lower_ids), (upper, upper_ids)):
            weight = tile_weights(unit, other)
            match = (labels[:, None] == other_ids[None, :]).astype(jnp.float32)
            same_sum = same_sum + jnp.sum(weight * match, axis=1)
            total = total + jnp.sum(weight, axis=1)
    return (same_sum / total, jnp.log(total))


def solution(mesh):
    return jax.shard_map(
        on_device,
        mesh=mesh,
        in_specs=(P("blk", None), P("blk")),
        out_specs=(P("blk"), P("blk")),
        check_vma=False,
    )
```

profile of v0, /device:TPU:1, one launch (start us, length us, event | category | flops | bytes accessed | tf_op | source)
XLA Modules:
  0.0 262.7 jit_solution(14988229466484633396)
XLA Ops:
  0.6 0.0 copy-start
  0.6 2.3 multiply_reduce_fusion
  3.0 0.5 copy-done
  3.5 0.4 divide_convert_fusion
  3.9 11.3 %collective-permute-start.15 = (bf16[768,1024]{1,0:T(8,128)(2,1)S(1)}, bf16[768,1024]{1,0:T(8,128)(2,1)S(1)}, u32[]{:S(2)}, u32[]{:S(2)}) collective-permute-start(bf16[768,1024]{1,0:T(8,128)(2,1)S(1)} %divide_convert_fusion), channel_id=1, source_target_pairs={{4,0},{5,1},{6,2},{7,3},{8,4},{9,5},{10,6},{11,7},{12,8},{13,9},{1... | collective-permute-start | bytes 4718600 | tf_op jit(solution)/shard_map/ppermute | solution.py:15
  15.2 0.0 collective-permute-start.13
  15.2 8.1 %collective-permute-start.11 = (bf16[768,1024]{1,0:T(8,128)(2,1)S(1)}, bf16[768,1024]{1,0:T(8,128)(2,1)S(1)}, u32[]{:S(2)}, u32[]{:S(2)}) collective-permute-start(bf16[768,1024]{1,0:T(8,128)(2,1)S(1)} %divide_convert_fusion), channel_id=1, source_target_pairs={{3,0},{4,1},{5,2},{6,3},{7,4},{8,5},{9,6},{10,7},{11,8},{12,9},{13... | collective-permute-start | bytes 4718600 | tf_op jit(solution)/shard_map/ppermute | solution.py:15
  23.3 0.0 collective-permute-start.9
  23.3 6.3 %collective-permute-start.7 = (bf16[768,1024]{1,0:T(8,128)(2,1)S(1)}, bf16[768,1024]{1,0:T(8,128)(2,1)S(1)}, u32[]{:S(2)}, u32[]{:S(2)}) collective-permute-start(bf16[768,1024]{1,0:T(8,128)(2,1)S(1)} %divide_convert_fusion), channel_id=1, source_target_pairs={{2,0},{3,1},{4,2},{5,3},{6,4},{7,5},{8,6},{9,7},{10,8},{11,9},{12,... | collective-permute-start | bytes 4718600 | tf_op jit(solution)/shard_map/ppermute | solution.py:15
  29.7 1.4 fusion.10
  31.1 75.9 %collective-permute-done.15 = bf16[768,1024]{1,0:T(8,128)(2,1)S(1)} collective-permute-done((bf16[768,1024]{1,0:T(8,128)(2,1)S(1)}, bf16[768,1024]{1,0:T(8,128)(2,1)S(1)}, u32[]{:S(2)}, u32[]{:S(2)}) %collective-permute-start.15) | collective-permute-done | bytes 1572896 | tf_op jit(solution)/shard_map/ppermute | solution.py:15
  107.0 0.0 collective-permute-start.5
  107.0 1.4 fusion.17
  108.5 0.0 collective-permute-done.13
  108.5 5.9 %collective-permute-start.3 = (bf16[768,1024]{1,0:T(8,128)(2,1)S(1)}, bf16[768,1024]{1,0:T(8,128)(2,1)S(1)}, u32[]{:S(2)}, u32[]{:S(2)}) collective-permute-start(bf16[768,1024]{1,0:T(8,128)(2,1)S(1)} %divide_convert_fusion), channel_id=1, source_target_pairs={{1,0},{2,1},{3,2},{4,3},{5,4},{6,5},{7,6},{8,7},{9,8},{10,9},{11,1... | collective-permute-start | bytes 4718600 | tf_op jit(solution)/shard_map/ppermute | solution.py:15
  114.4 1.4 fusion.16
  115.8 0.0 copy-start.1
  115.8 43.4 %collective-permute-done.11 = bf16[768,1024]{1,0:T(8,128)(2,1)S(1)} collective-permute-done((bf16[768,1024]{1,0:T(8,128)(2,1)S(1)}, bf16[768,1024]{1,0:T(8,128)(2,1)S(1)}, u32[]{:S(2)}, u32[]{:S(2)}) %collective-permute-start.11) | collective-permute-done | bytes 1572896 | tf_op jit(solution)/shard_map/ppermute | solution.py:15
  159.2 0.0 collective-permute-start.1
  159.2 1.4 fusion.15
  160.7 0.0 collective-permute-done.9
  160.7 27.9 %collective-permute-start.8 = (s32[768]{0:T(1024)S(1)}, s32[768]{0:T(1024)S(1)}, u32[]{:S(2)}, u32[]{:S(2)}) collective-permute-start(s32[768]{0:T(1024)S(1)} %copy-done.1), channel_id=1, source_target_pairs={{253,0},{254,1},{255,2},{0,3},{1,4},{2,5},{3,6},{4,7},{5,8},{6,9},... | collective-permute-start | bytes 9224 | tf_op jit(solution)/shard_map/ppermute | solution.py:15
  188.6 1.4 fusion.14
  190.0 35.1 %collective-permute-done.7 = bf16[768,1024]{1,0:T(8,128)(2,1)S(1)} collective-permute-done((bf16[768,1024]{1,0:T(8,128)(2,1)S(1)}, bf16[768,1024]{1,0:T(8,128)(2,1)S(1)}, u32[]{:S(2)}, u32[]{:S(2)}) %collective-permute-start.7) | collective-permute-done | bytes 1572896 | tf_op jit(solution)/shard_map/ppermute | solution.py:15
  225.1 0.0 collective-permute-start.6
  225.1 1.4 fusion.13
  226.6 0.0 collective-permute-done.8
  226.6 1.5 collective-permute-start.4
  228.1 0.0 collective-permute-done.5
  228.1 0.0 collective-permute-start.2
  228.1 1.4 fusion.12
  229.6 0.0 collective-permute-done.6
  229.6 1.8 collective-permute-start
  231.4 3.2 %collective-permute-done.4 = s32[768]{0:T(1024)S(1)} collective-permute-done((s32[768]{0:T(1024)S(1)}, s32[768]{0:T(1024)S(1)}, u32[]{:S(2)}, u32[]{:S(2)}) %collective-permute-start.4) | collective-permute-done | bytes 3104 | tf_op jit(solution)/shard_map/ppermute | solution.py:15
  234.6 8.7 %collective-permute-start.10 = (s32[768]{0:T(1024)S(1)}, s32[768]{0:T(1024)S(1)}, u32[]{:S(2)}, u32[]{:S(2)}) collective-permute-start(s32[768]{0:T(1024)S(1)} %copy-done.1), channel_id=1, source_target_pairs={{3,0},{4,1},{5,2},{6,3},{7,4},{8,5},{9,6},{10,7},{11,8},{12,9},{13... | collective-permute-start | bytes 9224 | tf_op jit(solution)/shard_map/ppermute | solution.py:15
  243.2 0.0 collective-permute-done.2
  243.2 1.8 collective-permute-start.14
  245.0 0.0 collective-permute-done.3
  245.0 1.2 collective-permute-start.12
  246.2 1.4 fusion.11
  247.6 0.0 collective-permute-done
  247.6 0.0 collective-permute-done.10
  247.6 0.0 collective-permute-done.14
  247.7 5.6 %collective-permute-done.12 = s32[768]{0:T(1024)S(1)} collective-permute-done((s32[768]{0:T(1024)S(1)}, s32[768]{0:T(1024)S(1)}, u32[]{:S(2)}, u32[]{:S(2)}) %collective-permute-start.12) | collective-permute-done | bytes 3104 | tf_op jit(solution)/shard_map/ppermute | solution.py:15
  253.2 0.0 collective-permute-done.1
  253.2 8.2 %select_reduce_fusion.7 = (f32[768]{0:T(1024)S(1)}, f32[768]{0:T(1024)S(1)}, f32[768]{0:T(1024)S(1)}, f32[768]{0:T(1024)S(1)}, f32[768]{0:T(1024)S(1)}, /*index=...) fusion(s32[768]{0:T(1024)S(1)} %copy-done.1, ...), kind=kOutput, calls=%fused_computation.16 | convolution fusion | flops 1240975872 | bytes 22103040 | tf_op jit(solution)/shard_map/dot_general | solution.py:19
  261.4 0.6 fusion.9
  262.1 0.6 add_divide_fusion
  (2 shorter events, 0.0 us)
Async XLA Ops:
  0.6 2.8 %copy-start = (f32[768,1024]{1,0:T(8,128)S(1)}, f32[768,1024]{1,0:T(8,128)}, u32[]{:S(2)}) copy-start(f32[768,1024]{1,0:T(8,128)} %param.2) | copy-start | bytes 9437188
  3.9 103.1 %collective-permute-start.15 = (bf16[768,1024]{1,0:T(8,128)(2,1)S(1)}, bf16[768,1024]{1,0:T(8,128)(2,1)S(1)}, u32[]{:S(2)}, u32[]{:S(2)}) collective-permute-start(bf16[768,1024]{1,0:T(8,128)(2,1)S(1)} %divide_convert_fusion), channel_id=1, source_target_pairs={{4,0},{5,1},{6,2},{7,3},{8,4},{9,5},{10,6},{11,7},{12,8},{13,9},{1... | collective-permute-start | bytes 4718600 | tf_op jit(solution)/shard_map/ppermute | solution.py:15
  15.2 93.3 %collective-permute-start.13 = (bf16[768,1024]{1,0:T(8,128)(2,1)S(1)}, bf16[768,1024]{1,0:T(8,128)(2,1)S(1)}, u32[]{:S(2)}, u32[]{:S(2)}) collective-permute-start(bf16[768,1024]{1,0:T(8,128)(2,1)S(1)} %divide_convert_fusion), channel_id=1, source_target_pairs={{252,0},{253,1},{254,2},{255,3},{0,4},{1,5},{2,6},{3,7},{4,8},{5,9... | collective-permute-start | bytes 4718600 | tf_op jit(solution)/shard_map/ppermute | solution.py:15
  15.2 144.0 %collective-permute-start.11 = (bf16[768,1024]{1,0:T(8,128)(2,1)S(1)}, bf16[768,1024]{1,0:T(8,128)(2,1)S(1)}, u32[]{:S(2)}, u32[]{:S(2)}) collective-permute-start(bf16[768,1024]{1,0:T(8,128)(2,1)S(1)} %divide_convert_fusion), channel_id=1, source_target_pairs={{3,0},{4,1},{5,2},{6,3},{7,4},{8,5},{9,6},{10,7},{11,8},{12,9},{13... | collective-permute-start | bytes 4718600 | tf_op jit(solution)/shard_map/ppermute | solution.py:15
  23.3 137.3 %collective-permute-start.9 = (bf16[768,1024]{1,0:T(8,128)(2,1)S(1)}, bf16[768,1024]{1,0:T(8,128)(2,1)S(1)}, u32[]{:S(2)}, u32[]{:S(2)}) collective-permute-start(bf16[768,1024]{1,0:T(8,128)(2,1)S(1)} %divide_convert_fusion), channel_id=1, source_target_pairs={{253,0},{254,1},{255,2},{0,3},{1,4},{2,5},{3,6},{4,7},{5,8},{6,9},... | collective-permute-start | bytes 4718600 | tf_op jit(solution)/shard_map/ppermute | solution.py:15
  23.3 201.8 %collective-permute-start.7 = (bf16[768,1024]{1,0:T(8,128)(2,1)S(1)}, bf16[768,1024]{1,0:T(8,128)(2,1)S(1)}, u32[]{:S(2)}, u32[]{:S(2)}) collective-permute-start(bf16[768,1024]{1,0:T(8,128)(2,1)S(1)} %divide_convert_fusion), channel_id=1, source_target_pairs={{2,0},{3,1},{4,2},{5,3},{6,4},{7,5},{8,6},{9,7},{10,8},{11,9},{12,... | collective-permute-start | bytes 4718600 | tf_op jit(solution)/shard_map/ppermute | solution.py:15
  107.0 121.1 %collective-permute-start.5 = (bf16[768,1024]{1,0:T(8,128)(2,1)S(1)}, bf16[768,1024]{1,0:T(8,128)(2,1)S(1)}, u32[]{:S(2)}, u32[]{:S(2)}) collective-permute-start(bf16[768,1024]{1,0:T(8,128)(2,1)S(1)} %divide_convert_fusion), channel_id=1, source_target_pairs={{254,0},{255,1},{0,2},{1,3},{2,4},{3,5},{4,6},{5,7},{6,8},{7,9},{8... | collective-permute-start | bytes 4718600 | tf_op jit(solution)/shard_map/ppermute | solution.py:15
  108.5 136.5 %collective-permute-start.3 = (bf16[768,1024]{1,0:T(8,128)(2,1)S(1)}, bf16[768,1024]{1,0:T(8,128)(2,1)S(1)}, u32[]{:S(2)}, u32[]{:S(2)}) collective-permute-start(bf16[768,1024]{1,0:T(8,128)(2,1)S(1)} %divide_convert_fusion), channel_id=1, source_target_pairs={{1,0},{2,1},{3,2},{4,3},{5,4},{6,5},{7,6},{8,7},{9,8},{10,9},{11,1... | collective-permute-start | bytes 4718600 | tf_op jit(solution)/shard_map/ppermute | solution.py:15
  115.8 44.9 %copy-start.1 = (s32[768]{0:T(1024)S(1)}, s32[768]{0:T(1024)}, u32[]{:S(2)}) copy-start(s32[768]{0:T(1024)} %param.3) | copy-start | bytes 9220
  159.2 94.0 %collective-permute-start.1 = (bf16[768,1024]{1,0:T(8,128)(2,1)S(1)}, bf16[768,1024]{1,0:T(8,128)(2,1)S(1)}, u32[]{:S(2)}, u32[]{:S(2)}) collective-permute-start(bf16[768,1024]{1,0:T(8,128)(2,1)S(1)} %divide_convert_fusion), channel_id=1, source_target_pairs={{255,0},{0,1},{1,2},{2,3},{3,4},{4,5},{5,6},{6,7},{7,8},{8,9},{9,1... | collective-permute-start | bytes 4718600 | tf_op jit(solution)/shard_map/ppermute | solution.py:15
  160.7 65.9 %collective-permute-start.8 = (s32[768]{0:T(1024)S(1)}, s32[768]{0:T(1024)S(1)}, u32[]{:S(2)}, u32[]{:S(2)}) collective-permute-start(s32[768]{0:T(1024)S(1)} %copy-done.1), channel_id=1, source_target_pairs={{253,0},{254,1},{255,2},{0,3},{1,4},{2,5},{3,6},{4,7},{5,8},{6,9},... | collective-permute-start | bytes 9224 | tf_op jit(solution)/shard_map/ppermute | solution.py:15
  225.1 4.4 %collective-permute-start.6 = (s32[768]{0:T(1024)S(1)}, s32[768]{0:T(1024)S(1)}, u32[]{:S(2)}, u32[]{:S(2)}) collective-permute-start(s32[768]{0:T(1024)S(1)} %copy-done.1), channel_id=1, source_target_pairs={{2,0},{3,1},{4,2},{5,3},{6,4},{7,5},{8,6},{9,7},{10,8},{11,9},{12,... | collective-permute-start | bytes 9224 | tf_op jit(solution)/shard_map/ppermute | solution.py:15
  226.6 8.0 %collective-permute-start.4 = (s32[768]{0:T(1024)S(1)}, s32[768]{0:T(1024)S(1)}, u32[]{:S(2)}, u32[]{:S(2)}) collective-permute-start(s32[768]{0:T(1024)S(1)} %copy-done.1), channel_id=1, source_target_pairs={{254,0},{255,1},{0,2},{1,3},{2,4},{3,5},{4,6},{5,7},{6,8},{7,9},{8... | collective-permute-start | bytes 9224 | tf_op jit(solution)/shard_map/ppermute | solution.py:15
  228.1 15.1 %collective-permute-start.2 = (s32[768]{0:T(1024)S(1)}, s32[768]{0:T(1024)S(1)}, u32[]{:S(2)}, u32[]{:S(2)}) collective-permute-start(s32[768]{0:T(1024)S(1)} %copy-done.1), channel_id=1, source_target_pairs={{1,0},{2,1},{3,2},{4,3},{5,4},{6,5},{7,6},{8,7},{9,8},{10,9},{11,1... | collective-permute-start | bytes 9224 | tf_op jit(solution)/shard_map/ppermute | solution.py:15
  229.6 18.0 %collective-permute-start = (s32[768]{0:T(1024)S(1)}, s32[768]{0:T(1024)S(1)}, u32[]{:S(2)}, u32[]{:S(2)}) collective-permute-start(s32[768]{0:T(1024)S(1)} %copy-done.1), channel_id=1, source_target_pairs={{255,0},{0,1},{1,2},{2,3},{3,4},{4,5},{5,6},{6,7},{7,8},{8,9},{9,1... | collective-permute-start | bytes 9224 | tf_op jit(solution)/shard_map/ppermute | solution.py:15
  234.6 13.1 %collective-permute-start.10 = (s32[768]{0:T(1024)S(1)}, s32[768]{0:T(1024)S(1)}, u32[]{:S(2)}, u32[]{:S(2)}) collective-permute-start(s32[768]{0:T(1024)S(1)} %copy-done.1), channel_id=1, source_target_pairs={{3,0},{4,1},{5,2},{6,3},{7,4},{8,5},{9,6},{10,7},{11,8},{12,9},{13... | collective-permute-start | bytes 9224 | tf_op jit(solution)/shard_map/ppermute | solution.py:15
  243.2 4.4 %collective-permute-start.14 = (s32[768]{0:T(1024)S(1)}, s32[768]{0:T(1024)S(1)}, u32[]{:S(2)}, u32[]{:S(2)}) collective-permute-start(s32[768]{0:T(1024)S(1)} %copy-done.1), channel_id=1, source_target_pairs={{4,0},{5,1},{6,2},{7,3},{8,4},{9,5},{10,6},{11,7},{12,8},{13,9},{1... | collective-permute-start | bytes 9224 | tf_op jit(solution)/shard_map/ppermute | solution.py:15
  245.0 8.2 %collective-permute-start.12 = (s32[768]{0:T(1024)S(1)}, s32[768]{0:T(1024)S(1)}, u32[]{:S(2)}, u32[]{:S(2)}) collective-permute-start(s32[768]{0:T(1024)S(1)} %copy-done.1), channel_id=1, source_target_pairs={{252,0},{253,1},{254,2},{255,3},{0,4},{1,5},{2,6},{3,7},{4,8},{5,9... | collective-permute-start | bytes 9224 | tf_op jit(solution)/shard_map/ppermute | solution.py:15
where the time goes:
time: 263 us
  waiting for transfers between devices  163 us (62%)
  starting transfers between devices  74.5 us (28%)
  matrix products  19.6 us (7%)
  other arithmetic  3.97 us (2%)
    ppermute x16, waiting for transfers between devices, passed_along(): return lax.ppermute(block, axis, route)  163 us
    ppermute x16, starting transfers between devices, passed_along(): return lax.ppermute(block, axis, route)  74.5 us
    dot_general x9, matrix products, tile_weights(): score = jnp.dot(mine, other.T, preferred_element_type=jnp.float32)  19.6 us
  transfers between devices with their start and end apart: 16, of which 5 were waited for; matrix products, arithmetic and copies ran while one was open for 4% of the time, Pallas kernels for 0%

commit v1 on v0

v1 whole, which is shorter than its diff:
```python
import functools
import math

import jax
import jax.numpy as jnp
from jax import lax
from jax.experimental import pallas as pl
from jax.experimental.pallas import tpu as pltpu
from jax.sharding import PartitionSpec as P

TAU = 0.1
SCALE = math.log2(math.e) / TAU
HEAD = 16
LATE = 128
F32 = jnp.float32
BF16 = jnp.bfloat16


def vmem(count):
    return [pl.BlockSpec(memory_space=pltpu.VMEM)] * count


def call(kernel, out_shape, operands, name, tiles):
    return pl.pallas_call(
        kernel,
        out_shape=out_shape,
        in_specs=vmem(len(operands)),
        out_specs=jax.tree.map(lambda _: vmem(1)[0], out_shape),
        name=name,
        cost_estimate=pl.CostEstimate(
            flops=int(2 * tiles * 768 * 768 * 1024),
            bytes_accessed=sum(a.size * a.dtype.itemsize for a in operands),
            transcendentals=int(tiles * 768 * 768),
        ),
        compiler_params=pltpu.CompilerParams(vmem_limit_bytes=48 * 1024 * 1024),
    )(*operands)


def label_row(head):
    return (head[0:1, :] + head[1:2, :])


def label_column(head):
    ones = jnp.ones((HEAD, 128), BF16)
    return lax.dot_general(head, ones, (((0,), (0,)), ((), ())), preferred_element_type=F32)


def to_lanes(partial):
    ones = jnp.ones((8, 128), F32)
    return lax.dot_general(
        ones, partial, (((1,), (1,)), ((), ())), precision=lax.Precision.HIGHEST, preferred_element_type=F32
    )[0:1]


def tile(left, left_labels, right, right_labels, rows, columns, own=None):
    m, n = left.shape[0], right.shape[0]
    step = 256
    row_total = row_same = None
    totals, sames = [], []
    labels2 = jnp.concatenate([left_labels, left_labels], axis=1)
    for j in range(0, n, step):
        score = lax.dot_general(
            left, right[j : j + step], (((1,), (1,)), ((), ())), preferred_element_type=F32
        )
        weight = jnp.exp2(score * SCALE - SCALE)
        if own is not None:
            r = lax.broadcasted_iota(jnp.int32, (m, step), 0) + own
            c = lax.broadcasted_iota(jnp.int32, (m, step), 1) + j
            weight = jnp.where(r == c, 0.0, weight)
        same = jnp.where(labels2 == right_labels[:, j : j + step], weight, 0.0)
        if rows:
            a, b = weight[:, :128] + weight[:, 128:], same[:, :128] + same[:, 128:]
            row_total = a if row_total is None else row_total + a
            row_same = b if row_same is None else row_same + b
        if columns:
            totals.append(jnp.sum(weight, axis=0, keepdims=True))
            sames.append(jnp.sum(same, axis=0, keepdims=True))
    out = []
    if rows:
        out += [row_total, row_same]
    if columns:
        out += [jnp.concatenate(totals, axis=1), jnp.concatenate(sames, axis=1)]
    return out


def pair(left_ref, first, count, left_labels, right_ref, right_labels, rows, columns, own=False, row_start=0):
    right = right_ref[HEAD:, :]
    row_out, col = [], None
    step = min(384, count)
    for i in range(0, count, step):
        m = min(step, count - i)
        left = left_ref[first + i : first + i + m, :]
        got = tile(
            left, left_labels[row_start + i : row_start + i + m], right, right_labels, rows, columns,
            own=i if own else None,
        )
        if rows:
            row_out.append(jnp.concatenate([to_lanes(got[0]), to_lanes(got[1])], axis=0))
        if columns:
            both = jnp.concatenate(got[-2:], axis=0)
            col = both if col is None else col + both
    out = []
    if rows:
        out.append(jnp.concatenate(row_out, axis=1))
    if columns:
        out.append(col)
    return out if len(out) > 1 else out[0]


def norm_kernel(x_ref, labels_ref, out_ref):
    rows = x_ref.shape[0]
    for i in range(0, rows, 128):
        x = x_ref[i : i + 128, :]
        scale = lax.rsqrt(jnp.sum(x * x, axis=1, keepdims=True) + 1e-06)
        out_ref[HEAD + i : HEAD + i + 128, :] = (x * scale).astype(BF16)
    labels = labels_ref[...]
    low = lax.rem(labels, 256)
    wide = jnp.concatenate([labels - low, low], axis=0).astype(F32)
    wide = jnp.concatenate([wide, jnp.zeros((HEAD - 2, rows), F32)], axis=0)
    wide = jnp.concatenate([wide, jnp.zeros((HEAD, x_ref.shape[1] - rows), F32)], axis=1)
    out_ref[0:HEAD, :] = wide.astype(BF16)


def head_of(ref, rows):
    return ref[0:HEAD, 0:rows]


def first_kernel(u_ref, x_ref, own_ref, early_ref, late_ref):
    rows = u_ref.shape[0] - HEAD
    cut = u_ref.shape[0] - LATE
    early_ref[...] = u_ref[0:cut, :]
    late_ref[...] = u_ref[cut:, :]
    own_row = label_row(head_of(u_ref, rows).astype(F32))
    own_column = label_column(head_of(u_ref, rows))
    x_column = label_column(head_of(x_ref, rows))
    inside = pair(u_ref, HEAD, rows, own_column, u_ref, own_row, False, True, own=True)
    other = pair(x_ref, HEAD, rows, x_column, u_ref, own_row, False, True)
    own_ref[...] = inside + other


def second_kernel(u_ref, x_ref, a_ref, own_in_ref, own_ref, a_sum_ref):
    rows = u_ref.shape[0] - HEAD
    a_row = label_row(head_of(a_ref, rows).astype(F32))
    own_column = label_column(head_of(u_ref, rows))
    x_column = label_column(head_of(x_ref, rows))
    own_sum, a_sum = pair(u_ref, HEAD, rows, own_column, a_ref, a_row, True, True)
    a_sum2 = pair(x_ref, HEAD, rows, x_column, a_ref, a_row, False, True)
    own_ref[...] = own_in_ref[...] + own_sum
    a_sum_ref[...] = a_sum + a_sum2


def third_kernel(f_ref, a_ref, a_in_ref, a_sum_ref):
    rows = a_ref.shape[0] - HEAD
    a_row = label_row(head_of(a_ref, rows).astype(F32))
    f_column = label_column(head_of(f_ref, rows))
    a_sum_ref[...] = a_in_ref[...] + pair(f_ref, HEAD, rows, f_column, a_ref, a_row, False, True)


def fourth_kernel(first, count, skip, b_ref, head_ref, a_ref, x_ref, a_in_ref, a_sum_ref, b_sum_ref):
    rows = a_ref.shape[0] - HEAD
    a_row = label_row(head_of(a_ref, rows).astype(F32))
    x_row = label_row(head_of(x_ref, rows).astype(F32))
    b_column = label_column(head_of(head_ref, rows))
    b_sum, a_sum = pair(b_ref, skip, count, b_column, a_ref, a_row, True, True, row_start=first)
    b_sum2 = pair(b_ref, skip, count, b_column, x_ref, x_row, True, False, row_start=first)
    a_sum_ref[...] = a_in_ref[...] + a_sum
    b_sum_ref[...] = b_sum + b_sum2


def on_device(embeddings, labels):
    rows, depth = embeddings.shape
    n = lax.axis_size("blk")
    up = [(i, (i + 2) % n if i % 2 else (i - 2) % n) for i in range(n)]
    down = [(i, (i - 2) % n if i % 2 else (i + 2) % n) for i in range(n)]
    swap = [(i, i ^ 1) for i in range(n)]
    back = lambda route: [(d, s) for s, d in route]
    send = lambda array, route: lax.ppermute(array, "blk", route)
    struct = jax.ShapeDtypeStruct
    sums = struct((2, rows), F32)

    u = call(norm_kernel, struct((rows + HEAD, depth), BF16), (embeddings, labels[None, :]), "unit", 0.1)
    a = send(u, up)
    x = send(u, swap)
    early, late = struct((rows + HEAD - LATE, depth), BF16), struct((LATE, depth), BF16)
    own, early, late = call(first_kernel, (sums, early, late), (u, x), "own_and_partner", 2)
    b_early = send(early, down)
    b_late = send(late, down)
    f = send(a, swap)
    own, a_sum = call(second_kernel, (sums, sums), (u, x, a, own), "with_a", 2)
    a_sum = call(third_kernel, sums, (f, a, a_sum), "a_with_f", 1)
    a_sum, b_sum1 = call(
        functools.partial(fourth_kernel, 0, rows - LATE, HEAD),
        (sums, struct((2, rows - LATE), F32)),
        (b_early, b_early, a, x, a_sum),
        "with_b_early",
        1.7,
    )
    a_sum, b_sum2 = call(
        functools.partial(fourth_kernel, rows - LATE, LATE, 0),
        (sums, struct((2, LATE), F32)),
        (b_late, b_early[0:HEAD], a, x, a_sum),
        "with_b_late",
        0.3,
    )
    b_sum = jnp.concatenate([b_sum1, b_sum2], axis=1)
    from_a = send(a_sum, back(up))
    from_b = send(b_sum, back(down))
    total, same = own + from_a + from_b
    return same / total, jnp.log(total)


def solution(mesh):
    return jax.shard_map(
        on_device,
        mesh=mesh,
        in_specs=(P("blk", None), P("blk")),
        out_specs=(P("blk"), P("blk")),
        check_vma=False,
    )
```

time: 263 us -> 77.9 us (0.30)
  waiting for transfers between devices: 163 us -> 28.2 us
  starting transfers between devices: 74.5 us -> 28.6 us
  matrix products: 19.6 us -> 0 us
  Pallas kernels: 0 us -> 16.2 us
  other arithmetic: 3.97 us -> 0.68 us
    ppermute x16 -> x7, waiting for transfers between devices: 163 us -> 28.2 us  [on_device(): send = lambda array, route: lax.ppermute(array, 'blk', route)]
    ppermute x16 -> x7, starting transfers between devices: 74.5 us -> 28.6 us  [on_device(): send = lambda array, route: lax.ppermute(array, 'blk', route)]
    dot_general x9 -> x0, matrix products: 19.6 us -> none  [tile_weights(): score = jnp.dot(mine, other.T, preferred_element_type=jnp.float32)]
    pallas_call x0 -> x6, Pallas kernels: none -> 16.2 us  [call(): pl.pallas_call(kernel, out_shape=out_shape, in_specs=vmem(len(operands)),...]
  transfers between devices with their start and end apart: 16 -> 7, of which waited for: 5 -> 3; matrix products, arithmetic and copies ran while one was open for 4% -> 0% of each run, Pallas kernels for 0% -> 18%
where the time goes in v1:
time: 77.9 us; the launch traced here: 77 us
  starting transfers between devices  28.6 us (37%)
  waiting for transfers between devices  28.2 us (36%)
  Pallas kernels  16.2 us (21%)
  local copies, waits for them, and re-layouts  2.58 us (3%)
    ppermute x7, starting transfers between devices, on_device(): send = lambda array, route: lax.ppermute(array, 'blk', route)  28.6 us
    ppermute x7, waiting for transfers between devices, on_device(): send = lambda array, route: lax.ppermute(array, 'blk', route)  28.2 us
    pallas_call x6, Pallas kernels, call(): pl.pallas_call(kernel, out_shape=out_shape, in_specs=vmem(len(operands)),...  16.2 us
    unnamed x2, local copies, waits for them, and re-layouts  1.89 us
  transfers between devices with their start and end apart: 7, of which 3 were waited for; matrix products, arithmetic and copies ran while one was open for 0% of the time, Pallas kernels for 18%

profile of v1, /device:TPU:1, one launch (start us, length us, event | category | flops | bytes accessed | tf_op | source)
XLA Modules:
  0.0 77.0 jit_solution(185686437143562694)
XLA Ops:
  0.6 0.7 broadcast_in_dim.3.labels_ref
  1.3 0.0 copy-start
  1.3 1.9 %copy-done = f32[768,1024]{1,0:T(8,128)S(1)} copy-done((f32[768,1024]{1,0:T(8,128)S(1)}, f32[768,1024]{1,0:T(8,128)}, u32[]{:S(2)}) %copy-start) | copy-done | bytes 3145752
  3.2 0.4 unit.1.u_ref
  3.6 2.2 %collective-permute-start.1 = (bf16[784,1024]{1,0:T(8,128)(2,1)S(1)}, bf16[784,1024]{1,0:T(8,128)(2,1)S(1)}, u32[]{:S(2)}, u32[]{:S(2)}) collective-permute-start(bf16[784,1024]{1,0:T(8,128)(2,1)S(1)} %unit.1.u_ref), channel_id=1, source_target_pairs={{0,254},{1,3},{2,0},{3,5},{4,2},{5,7},{6,4},{7,9},{8,6},{9,11},{10... | collective-permute-start | bytes 4816904 | tf_op jit(solution)/shard_map/ppermute | solution.py:177
  5.8 9.9 %collective-permute-start = (bf16[784,1024]{1,0:T(8,128)(2,1)S(1)}, bf16[784,1024]{1,0:T(8,128)(2,1)S(1)}, u32[]{:S(2)}, u32[]{:S(2)}) collective-permute-start(bf16[784,1024]{1,0:T(8,128)(2,1)S(1)} %unit.1.u_ref), channel_id=1, source_target_pairs={{0,1},{1,0},{2,3},{3,2},{4,5},{5,4},{6,7},{7,6},{8,9},{9,8},{10,11... | collective-permute-start | bytes 4816904 | tf_op jit(solution)/shard_map/ppermute | solution.py:177
  15.7 17.2 %collective-permute-done.1.a_ref = bf16[784,1024]{1,0:T(8,128)(2,1)S(1)} collective-permute-done((bf16[784,1024]{1,0:T(8,128)(2,1)S(1)}, bf16[784,1024]{1,0:T(8,128)(2,1)S(1)}, u32[]{:S(2)}, u32[]{:S(2)}) %collective-permute-start.1) | collective-permute-done | bytes 1605664 | tf_op jit(solution)/shard_map/ppermute | solution.py:177
  32.9 1.1 %collective-permute-start.4 = (bf16[784,1024]{1,0:T(8,128)(2,1)S(1)}, bf16[784,1024]{1,0:T(8,128)(2,1)S(1)}, u32[]{:S(2)}, u32[]{:S(2)}) collective-permute-start(bf16[784,1024]{1,0:T(8,128)(2,1)S(1)} %collective-permute-done.1.a_ref), channel_id=1, source_target_pairs={{0,1},{1,0},{2,3},{3,2},{4,5},{5,4},{6,7},{7,6},{8,9},{9,8},{10,11... | collective-permute-start | bytes 4816904 | tf_op jit(solution)/shard_map/ppermute | solution.py:177
  34.0 0.0 collective-permute-done.x_ref
  34.0 3.1 %own_and_partner.1 = (f32[2,768]{1,0:T(2,128)S(1)}, bf16[656,1024]{1,0:T(8,128)(2,1)S(1)}, bf16[128,1024]{1,0:T(8,128)(2,1)S(1)}) custom-call(bf16[784,1024]{1,0:T(8,128)(2,1)S(1)} %unit.1.u_ref, bf16[784,1024]{1,0:T(8,128)(2,1)S(1)} %collective-permute-done.x_ref), custom_call_target="tpu_custom_call" | custom-call | flops 2415919104 | bytes 3211264 | tf_op jit(solution)/shard_map/own_and_partner/pallas_call | solution.py:24
  37.1 7.7 %collective-permute-start.3 = (bf16[656,1024]{1,0:T(8,128)(2,1)S(1)}, bf16[656,1024]{1,0:T(8,128)(2,1)S(1)}, u32[]{:S(2)}, u32[]{:S(2)}) collective-permute-start(bf16[656,1024]{1,0:T(8,128)(2,1)S(1)} %get-tuple-element.14), channel_id=1, source_target_pairs={{0,2},{1,255},{2,4},{3,1},{4,6},{5,3},{6,8},{7,5},{8,10},{9,7},{10... | collective-permute-start | bytes 4030472 | tf_op jit(solution)/shard_map/ppermute | solution.py:177
  44.8 0.3 collective-permute-start.2
  45.0 4.6 %with_a.1 = (f32[2,768]{1,0:T(2,128)S(1)}, f32[2,768]{1,0:T(2,128)S(1)}) custom-call(bf16[784,1024]{1,0:T(8,128)(2,1)S(1)} %unit.1.u_ref, bf16[784,1024]{1,0:T(8,128)(2,1)S(1)} %collective-permute-done.x_ref, bf16[784,1024]{1,0:T(8,128)(2,1)S(1)} %collective-permute-done.1.a_ref, f32[2,768]{1,0:T(2,128)S(1)} %get-tuple-element.11.own_in_ref), custom_call_target="tpu_custom_call" | custom-call | flops 2415919104 | bytes 4823040 | tf_op jit(solution)/shard_map/with_a/pallas_call | solution.py:24
  49.6 10.0 %collective-permute-done.3.b_ref.head_ref = bf16[656,1024]{1,0:T(8,128)(2,1)S(1)} collective-permute-done((bf16[656,1024]{1,0:T(8,128)(2,1)S(1)}, bf16[656,1024]{1,0:T(8,128)(2,1)S(1)}, u32[]{:S(2)}, u32[]{:S(2)}) %collective-permute-start.3) | collective-permute-done | bytes 1343520 | tf_op jit(solution)/shard_map/ppermute | solution.py:177
  59.7 0.0 collective-permute-done.4.f_ref
  59.7 1.7 %a_with_f.1.a_in_ref = f32[2,768]{1,0:T(2,128)S(1)} custom-call(bf16[784,1024]{1,0:T(8,128)(2,1)S(1)} %collective-permute-done.4.f_ref, bf16[784,1024]{1,0:T(8,128)(2,1)S(1)} %collective-permute-done.1.a_ref, f32[2,768]{1,0:T(2,128)S(1)} %get-tuple-element.15.a_in_ref), custom_call_target="tpu_custom_call" | custom-call | flops 1207959552 | bytes 3217408 | tf_op jit(solution)/shard_map/a_with_f/pallas_call | solution.py:24
  61.4 4.6 %with_b_early.1 = (f32[2,768]{1,0:T(2,128)S(1)}, f32[2,640]{1,0:T(2,128)S(1)}) custom-call(bf16[656,1024]{1,0:T(8,128)(2,1)S(1)} %collective-permute-done.3.b_ref.head_ref, bf16[656,1024]{1,0:T(8,128)(2,1)S(1)} %collective-permute-done.3.b_ref.head_ref, bf16[784,1024]{1,0:T(8,128)(2,1)S(1)} %collective-permute-done.1.a_ref, ...), custom_call_target="tpu_custom_call" | custom-call | flops 2053531264 | bytes 5904384 | tf_op jit(solution)/shard_map/with_b_early/pallas_call | solution.py:24
  66.0 0.0 collective-permute-done.2.b_ref
  66.0 1.8 %with_b_late.1 = (f32[2,768]{1,0:T(2,128)S(1)}, f32[2,128]{1,0:T(2,128)S(1)}) custom-call(bf16[128,1024]{1,0:T(8,128)(2,1)S(1)} %collective-permute-done.2.b_ref, bf16[16,1024]{1,0:T(8,128)(2,1)S(1)} %slice.4.head_ref, bf16[784,1024]{1,0:T(8,128)(2,1)S(1)} %collective-permute-done.1.a_ref, bf16[784,1024]{1,0:T(8,128)(2,1)S(1)} %collective-permute-done.x_ref, ...), custom_call_target="tpu_custom_call" | custom-call | flops 362387872 | bytes 3512320 | tf_op jit(solution)/shard_map/with_b_late/pallas_call | solution.py:24
  67.8 0.1 pad_maximum_fusion
  67.9 0.1 collective-permute-start.6
  68.0 7.4 %collective-permute-start.5 = (f32[2,768]{1,0:T(2,128)S(1)}, f32[2,768]{1,0:T(2,128)S(1)}, u32[]{:S(2)}, u32[]{:S(2)}) collective-permute-start(f32[2,768]{1,0:T(2,128)S(1)} %get-tuple-element.17), channel_id=1, source_target_pairs={{254,0},{3,1},{0,2},{5,3},{2,4},{7,5},{4,6},{9,7},{6,8},{11,9},{8,... | collective-permute-start | bytes 18440 | tf_op jit(solution)/shard_map/ppermute | solution.py:177
  75.4 0.9 %collective-permute-done.6 = f32[2,768]{1,0:T(2,128)S(1)} collective-permute-done((f32[2,768]{1,0:T(2,128)S(1)}, f32[2,768]{1,0:T(2,128)S(1)}, u32[]{:S(2)}, u32[]{:S(2)}) %collective-permute-start.6) | collective-permute-done | bytes 6176 | tf_op jit(solution)/shard_map/ppermute | solution.py:177
  76.3 0.0 collective-permute-done.5
  76.4 0.6 log_reduce_fusion
  (2 shorter events, 0.0 us)
Async XLA Ops:
  1.3 1.9 %copy-start = (f32[768,1024]{1,0:T(8,128)S(1)}, f32[768,1024]{1,0:T(8,128)}, u32[]{:S(2)}) copy-start(f32[768,1024]{1,0:T(8,128)} %x_ref.1) | copy-start | bytes 9437188
  3.6 29.3 %collective-permute-start.1 = (bf16[784,1024]{1,0:T(8,128)(2,1)S(1)}, bf16[784,1024]{1,0:T(8,128)(2,1)S(1)}, u32[]{:S(2)}, u32[]{:S(2)}) collective-permute-start(bf16[784,1024]{1,0:T(8,128)(2,1)S(1)} %unit.1.u_ref), channel_id=1, source_target_pairs={{0,254},{1,3},{2,0},{3,5},{4,2},{5,7},{6,4},{7,9},{8,6},{9,11},{10... | collective-permute-start | bytes 4816904 | tf_op jit(solution)/shard_map/ppermute | solution.py:177
  5.8 28.2 %collective-permute-start = (bf16[784,1024]{1,0:T(8,128)(2,1)S(1)}, bf16[784,1024]{1,0:T(8,128)(2,1)S(1)}, u32[]{:S(2)}, u32[]{:S(2)}) collective-permute-start(bf16[784,1024]{1,0:T(8,128)(2,1)S(1)} %unit.1.u_ref), channel_id=1, source_target_pairs={{0,1},{1,0},{2,3},{3,2},{4,5},{5,4},{6,7},{7,6},{8,9},{9,8},{10,11... | collective-permute-start | bytes 4816904 | tf_op jit(solution)/shard_map/ppermute | solution.py:177
  32.9 26.8 %collective-permute-start.4 = (bf16[784,1024]{1,0:T(8,128)(2,1)S(1)}, bf16[784,1024]{1,0:T(8,128)(2,1)S(1)}, u32[]{:S(2)}, u32[]{:S(2)}) collective-permute-start(bf16[784,1024]{1,0:T(8,128)(2,1)S(1)} %collective-permute-done.1.a_ref), channel_id=1, source_target_pairs={{0,1},{1,0},{2,3},{3,2},{4,5},{5,4},{6,7},{7,6},{8,9},{9,8},{10,11... | collective-permute-start | bytes 4816904 | tf_op jit(solution)/shard_map/ppermute | solution.py:177
  37.1 22.6 %collective-permute-start.3 = (bf16[656,1024]{1,0:T(8,128)(2,1)S(1)}, bf16[656,1024]{1,0:T(8,128)(2,1)S(1)}, u32[]{:S(2)}, u32[]{:S(2)}) collective-permute-start(bf16[656,1024]{1,0:T(8,128)(2,1)S(1)} %get-tuple-element.14), channel_id=1, source_target_pairs={{0,2},{1,255},{2,4},{3,1},{4,6},{5,3},{6,8},{7,5},{8,10},{9,7},{10... | collective-permute-start | bytes 4030472 | tf_op jit(solution)/shard_map/ppermute | solution.py:177
  44.8 21.2 %collective-permute-start.2 = (bf16[128,1024]{1,0:T(8,128)(2,1)S(1)}, bf16[128,1024]{1,0:T(8,128)(2,1)S(1)}, u32[]{:S(2)}, u32[]{:S(2)}) collective-permute-start(bf16[128,1024]{1,0:T(8,128)(2,1)S(1)} %get-tuple-element.13), channel_id=1, source_target_pairs={{0,2},{1,255},{2,4},{3,1},{4,6},{5,3},{6,8},{7,5},{8,10},{9,7},{10... | collective-permute-start | bytes 786440 | tf_op jit(solution)/shard_map/ppermute | solution.py:177
  67.9 8.4 %collective-permute-start.6 = (f32[2,768]{1,0:T(2,128)S(1)}, f32[2,768]{1,0:T(2,128)S(1)}, u32[]{:S(2)}, u32[]{:S(2)}) collective-permute-start(f32[2,768]{1,0:T(2,128)S(1)} %pad_maximum_fusion), channel_id=1, source_target_pairs={{2,0},{255,1},{4,2},{1,3},{6,4},{3,5},{8,6},{5,7},{10,8},{7,9},{12... | collective-permute-start | bytes 18440 | tf_op jit(solution)/shard_map/ppermute | solution.py:177
  68.0 8.3 %collective-permute-start.5 = (f32[2,768]{1,0:T(2,128)S(1)}, f32[2,768]{1,0:T(2,128)S(1)}, u32[]{:S(2)}, u32[]{:S(2)}) collective-permute-start(f32[2,768]{1,0:T(2,128)S(1)} %get-tuple-element.17), channel_id=1, source_target_pairs={{254,0},{3,1},{0,2},{5,3},{2,4},{7,5},{4,6},{9,7},{6,8},{11,9},{8,... | collective-permute-start | bytes 18440 | tf_op jit(solution)/shard_map/ppermute | solution.py:177

commit v2 on v0

v2 whole, which is shorter than its diff:
```python
import functools
import math

import jax
import jax.numpy as jnp
from jax import lax
from jax.experimental import pallas as pl
from jax.experimental.pallas import tpu as pltpu
from jax.sharding import PartitionSpec as P

TAU = 0.1
SCALE = math.log2(math.e) / TAU
LANES = 128
HEAD = 16
EARLY = 512
LATE = 256
CHUNK = 512
STEP = 256
F32 = jnp.float32
BF16 = jnp.bfloat16


def call(kernel, out_shape, operands, name, tiles, in_specs=None, scratch=(), limit=48):
    vmem = pl.BlockSpec(memory_space=pltpu.VMEM)
    return pl.pallas_call(
        kernel,
        out_shape=out_shape,
        in_specs=in_specs or [vmem] * len(operands),
        out_specs=jax.tree.map(lambda _: vmem, out_shape),
        scratch_shapes=scratch,
        name=name,
        cost_estimate=pl.CostEstimate(
            flops=int(1.2e10 * tiles),
            bytes_accessed=1024,
            transcendentals=0,
        ),
        compiler_params=pltpu.CompilerParams(vmem_limit_bytes=limit * 1024 * 1024),
    )(*operands)


def images(ref, n, first, count, head=HEAD):
    slabs = (ref.shape[0] - head) // n
    return jnp.concatenate(
        [ref[head + k * n + first : head + k * n + first + count, :] for k in range(slabs)], axis=1
    )


def label_row(ref, n):
    head = ref[0:HEAD, :].astype(F32)
    groups = n // LANES
    return jnp.concatenate([head[k : k + 1] + head[k + groups : k + groups + 1] for k in range(groups)], axis=1)


def label_column(ref, n):
    groups = n // LANES
    row = lax.broadcasted_iota(jnp.int32, (HEAD, n), 0)
    group = lax.broadcasted_iota(jnp.int32, (HEAD, n), 1) // LANES
    pick = jnp.where((row == group) | (row == group + groups), 1.0, 0.0).astype(BF16)
    spread = lax.dot_general(ref[0:HEAD, :], pick, (((0,), (0,)), ((), ())), preferred_element_type=F32)
    return jnp.concatenate([spread[:, k * LANES : (k + 1) * LANES] for k in range(groups)], axis=0)


def along_lanes(partial):
    return jnp.concatenate(
        [
            jnp.sum(partial[i : i + LANES].T, axis=0, keepdims=True)
            for i in range(0, partial.shape[0], LANES)
        ],
        axis=1,
    )


def weigh(left, left_labels, right, right_labels, rows, columns, own=None):
    m, n = left.shape[0], right.shape[0]
    row_parts, column = [], None
    for i in range(0, m, CHUNK):
        chunk = min(CHUNK, m - i)
        here = left[i : i + chunk]
        labels = jnp.concatenate([left_labels[i : i + chunk]] * (STEP // LANES), axis=1)
        totals, sames, row_total, row_same = [], [], None, None
        for j in range(0, n, STEP):
            score = lax.dot_general(
                here, right[j : j + STEP], (((1,), (1,)), ((), ())), preferred_element_type=F32
            )
            weight = jnp.exp2(score * SCALE)
            if own is not None:
                r = lax.broadcasted_iota(jnp.int32, (chunk, STEP), 0) + (own + i)
                c = lax.broadcasted_iota(jnp.int32, (chunk, STEP), 1) + j
                weight = jnp.where(r == c, 0.0, weight)
            same = jnp.where(labels == right_labels[:, j : j + STEP], weight, 0.0)
            if rows:
                for k in range(0, STEP, LANES):
                    a, b = weight[:, k : k + LANES], same[:, k : k + LANES]
                    row_total = a if row_total is None else row_total + a
                    row_same = b if row_same is None else row_same + b
            if columns:
                totals.append(jnp.sum(weight, axis=0, keepdims=True))
                sames.append(jnp.sum(same, axis=0, keepdims=True))
        if rows:
            row_parts.append((row_total, row_same))
        if columns:
            both = jnp.concatenate([jnp.concatenate(totals, axis=1), jnp.concatenate(sames, axis=1)], axis=0)
            column = both if column is None else column + both
    rows_out = tuple(jnp.concatenate(p, axis=0) for p in zip(*row_parts)) if rows else None
    return rows_out, column


def add(*pairs):
    total, same = pairs[0]
    for more_total, more_same in pairs[1:]:
        total, same = total + more_total, same + more_same
    return jnp.concatenate([along_lanes(total), along_lanes(same)], axis=0)


def early_part(ref):
    return images(ref, EARLY, 0, EARLY)


def late_part(ref):
    return images(ref, LATE, 0, LATE, head=0)


def columns_of(early_ref, late):
    column = label_column(early_ref, EARLY + LATE)
    return column[EARLY:] if late else column[:EARLY]


def row_of(early_ref, late):
    row = label_row(early_ref, EARLY + LATE)
    return row[:, EARLY:] if late else row[:, :EARLY]


def unit_kernel(x_ref, labels_hbm, early_ref, late_ref, held, labels_ref, sems):
    n, depth = x_ref.shape
    parts = sems.shape[0] - 1
    part = n // parts
    copies = [
        pltpu.make_async_copy(x_ref.at[pl.ds(i * part, part), :], held.at[pl.ds(i * part, part), :], sems.at[i])
        for i in range(parts)
    ]
    labels_copy = pltpu.make_async_copy(labels_hbm, labels_ref, sems.at[parts])
    labels_copy.start()
    for copy in copies:
        copy.start()
    labels_copy.wait()
    labels = labels_ref[...]
    low = lax.rem(labels, 256)
    blank = jnp.zeros((HEAD - 2 * labels.shape[0], LANES), F32)
    head = jnp.concatenate([(labels - low).astype(F32), low.astype(F32), blank], axis=0)
    early_ref[0:HEAD, :] = head.astype(BF16)
    for i in range(parts):
        copies[i].wait()
        for q in range(i * part, (i + 1) * part, 64):
            x = held[q : q + 64, :]
            unit = (x * lax.rsqrt(jnp.sum(x * x, axis=1, keepdims=True) + 1e-06)).astype(BF16)
            for k in range(depth // LANES):
                slab = unit[:, k * LANES : (k + 1) * LANES]
                if q < EARLY:
                    early_ref[HEAD + k * EARLY + q : HEAD + k * EARLY + q + 64, :] = slab
                else:
                    late_ref[k * LATE + q - EARLY : k * LATE + q - EARLY + 64, :] = slab


def own_kernel(ue_ref, ul_ref, own_ref, copy_ref):
    copy_ref[...] = ul_ref[...]
    unit = jnp.concatenate([early_part(ue_ref), late_part(ul_ref)], axis=0)
    labels = label_row(ue_ref, EARLY + LATE)
    _, own = weigh(unit, label_column(ue_ref, EARLY + LATE), unit, labels, False, True, own=0)
    own_ref[...] = own


def partner_kernel(ue_ref, ul_ref, xe_ref, xl_ref, own_in_ref, own_ref):
    unit = jnp.concatenate([early_part(ue_ref), late_part(ul_ref)], axis=0)
    labels = label_row(ue_ref, EARLY + LATE)
    _, a = weigh(early_part(xe_ref), columns_of(xe_ref, False), unit, labels, False, True)
    _, b = weigh(late_part(xl_ref), columns_of(xe_ref, True), unit, labels, False, True)
    own_ref[...] = own_in_ref[...] + a + b


def is_even():
    return lax.rem(lax.axis_index("blk"), 2) == 0


def pick_kernel(p_ref, n_ref, after_ref, out_ref):
    even = is_even()

    @pl.when(even)
    def _():
        out_ref[...] = n_ref[...]

    @pl.when(jnp.logical_not(even))
    def _():
        out_ref[...] = p_ref[...]


def early_kernel(ue_ref, ul_ref, xe_ref, xl_ref, pe_ref, ne_ref, own_in_ref, own_ref, p_ref, n_ref):
    n, labels = early_part(ne_ref), columns_of(ne_ref, False)
    n1, own1 = weigh(n, labels, early_part(ue_ref), row_of(ue_ref, False), True, True)
    n2, own2 = weigh(n, labels, late_part(ul_ref), row_of(ue_ref, True), True, True)
    n3, _ = weigh(n, labels, early_part(xe_ref), row_of(xe_ref, False), True, False)
    n4, _ = weigh(n, labels, late_part(xl_ref), row_of(xe_ref, True), True, False)
    n5, p1 = weigh(n, labels, early_part(pe_ref), row_of(pe_ref, False), True, True)
    n_ref[...] = add(n1, n2, n3, n4, n5)
    own_ref[:, :EARLY] = own_in_ref[:, :EARLY] + own1
    own_ref[:, EARLY:] = own_in_ref[:, EARLY:] + own2
    p, labels = early_part(pe_ref), row_of(pe_ref, False)
    _, p2 = weigh(early_part(xe_ref), columns_of(xe_ref, False), p, labels, False, True)
    _, p3 = weigh(late_part(xl_ref), columns_of(xe_ref, True), p, labels, False, True)
    p_ref[...] = p1 + p2 + p3


def early_f_kernel(fe_ref, pe_ref, ne_ref, p_in_ref, n_in_ref, p_ref, n_ref):
    even = is_even()
    right = jnp.where(even, early_part(ne_ref), early_part(pe_ref))
    labels = jnp.where(even, row_of(ne_ref, False), row_of(pe_ref, False))
    _, more = weigh(early_part(fe_ref), columns_of(fe_ref, False), right, labels, False, True)
    p_ref[...] = p_in_ref[...] + jnp.where(even, 0.0, more)
    n_ref[...] = n_in_ref[...] + jnp.where(even, more, 0.0)


def late_kernel(
    ue_ref, ul_ref, xe_ref, xl_ref, pe_ref, ne_ref, pl_ref, nl_ref, own_in_ref, p_in_ref, n_in_ref,
    own_ref, p_ref, n_ref,
):
    n, labels = late_part(nl_ref), columns_of(ne_ref, True)
    n1, own1 = weigh(n, labels, early_part(ue_ref), row_of(ue_ref, False), True, True)
    n2, own2 = weigh(n, labels, late_part(ul_ref), row_of(ue_ref, True), True, True)
    n3, _ = weigh(n, labels, early_part(xe_ref), row_of(xe_ref, False), True, False)
    n4, _ = weigh(n, labels, late_part(xl_ref), row_of(xe_ref, True), True, False)
    n5, p1 = weigh(n, labels, early_part(pe_ref), row_of(pe_ref, False), True, True)
    n6, p2 = weigh(n, labels, late_part(pl_ref), row_of(pe_ref, True), True, True)
    p, labels = late_part(pl_ref), columns_of(pe_ref, True)
    p3, n7 = weigh(p, labels, early_part(ne_ref), row_of(ne_ref, False), True, True)
    p4, _ = weigh(p, labels, early_part(xe_ref), row_of(xe_ref, False), True, False)
    p5, _ = weigh(p, labels, late_part(xl_ref), row_of(xe_ref, True), True, False)
    own_ref[:, :EARLY] = own_in_ref[:, :EARLY] + own1
    own_ref[:, EARLY:] = own_in_ref[:, EARLY:] + own2
    n_ref[:, :EARLY] = n_in_ref[...] + n7
    n_ref[:, EARLY:] = add(n1, n2, n3, n4, n5, n6)
    p_ref[:, :EARLY] = p_in_ref[...] + p1
    p_ref[:, EARLY:] = p2 + add(p3, p4, p5)


def late_f_kernel(fe_ref, fl_ref, pe_ref, ne_ref, pl_ref, nl_ref, p_in_ref, n_in_ref, p_ref, n_ref):
    even = is_even()
    right = jnp.where(even, early_part(ne_ref), early_part(pe_ref))
    late = jnp.where(even, late_part(nl_ref), late_part(pl_ref))
    labels = jnp.where(even, row_of(ne_ref, False), row_of(pe_ref, False))
    late_labels = jnp.where(even, row_of(ne_ref, True), row_of(pe_ref, True))
    f, f_labels = late_part(fl_ref), columns_of(fe_ref, True)
    _, a = weigh(f, f_labels, right, labels, False, True)
    _, b = weigh(f, f_labels, late, late_labels, False, True)
    _, c = weigh(early_part(fe_ref), columns_of(fe_ref, False), late, late_labels, False, True)
    more = jnp.concatenate([a, b + c], axis=1)
    p_ref[...] = p_in_ref[...] + jnp.where(even, 0.0, more)
    n_ref[...] = n_in_ref[...] + jnp.where(even, more, 0.0)


def last_kernel(own_ref, a_ref, b_ref, agreement_ref, log_ref):
    sums = own_ref[...] + a_ref[...] + b_ref[...]
    agreement = sums[1:2] / sums[0:1]
    log_weight = jnp.log(sums[0:1]) - 1.0 / TAU
    for k in range(agreement_ref.shape[0]):
        agreement_ref[k : k + 1, :] = agreement[:, k * LANES : (k + 1) * LANES]
        log_ref[k : k + 1, :] = log_weight[:, k * LANES : (k + 1) * LANES]


def on_device(embeddings, labels):
    n, depth = embeddings.shape
    slabs = depth // LANES
    size = lax.axis_size("blk")
    up = [(i, (i + 2) % size) for i in range(size)]
    down = [(i, (i - 2) % size) for i in range(size)]
    swap = [(i, i ^ 1) for i in range(size)]
    send = lambda array, route: lax.ppermute(array, "blk", route)
    struct = jax.ShapeDtypeStruct
    sums, early_sums = struct((2, n), F32), struct((2, EARLY), F32)
    early, late = struct((HEAD + slabs * EARLY, LANES), BF16), struct((slabs * LATE, LANES), BF16)

    ue, ul = call(
        unit_kernel,
        (early, late),
        (embeddings, labels.reshape(n // LANES, LANES)),
        "unit",
        0.1,
        in_specs=[pl.BlockSpec(memory_space=pl.ANY)] * 2,
        scratch=[
            pltpu.VMEM((n, depth), F32),
            pltpu.VMEM((n // LANES, LANES), jnp.int32),
            pltpu.SemaphoreType.DMA((7,)),
        ],
        limit=52,
    )
    pe = send(ue, up)
    ne = send(ue, down)
    xe = send(ue, swap)
    xl = send(ul, swap)
    own, copy = call(own_kernel, (sums, late), (ue, ul), "own", 1)
    late_p = send(copy, up)
    late_n = send(copy, down)
    own = call(partner_kernel, sums, (ue, ul, xe, xl, own), "with_partner", 1)

    fe = send(call(pick_kernel, early, (pe, ne, own), "pick", 0.1), swap)
    own, p, q = call(
        early_kernel, (sums, early_sums, early_sums), (ue, ul, xe, xl, pe, ne, own), "early", 2.5
    )
    p, q = call(early_f_kernel, (early_sums, early_sums), (fe, pe, ne, p, q), "early_f", 0.5)
    fl = send(call(pick_kernel, late, (late_p, late_n, p), "pick_late", 0.1), swap)
    own, p, q = call(
        late_kernel, (sums, sums, sums), (ue, ul, xe, xl, pe, ne, late_p, late_n, own, p, q), "late", 1.5
    )
    p, q = call(late_f_kernel, (sums, sums), (fe, fl, pe, ne, late_p, late_n, p, q), "late_f", 0.6)
    from_lower = send(q, up)
    from_upper = send(p, down)
    shape = struct((n // LANES, LANES), F32)
    agreement, log_weight = call(last_kernel, (shape, shape), (own, from_lower, from_upper), "last", 0.01)
    return agreement.reshape(n), log_weight.reshape(n)


def solution(mesh):
    return jax.shard_map(
        on_device,
        mesh=mesh,
        in_specs=(P("blk", None), P("blk")),
        out_specs=(P("blk"), P("blk")),
        check_vma=False,
    )
```

time: 263 us -> 64.5 us (0.25)
  waiting for transfers between devices: 163 us -> 19.2 us
  starting transfers between devices: 74.5 us -> 28.2 us
  matrix products: 19.6 us -> 0 us
  Pallas kernels: 0 us -> 15.5 us
  other arithmetic: 3.97 us -> 0 us
    ppermute x16 -> x10, waiting for transfers between devices: 163 us -> 19.2 us  [on_device(): send = lambda array, route: lax.ppermute(array, 'blk', route)]
    ppermute x16 -> x10, starting transfers between devices: 74.5 us -> 28.2 us  [on_device(): send = lambda array, route: lax.ppermute(array, 'blk', route)]
    dot_general x9 -> x0, matrix products: 19.6 us -> none  [tile_weights(): score = jnp.dot(mine, other.T, preferred_element_type=jnp.float32)]
    pallas_call x0 -> x10, Pallas kernels: none -> 15.5 us  [call(): pl.pallas_call(kernel, out_shape=out_shape, in_specs=in_specs or [vmem] *...]
  transfers between devices with their start and end apart: 16 -> 10, of which waited for: 5 -> 3; matrix products, arithmetic and copies ran while one was open for 4% -> 0% of each run, Pallas kernels for 0% -> 18%
where the time goes in v2:
time: 64.5 us; the launch traced here: 64.4 us
  starting transfers between devices  28.2 us (44%)
  waiting for transfers between devices  19.2 us (30%)
  Pallas kernels  15.5 us (24%)
  between operations  0.75 us (1%)
  local copies, waits for them, and re-layouts  0.69 us (1%)
    ppermute x10, starting transfers between devices, on_device(): send = lambda array, route: lax.ppermute(array, 'blk', route)  28.2 us
    ppermute x10, waiting for transfers between devices, on_device(): send = lambda array, route: lax.ppermute(array, 'blk', route)  19.2 us
    pallas_call x10, Pallas kernels, call(): pl.pallas_call(kernel, out_shape=out_shape, in_specs=in_specs or [vmem] *...  15.5 us
  transfers between devices with their start and end apart: 10, of which 3 were waited for; matrix products, arithmetic and copies ran while one was open for 0% of the time, Pallas kernels for 18%

profile of v2, /device:TPU:1, one launch (start us, length us, event | category | flops | bytes accessed | tf_op | source)
XLA Modules:
  0.0 64.4 jit_solution(6688770248482426975)
XLA Ops:
  0.6 0.0 copy-start.2
  0.6 0.7 %copy-done.2 = s32[768]{0:T(1024)S(1)} copy-done((s32[768]{0:T(1024)S(1)}, s32[768]{0:T(1024)}, u32[]{:S(2)}) %copy-start.2) | copy-done | bytes 3096
  1.3 2.0 %unit.1 = (bf16[4112,128]{1,0:T(8,128)(2,1)S(1)}, bf16[2048,128]{1,0:T(8,128)(2,1)S(1)}) custom-call(f32[768,1024]{1,0:T(8,128)} %x_ref.1, s32[6,128]{1,0:T(8,128)S(1)} %bitcast.3), custom_call_target="tpu_custom_call" | custom-call | flops 1200000000 | bytes 1024 | tf_op jit(solution)/shard_map/unit/pallas_call | solution.py:25
  3.3 3.3 %collective-permute-start = (bf16[4112,128]{1,0:T(8,128)(2,1)S(1)}, bf16[4112,128]{1,0:T(8,128)(2,1)S(1)}, u32[]{:S(2)}, u32[]{:S(2)}) collective-permute-start(bf16[4112,128]{1,0:T(8,128)(2,1)S(1)} %get-tuple-element.18.ue_ref), channel_id=1, source_target_pairs={{0,1},{1,0},{2,3},{3,2},{4,5},{5,4},{6,7},{7,6},{8,9},{9,8},{10,11... | collective-permute-start | bytes 3158024 | tf_op jit(solution)/shard_map/ppermute | solution.py:275
  6.7 0.0 collective-permute-start.2
  6.7 8.5 %collective-permute-start.3 = (bf16[4112,128]{1,0:T(8,128)(2,1)S(1)}, bf16[4112,128]{1,0:T(8,128)(2,1)S(1)}, u32[]{:S(2)}, u32[]{:S(2)}) collective-permute-start(bf16[4112,128]{1,0:T(8,128)(2,1)S(1)} %get-tuple-element.18.ue_ref), channel_id=1, source_target_pairs={{0,254},{1,255},{2,0},{3,1},{4,2},{5,3},{6,4},{7,5},{8,6},{9,7},{1... | collective-permute-start | bytes 3158024 | tf_op jit(solution)/shard_map/ppermute | solution.py:275
  15.2 0.5 collective-permute-start.1
  15.6 1.7 %own.1 = (f32[2,768]{1,0:T(2,128)S(1)}, bf16[2048,128]{1,0:T(8,128)(2,1)S(1)}) custom-call(bf16[4112,128]{1,0:T(8,128)(2,1)S(1)} %get-tuple-element.18.ue_ref, bf16[2048,128]{1,0:T(8,128)(2,1)S(1)} %get-tuple-element.19.ul_ref), custom_call_target="tpu_custom_call" | custom-call | flops 12000000000 | bytes 1024 | tf_op jit(solution)/shard_map/own/pallas_call | solution.py:25
  17.3 0.1 collective-permute-start.4
  17.4 0.0 collective-permute-done.1.xl_ref
  17.4 6.9 %collective-permute-start.5 = (bf16[2048,128]{1,0:T(8,128)(2,1)S(1)}, bf16[2048,128]{1,0:T(8,128)(2,1)S(1)}, u32[]{:S(2)}, u32[]{:S(2)}) collective-permute-start(bf16[2048,128]{1,0:T(8,128)(2,1)S(1)} %get-tuple-element.20), channel_id=1, source_target_pairs={{0,254},{1,255},{2,0},{3,1},{4,2},{5,3},{6,4},{7,5},{8,6},{9,7},{1... | collective-permute-start | bytes 1572872 | tf_op jit(solution)/shard_map/ppermute | solution.py:275
  24.3 0.0 collective-permute-done.xe_ref
  24.3 1.6 %with_partner.1.own_in_ref.after_ref = f32[2,768]{1,0:T(2,128)S(1)} custom-call(bf16[4112,128]{1,0:T(8,128)(2,1)S(1)} %get-tuple-element.18.ue_ref, bf16[2048,128]{1,0:T(8,128)(2,1)S(1)} %get-tuple-element.19.ul_ref, bf16[4112,128]{1,0:T(8,128)(2,1)S(1)} %collective-permute-done.xe_ref, bf16[2048,128]{1,0:T(8,128)(2,1)S(1)} %collective-permute-done.1.xl_ref, ...), custom_call_target="tpu_custom_call" | custom-call | flops 12000000000 | bytes 1024 | tf_op jit(solution)/shard_map/with_partner/pallas_call | solution.py:25
  25.9 12.8 %collective-permute-done.2.pe_ref.p_ref = bf16[4112,128]{1,0:T(8,128)(2,1)S(1)} collective-permute-done((bf16[4112,128]{1,0:T(8,128)(2,1)S(1)}, bf16[4112,128]{1,0:T(8,128)(2,1)S(1)}, u32[]{:S(2)}, u32[]{:S(2)}) %collective-permute-start.2) | collective-permute-done | bytes 1052704 | tf_op jit(solution)/shard_map/ppermute | solution.py:275
  38.7 0.0 collective-permute-done.3.ne_ref.n_ref
  38.7 0.0 copy-start
  38.7 0.1 pick.1
  38.8 1.0 %collective-permute-start.6 = (bf16[4112,128]{1,0:T(8,128)(2,1)S(1)}, bf16[4112,128]{1,0:T(8,128)(2,1)S(1)}, u32[]{:S(2)}, u32[]{:S(2)}) collective-permute-start(bf16[4112,128]{1,0:T(8,128)(2,1)S(1)} %pick.1), channel_id=1, source_target_pairs={{0,1},{1,0},{2,3},{3,2},{4,5},{5,4},{6,7},{7,6},{8,9},{9,8},{10,11... | collective-permute-start | bytes 3158024 | tf_op jit(solution)/shard_map/ppermute | solution.py:275
  39.8 3.8 %early.1 = (f32[2,768]{1,0:T(2,128)S(1)}, f32[2,512]{1,0:T(2,128)S(1)}, f32[2,512]{1,0:T(2,128)S(1)}) custom-call(bf16[4112,128]{1,0:T(8,128)(2,1)S(1)} %get-tuple-element.18.ue_ref, bf16[2048,128]{1,0:T(8,128)(2,1)S(1)} %get-tuple-element.19.ul_ref, bf16[4112,128]{1,0:T(8,128)(2,1)S(1)} %collective-permute-done.xe_ref, ...), custom_call_target="tpu_custom_call" | custom-call | flops 30000001024 | bytes 1024 | tf_op jit(solution)/shard_map/early/pallas_call | solution.py:25
  43.6 0.0 collective-permute-done.6.fe_ref
  43.6 0.0 copy-done
  43.6 0.9 %early_f.1 = (f32[2,512]{1,0:T(2,128)S(1)}, f32[2,512]{1,0:T(2,128)S(1)}) custom-call(bf16[4112,128]{1,0:T(8,128)(2,1)S(1)} %collective-permute-done.6.fe_ref, bf16[4112,128]{1,0:T(8,128)(2,1)S(1)} %collective-permute-done.2.pe_ref.p_ref, bf16[4112,128]{1,0:T(8,128)(2,1)S(1)} %collective-permute-done.3.ne_ref.n_ref, ...), custom_call_target="tpu_custom_call" | custom-call | flops 6000000000 | bytes 1024 | tf_op jit(solution)/shard_map/early_f/pallas_call | solution.py:25
  44.5 5.4 %collective-permute-done.4.pl_ref.p_ref = bf16[2048,128]{1,0:T(8,128)(2,1)S(1)} collective-permute-done((bf16[2048,128]{1,0:T(8,128)(2,1)S(1)}, bf16[2048,128]{1,0:T(8,128)(2,1)S(1)}, u32[]{:S(2)}, u32[]{:S(2)}) %collective-permute-start.4) | collective-permute-done | bytes 524320 | tf_op jit(solution)/shard_map/ppermute | solution.py:275
  49.9 0.0 collective-permute-done.5.nl_ref.n_ref
  50.0 0.9 %collective-permute-start.7 = (bf16[2048,128]{1,0:T(8,128)(2,1)S(1)}, bf16[2048,128]{1,0:T(8,128)(2,1)S(1)}, u32[]{:S(2)}, u32[]{:S(2)}) collective-permute-start(bf16[2048,128]{1,0:T(8,128)(2,1)S(1)} %pick_late.1), channel_id=1, source_target_pairs={{0,1},{1,0},{2,3},{3,2},{4,5},{5,4},{6,7},{7,6},{8,9},{9,8},{10,11... | collective-permute-start | bytes 1572872 | tf_op jit(solution)/shard_map/ppermute | solution.py:275
  50.9 0.0 copy-start.1
  50.9 3.8 %late.1 = (f32[2,768]{1,0:T(2,128)S(1)}, f32[2,768]{1,0:T(2,128)S(1)}, f32[2,768]{1,0:T(2,128)S(1)}) custom-call(bf16[4112,128]{1,0:T(8,128)(2,1)S(1)} %get-tuple-element.18.ue_ref, bf16[2048,128]{1,0:T(8,128)(2,1)S(1)} %get-tuple-element.19.ul_ref, bf16[4112,128]{1,0:T(8,128)(2,1)S(1)} %collective-permute-done.xe_ref, ...), custom_call_target="tpu_custom_call" | custom-call | flops 17999998976 | bytes 1024 | tf_op jit(solution)/shard_map/late/pallas_call | solution.py:25
  54.7 0.0 collective-permute-done.7.fl_ref
  54.7 0.0 copy-done.1
  54.7 1.1 %late_f.1 = (f32[2,768]{1,0:T(2,128)S(1)}, f32[2,768]{1,0:T(2,128)S(1)}) custom-call(bf16[4112,128]{1,0:T(8,128)(2,1)S(1)} %collective-permute-done.6.fe_ref, bf16[2048,128]{1,0:T(8,128)(2,1)S(1)} %collective-permute-done.7.fl_ref, bf16[4112,128]{1,0:T(8,128)(2,1)S(1)} %collective-permute-done.2.pe_ref.p_ref, bf16[4112,128]{1,0:T(8,128)(2,1)S(1)} %copy-done.1, ...), custom_call_target="tpu_custom_call" | custom-call | flops 7200000000 | bytes 1024 | tf_op jit(solution)/shard_map/late_f/pallas_call | solution.py:25
  55.7 0.1 collective-permute-start.8
  55.8 7.0 %collective-permute-start.9 = (f32[2,768]{1,0:T(2,128)S(1)}, f32[2,768]{1,0:T(2,128)S(1)}, u32[]{:S(2)}, u32[]{:S(2)}) collective-permute-start(f32[2,768]{1,0:T(2,128)S(1)} %get-tuple-element.31), channel_id=1, source_target_pairs={{0,254},{1,255},{2,0},{3,1},{4,2},{5,3},{6,4},{7,5},{8,6},{9,7},{1... | collective-permute-start | bytes 18440 | tf_op jit(solution)/shard_map/ppermute | solution.py:275
  62.8 0.9 %collective-permute-done.8.a_ref = f32[2,768]{1,0:T(2,128)S(1)} collective-permute-done((f32[2,768]{1,0:T(2,128)S(1)}, f32[2,768]{1,0:T(2,128)S(1)}, u32[]{:S(2)}, u32[]{:S(2)}) %collective-permute-start.8) | collective-permute-done | bytes 6176 | tf_op jit(solution)/shard_map/ppermute | solution.py:275
  63.7 0.0 collective-permute-done.9.b_ref
  63.7 0.6 last.1
  (1 shorter events, 0.0 us)
Async XLA Ops:
  0.6 0.7 %copy-start.2 = (s32[768]{0:T(1024)S(1)}, s32[768]{0:T(1024)}, u32[]{:S(2)}) copy-start(s32[768]{0:T(1024)} %param.3) | copy-start | bytes 9220
  3.3 20.9 %collective-permute-start = (bf16[4112,128]{1,0:T(8,128)(2,1)S(1)}, bf16[4112,128]{1,0:T(8,128)(2,1)S(1)}, u32[]{:S(2)}, u32[]{:S(2)}) collective-permute-start(bf16[4112,128]{1,0:T(8,128)(2,1)S(1)} %get-tuple-element.18.ue_ref), channel_id=1, source_target_pairs={{0,1},{1,0},{2,3},{3,2},{4,5},{5,4},{6,7},{7,6},{8,9},{9,8},{10,11... | collective-permute-start | bytes 3158024 | tf_op jit(solution)/shard_map/ppermute | solution.py:275
  6.7 32.0 %collective-permute-start.2 = (bf16[4112,128]{1,0:T(8,128)(2,1)S(1)}, bf16[4112,128]{1,0:T(8,128)(2,1)S(1)}, u32[]{:S(2)}, u32[]{:S(2)}) collective-permute-start(bf16[4112,128]{1,0:T(8,128)(2,1)S(1)} %get-tuple-element.18.ue_ref), channel_id=1, source_target_pairs={{0,2},{1,3},{2,4},{3,5},{4,6},{5,7},{6,8},{7,9},{8,10},{9,11},{10,... | collective-permute-start | bytes 3158024 | tf_op jit(solution)/shard_map/ppermute | solution.py:275
  6.7 32.0 %collective-permute-start.3 = (bf16[4112,128]{1,0:T(8,128)(2,1)S(1)}, bf16[4112,128]{1,0:T(8,128)(2,1)S(1)}, u32[]{:S(2)}, u32[]{:S(2)}) collective-permute-start(bf16[4112,128]{1,0:T(8,128)(2,1)S(1)} %get-tuple-element.18.ue_ref), channel_id=1, source_target_pairs={{0,254},{1,255},{2,0},{3,1},{4,2},{5,3},{6,4},{7,5},{8,6},{9,7},{1... | collective-permute-start | bytes 3158024 | tf_op jit(solution)/shard_map/ppermute | solution.py:275
  15.2 2.2 %collective-permute-start.1 = (bf16[2048,128]{1,0:T(8,128)(2,1)S(1)}, bf16[2048,128]{1,0:T(8,128)(2,1)S(1)}, u32[]{:S(2)}, u32[]{:S(2)}) collective-permute-start(bf16[2048,128]{1,0:T(8,128)(2,1)S(1)} %get-tuple-element.19.ul_ref), channel_id=1, source_target_pairs={{0,1},{1,0},{2,3},{3,2},{4,5},{5,4},{6,7},{7,6},{8,9},{9,8},{10,11... | collective-permute-start | bytes 1572872 | tf_op jit(solution)/shard_map/ppermute | solution.py:275
  17.3 32.6 %collective-permute-start.4 = (bf16[2048,128]{1,0:T(8,128)(2,1)S(1)}, bf16[2048,128]{1,0:T(8,128)(2,1)S(1)}, u32[]{:S(2)}, u32[]{:S(2)}) collective-permute-start(bf16[2048,128]{1,0:T(8,128)(2,1)S(1)} %get-tuple-element.20), channel_id=1, source_target_pairs={{0,2},{1,3},{2,4},{3,5},{4,6},{5,7},{6,8},{7,9},{8,10},{9,11},{10,... | collective-permute-start | bytes 1572872 | tf_op jit(solution)/shard_map/ppermute | solution.py:275
  17.4 32.5 %collective-permute-start.5 = (bf16[2048,128]{1,0:T(8,128)(2,1)S(1)}, bf16[2048,128]{1,0:T(8,128)(2,1)S(1)}, u32[]{:S(2)}, u32[]{:S(2)}) collective-permute-start(bf16[2048,128]{1,0:T(8,128)(2,1)S(1)} %get-tuple-element.20), channel_id=1, source_target_pairs={{0,254},{1,255},{2,0},{3,1},{4,2},{5,3},{6,4},{7,5},{8,6},{9,7},{1... | collective-permute-start | bytes 1572872 | tf_op jit(solution)/shard_map/ppermute | solution.py:275
  38.7 4.9 %copy-start = (bf16[4112,128]{1,0:T(8,128)(2,1)}, bf16[4112,128]{1,0:T(8,128)(2,1)S(1)}, u32[]{:S(2)}) copy-start(bf16[4112,128]{1,0:T(8,128)(2,1)S(1)} %collective-permute-done.3.ne_ref.n_ref) | copy-start | bytes 3158020
  38.8 4.8 %collective-permute-start.6 = (bf16[4112,128]{1,0:T(8,128)(2,1)S(1)}, bf16[4112,128]{1,0:T(8,128)(2,1)S(1)}, u32[]{:S(2)}, u32[]{:S(2)}) collective-permute-start(bf16[4112,128]{1,0:T(8,128)(2,1)S(1)} %pick.1), channel_id=1, source_target_pairs={{0,1},{1,0},{2,3},{3,2},{4,5},{5,4},{6,7},{7,6},{8,9},{9,8},{10,11... | collective-permute-start | bytes 3158024 | tf_op jit(solution)/shard_map/ppermute | solution.py:275
  50.0 4.7 %collective-permute-start.7 = (bf16[2048,128]{1,0:T(8,128)(2,1)S(1)}, bf16[2048,128]{1,0:T(8,128)(2,1)S(1)}, u32[]{:S(2)}, u32[]{:S(2)}) collective-permute-start(bf16[2048,128]{1,0:T(8,128)(2,1)S(1)} %pick_late.1), channel_id=1, source_target_pairs={{0,1},{1,0},{2,3},{3,2},{4,5},{5,4},{6,7},{7,6},{8,9},{9,8},{10,11... | collective-permute-start | bytes 1572872 | tf_op jit(solution)/shard_map/ppermute | solution.py:275
  50.9 3.8 %copy-start.1 = (bf16[4112,128]{1,0:T(8,128)(2,1)S(1)}, bf16[4112,128]{1,0:T(8,128)(2,1)}, u32[]{:S(2)}) copy-start(bf16[4112,128]{1,0:T(8,128)(2,1)} %copy-done) | copy-start | bytes 3158020
  55.7 8.0 %collective-permute-start.8 = (f32[2,768]{1,0:T(2,128)S(1)}, f32[2,768]{1,0:T(2,128)S(1)}, u32[]{:S(2)}, u32[]{:S(2)}) collective-permute-start(f32[2,768]{1,0:T(2,128)S(1)} %get-tuple-element.30), channel_id=1, source_target_pairs={{0,2},{1,3},{2,4},{3,5},{4,6},{5,7},{6,8},{7,9},{8,10},{9,11},{10,... | collective-permute-start | bytes 18440 | tf_op jit(solution)/shard_map/ppermute | solution.py:275
  55.8 7.9 %collective-permute-start.9 = (f32[2,768]{1,0:T(2,128)S(1)}, f32[2,768]{1,0:T(2,128)S(1)}, u32[]{:S(2)}, u32[]{:S(2)}) collective-permute-start(f32[2,768]{1,0:T(2,128)S(1)} %get-tuple-element.31), channel_id=1, source_target_pairs={{0,254},{1,255},{2,0},{3,1},{4,2},{5,3},{6,4},{7,5},{8,6},{9,7},{1... | collective-permute-start | bytes 18440 | tf_op jit(solution)/shard_map/ppermute | solution.py:275

commit v3 on v2

--- a/solution.py
+++ b/solution.py
@@ -20,7 +20,7 @@
 BF16 = jnp.bfloat16
 
 
-def call(kernel, out_shape, operands, name, tiles, in_specs=None, scratch=(), limit=48):
+def call(kernel, out_shape, operands, name, tiles, in_specs=None, scratch=(), limit=28):
     vmem = pl.BlockSpec(memory_space=pltpu.VMEM)
     return pl.pallas_call(
         kernel,
@@ -120,45 +120,52 @@
     return images(ref, LATE, 0, LATE, head=0)
 
 
-def columns_of(early_ref, late):
-    column = label_column(early_ref, EARLY + LATE)
-    return column[EARLY:] if late else column[:EARLY]
-
-
 def row_of(early_ref, late):
     row = label_row(early_ref, EARLY + LATE)
     return row[:, EARLY:] if late else row[:, :EARLY]
 
 
-def unit_kernel(x_ref, labels_hbm, early_ref, late_ref, held, labels_ref, sems):
-    n, depth = x_ref.shape
-    parts = sems.shape[0] - 1
-    part = n // parts
+def normalise(x_ref, first, held, sems, write):
+    rows, parts = held.shape[0], sems.shape[0]
+    part = rows // parts
     copies = [
-        pltpu.make_async_copy(x_ref.at[pl.ds(i * part, part), :], held.at[pl.ds(i * part, part), :], sems.at[i])
+        pltpu.make_async_copy(
+            x_ref.at[pl.ds(first + i * part, part), :], held.at[pl.ds(i * part, part), :], sems.at[i]
+        )
         for i in range(parts)
     ]
-    labels_copy = pltpu.make_async_copy(labels_hbm, labels_ref, sems.at[parts])
-    labels_copy.start()
     for copy in copies:
         copy.start()
+    for i in range(parts):
+        copies[i].wait()
+        for q in range(i * part, (i + 1) * part, 64):
+            x = held[q : q + 64, :]
+            unit = (x * lax.rsqrt(jnp.sum(x * x, axis=1, keepdims=True) + 1e-06)).astype(BF16)
+            for k in range(x.shape[1] // LANES):
+                write(k, q, unit[:, k * LANES : (k + 1) * LANES])
+
+
+def unit_early_kernel(x_ref, labels_hbm, out_ref, held, labels_ref, sems, labels_sem):
+    labels_copy = pltpu.make_async_copy(labels_hbm, labels_ref, labels_sem)
+    labels_copy.start()
+
+    def write(slab, row, unit):
+        out_ref[HEAD + slab * EARLY + row : HEAD + slab * EARLY + row + 64, :] = unit
+
+    normalise(x_ref, 0, held, sems, write)
     labels_copy.wait()
     labels = labels_ref[...]
     low = lax.rem(labels, 256)
     blank = jnp.zeros((HEAD - 2 * labels.shape[0], LANES), F32)
     head = jnp.concatenate([(labels - low).astype(F32), low.astype(F32), blank], axis=0)
-    early_ref[0:HEAD, :] = head.astype(BF16)
-    for i in range(parts):
-        copies[i].wait()
-        for q in range(i * part, (i + 1) * part, 64):
-            x = held[q : q + 64, :]
-            unit = (x * lax.rsqrt(jnp.sum(x * x, axis=1, keepdims=True) + 1e-06)).astype(BF16)
-            for k in range(depth // LANES):
-                slab = unit[:, k * LANES : (k + 1) * LANES]
-                if q < EARLY:
-                    early_ref[HEAD + k * EARLY + q : HEAD + k * EARLY + q + 64, :] = slab
-                else:
-                    late_ref[k * LATE + q - EARLY : k * LATE + q - EARLY + 64, :] = slab
+    out_ref[0:HEAD, :] = head.astype(BF16)
+
+
+def unit_late_kernel(x_ref, after_ref, out_ref, held, sems):
+    def write(slab, row, unit):
+        out_ref[slab * LATE + row : slab * LATE + row + 64, :] = unit
+
+    normalise(x_ref, EARLY, held, sems, write)
 
 
 def own_kernel(ue_ref, ul_ref, own_ref, copy_ref):
@@ -169,11 +176,12 @@
     own_ref[...] = own
 
 
-def partner_kernel(ue_ref, ul_ref, xe_ref, xl_ref, own_in_ref, own_ref):
+def partner_kernel(ue_ref, ul_ref, xe_ref, xl_ref, own_in_ref, own_ref, x_labels_ref):
     unit = jnp.concatenate([early_part(ue_ref), late_part(ul_ref)], axis=0)
-    labels = label_row(ue_ref, EARLY + LATE)
-    _, a = weigh(early_part(xe_ref), columns_of(xe_ref, False), unit, labels, False, True)
-    _, b = weigh(late_part(xl_ref), columns_of(xe_ref, True), unit, labels, False, True)
+    labels, x_labels = label_row(ue_ref, EARLY + LATE), label_column(xe_ref, EARLY + LATE)
+    x_labels_ref[...] = x_labels
+    _, a = weigh(early_part(xe_ref), x_labels[:EARLY], unit, labels, False, True)
+    _, b = weigh(late_part(xl_ref), x_labels[EARLY:], unit, labels, False, True)
     own_ref[...] = own_in_ref[...] + a + b
 
 
@@ -193,64 +201,84 @@
         out_ref[...] = p_ref[...]
 
 
-def early_kernel(ue_ref, ul_ref, xe_ref, xl_ref, pe_ref, ne_ref, own_in_ref, own_ref, p_ref, n_ref):
-    n, labels = early_part(ne_ref), columns_of(ne_ref, False)
+def early_kernel(
+    ue_ref, ul_ref, xe_ref, xl_ref, pe_ref, ne_ref, x_labels_ref, own_in_ref,
+    own_ref, p_ref, n_ref, p_labels_ref, n_labels_ref,
+):
+    p_labels_ref[...] = label_column(pe_ref, EARLY + LATE)
+    n_labels = label_column(ne_ref, EARLY + LATE)
+    n_labels_ref[...] = n_labels
+    n, labels = early_part(ne_ref), n_labels[:EARLY]
     n1, own1 = weigh(n, labels, early_part(ue_ref), row_of(ue_ref, False), True, True)
     n2, own2 = weigh(n, labels, late_part(ul_ref), row_of(ue_ref, True), True, True)
-    n3, _ = weigh(n, labels, early_part(xe_ref), row_of(xe_ref, False), True, False)
-    n4, _ = weigh(n, labels, late_part(xl_ref), row_of(xe_ref, True), True, False)
-    n5, p1 = weigh(n, labels, early_part(pe_ref), row_of(pe_ref, False), True, True)
-    n_ref[...] = add(n1, n2, n3, n4, n5)
+    n3, p1 = weigh(n, labels, early_part(pe_ref), row_of(pe_ref, False), True, True)
     own_ref[:, :EARLY] = own_in_ref[:, :EARLY] + own1
     own_ref[:, EARLY:] = own_in_ref[:, EARLY:] + own2
+    labels = row_of(ne_ref, False)
+    _, n4 = weigh(early_part(xe_ref), x_labels_ref[:EARLY], n, labels, False, True)
+    _, n5 = weigh(late_part(xl_ref), x_labels_ref[EARLY:], n, labels, False, True)
+    n_ref[...] = n4 + n5 + add(n1, n2, n3)
     p, labels = early_part(pe_ref), row_of(pe_ref, False)
-    _, p2 = weigh(early_part(xe_ref), columns_of(xe_ref, False), p, labels, False, True)
-    _, p3 = weigh(late_part(xl_ref), columns_of(xe_ref, True), p, labels, False, True)
+    _, p2 = weigh(early_part(xe_ref), x_labels_ref[:EARLY], p, labels, False, True)
+    _, p3 = weigh(late_part(xl_ref), x_labels_ref[EARLY:], p, labels, False, True)
     p_ref[...] = p1 + p2 + p3
 
 
-def early_f_kernel(fe_ref, pe_ref, ne_ref, p_in_ref, n_in_ref, p_ref, n_ref):
+def early_f_kernel(fe_ref, pe_ref, ne_ref, p_in_ref, n_in_ref, p_ref, n_ref, f_labels_ref):
     even = is_even()
     right = jnp.where(even, early_part(ne_ref), early_part(pe_ref))
     labels = jnp.where(even, row_of(ne_ref, False), row_of(pe_ref, False))
-    _, more = weigh(early_part(fe_ref), columns_of(fe_ref, False), right, labels, False, True)
+    f_labels = label_column(fe_ref, EARLY + LATE)
+    f_labels_ref[...] = f_labels
+    _, more = weigh(early_part(fe_ref), f_labels[:EARLY], right, labels, False, True)
     p_ref[...] = p_in_ref[...] + jnp.where(even, 0.0, more)
     n_ref[...] = n_in_ref[...] + jnp.where(even, more, 0.0)
 
 
-def late_kernel(
-    ue_ref, ul_ref, xe_ref, xl_ref, pe_ref, ne_ref, pl_ref, nl_ref, own_in_ref, p_in_ref, n_in_ref,
-    own_ref, p_ref, n_ref,
+def late_n_kernel(
+    ue_ref, ul_ref, xe_ref, xl_ref, pe_ref, ne_ref, nl_ref, x_labels_ref, n_labels_ref, own_in_ref, p_in_ref,
+    own_ref, p_ref, n_ref, part_ref,
 ):
-    n, labels = late_part(nl_ref), columns_of(ne_ref, True)
+    n, labels = late_part(nl_ref), n_labels_ref[EARLY:]
     n1, own1 = weigh(n, labels, early_part(ue_ref), row_of(ue_ref, False), True, True)
     n2, own2 = weigh(n, labels, late_part(ul_ref), row_of(ue_ref, True), True, True)
-    n3, _ = weigh(n, labels, early_part(xe_ref), row_of(xe_ref, False), True, False)
-    n4, _ = weigh(n, labels, late_part(xl_ref), row_of(xe_ref, True), True, False)
-    n5, p1 = weigh(n, labels, early_part(pe_ref), row_of(pe_ref, False), True, True)
-    n6, p2 = weigh(n, labels, late_part(pl_ref), row_of(pe_ref, True), True, True)
-    p, labels = late_part(pl_ref), columns_of(pe_ref, True)
-    p3, n7 = weigh(p, labels, early_part(ne_ref), row_of(ne_ref, False), True, True)
-    p4, _ = weigh(p, labels, early_part(xe_ref), row_of(xe_ref, False), True, False)
-    p5, _ = weigh(p, labels, late_part(xl_ref), row_of(xe_ref, True), True, False)
+    n3, p1 = weigh(n, labels, early_part(pe_ref), row_of(pe_ref, False), True, True)
+    for k in range(2):
+        part_ref[k] = n1[k] + n2[k] + n3[k]
+    labels = row_of(ne_ref, True)
+    _, n4 = weigh(early_part(xe_ref), x_labels_ref[:EARLY], n, labels, False, True)
+    _, n5 = weigh(late_part(xl_ref), x_labels_ref[EARLY:], n, labels, False, True)
     own_ref[:, :EARLY] = own_in_ref[:, :EARLY] + own1
     own_ref[:, EARLY:] = own_in_ref[:, EARLY:] + own2
-    n_ref[:, :EARLY] = n_in_ref[...] + n7
-    n_ref[:, EARLY:] = add(n1, n2, n3, n4, n5, n6)
-    p_ref[:, :EARLY] = p_in_ref[...] + p1
-    p_ref[:, EARLY:] = p2 + add(p3, p4, p5)
-
-
-def late_f_kernel(fe_ref, fl_ref, pe_ref, ne_ref, pl_ref, nl_ref, p_in_ref, n_in_ref, p_ref, n_ref):
+    p_ref[...] = p_in_ref[...] + p1
+    n_ref[...] = n4 + n5
+
+
+def late_p_kernel(
+    xe_ref, xl_ref, pe_ref, ne_ref, pl_ref, nl_ref, x_labels_ref, p_labels_ref, n_labels_ref,
+    p_in_ref, n_in_ref, n_late_ref, n_part_ref, p_ref, n_ref,
+):
+    p, labels = late_part(pl_ref), row_of(pe_ref, True)
+    _, p1 = weigh(early_part(xe_ref), x_labels_ref[:EARLY], p, labels, False, True)
+    _, p2 = weigh(late_part(xl_ref), x_labels_ref[EARLY:], p, labels, False, True)
+    p3, n1 = weigh(p, p_labels_ref[EARLY:], early_part(ne_ref), row_of(ne_ref, False), True, True)
+    n2, p4 = weigh(late_part(nl_ref), n_labels_ref[EARLY:], p, labels, True, True)
+    p_ref[:, :EARLY] = p_in_ref[...]
+    p_ref[:, EARLY:] = p1 + p2 + p4 + add(p3)
+    n_ref[:, :EARLY] = n_in_ref[...] + n1
+    n_ref[:, EARLY:] = n_late_ref[...] + add((n_part_ref[0], n_part_ref[1]), n2)
+
+
+def end_kernel(fe_ref, fl_ref, pe_ref, ne_ref, pl_ref, nl_ref, f_labels_ref, p_in_ref, n_in_ref, p_ref, n_ref):
     even = is_even()
     right = jnp.where(even, early_part(ne_ref), early_part(pe_ref))
     late = jnp.where(even, late_part(nl_ref), late_part(pl_ref))
     labels = jnp.where(even, row_of(ne_ref, False), row_of(pe_ref, False))
     late_labels = jnp.where(even, row_of(ne_ref, True), row_of(pe_ref, True))
-    f, f_labels = late_part(fl_ref), columns_of(fe_ref, True)
+    f, f_labels = late_part(fl_ref), f_labels_ref[EARLY:]
     _, a = weigh(f, f_labels, right, labels, False, True)
     _, b = weigh(f, f_labels, late, late_labels, False, True)
-    _, c = weigh(early_part(fe_ref), columns_of(fe_ref, False), late, late_labels, False, True)
+    _, c = weigh(early_part(fe_ref), f_labels_ref[:EARLY], late, late_labels, False, True)
     more = jnp.concatenate([a, b + c], axis=1)
     p_ref[...] = p_in_ref[...] + jnp.where(even, 0.0, more)
     n_ref[...] = n_in_ref[...] + jnp.where(even, more, 0.0)
@@ -277,39 +305,70 @@
     sums, early_sums = struct((2, n), F32), struct((2, EARLY), F32)
     early, late = struct((HEAD + slabs * EARLY, LANES), BF16), struct((slabs * LATE, LANES), BF16)
 
-    ue, ul = call(
-        unit_kernel,
-        (early, late),
-        (embeddings, labels.reshape(n // LANES, LANES)),
-        "unit",
+    hbm = pl.BlockSpec(memory_space=pltpu.HBM)
+    labels = pltpu.with_memory_space_constraint(labels.reshape(n // LANES, LANES), pltpu.HBM)
+    ue = call(
+        unit_early_kernel,
+        early,
+        (embeddings, labels),
+        "unit_early",
         0.1,
-        in_specs=[pl.BlockSpec(memory_space=pl.ANY)] * 2,
+        in_specs=[hbm, hbm],
         scratch=[
-            pltpu.VMEM((n, depth), F32),
+            pltpu.VMEM((EARLY, depth), F32),
             pltpu.VMEM((n // LANES, LANES), jnp.int32),
-            pltpu.SemaphoreType.DMA((7,)),
+            pltpu.SemaphoreType.DMA((8,)),
+            pltpu.SemaphoreType.DMA,
         ],
         limit=52,
     )
+    ul = call(
+        unit_late_kernel,
+        late,
+        (embeddings, ue),
+        "unit_late",
+        0.1,
+        in_specs=[hbm, pl.BlockSpec(memory_space=pltpu.VMEM)],
+        scratch=[pltpu.VMEM((LATE, depth), F32), pltpu.SemaphoreType.DMA((4,))],
+        limit=52,
+    )
     pe = send(ue, up)
     ne = send(ue, down)
-    xe = send(ue, swap)
+    xe = send(lax.optimization_barrier((ue, ul))[0], swap)
     xl = send(ul, swap)
     own, copy = call(own_kernel, (sums, late), (ue, ul), "own", 1)
     late_p = send(copy, up)
     late_n = send(copy, down)
-    own = call(partner_kernel, sums, (ue, ul, xe, xl, own), "with_partner", 1)
+    column, late_sums, part = struct((n, LANES), F32), struct((2, LATE), F32), struct((2, LATE, LANES), F32)
+    own, x_labels = call(partner_kernel, (sums, column), (ue, ul, xe, xl, own), "with_partner", 1)
 
     fe = send(call(pick_kernel, early, (pe, ne, own), "pick", 0.1), swap)
-    own, p, q = call(
-        early_kernel, (sums, early_sums, early_sums), (ue, ul, xe, xl, pe, ne, own), "early", 2.5
-    )
-    p, q = call(early_f_kernel, (early_sums, early_sums), (fe, pe, ne, p, q), "early_f", 0.5)
-    fl = send(call(pick_kernel, late, (late_p, late_n, p), "pick_late", 0.1), swap)
-    own, p, q = call(
-        late_kernel, (sums, sums, sums), (ue, ul, xe, xl, pe, ne, late_p, late_n, own, p, q), "late", 1.5
-    )
-    p, q = call(late_f_kernel, (sums, sums), (fe, fl, pe, ne, late_p, late_n, p, q), "late_f", 0.6)
+    own, p, q, p_labels, q_labels = call(
+        early_kernel,
+        (sums, early_sums, early_sums, column, column),
+        (ue, ul, xe, xl, pe, ne, x_labels, own),
+        "early",
+        2.5,
+    )
+    p, q, f_labels = call(
+        early_f_kernel, (early_sums, early_sums, column), (fe, pe, ne, p, q), "early_f", 0.5
+    )
+    own, p, q_late, q_part = call(
+        late_n_kernel,
+        (sums, early_sums, late_sums, part),
+        (ue, ul, xe, xl, pe, ne, late_n, x_labels, q_labels, own, p),
+        "late_n",
+        1,
+    )
+    fl = send(call(pick_kernel, late, (late_p, late_n, q_late), "pick_late", 0.1), swap)
+    p, q = call(
+        late_p_kernel,
+        (sums, sums),
+        (xe, xl, pe, ne, late_p, late_n, x_labels, p_labels, q_labels, p, q, q_late, q_part),
+        "late_p",
+        0.7,
+    )
+    p, q = call(end_kernel, (sums, sums), (fe, fl, pe, ne, late_p, late_n, f_labels, p, q), "end", 0.6)
     from_lower = send(q, up)
     from_upper = send(p, down)
     shape = struct((n // LANES, LANES), F32)

time: 64.5 us -> 62.1 us (0.963)
  starting transfers between devices: 28.2 us -> 25.8 us
  local copies, waits for them, and re-layouts: 0.69 us -> 0 us
    ppermute x10, starting transfers between devices: 28.2 us -> 25.8 us  [on_device(): send = lambda array, route: lax.ppermute(array, 'blk', route)]
    unnamed x6 -> x0, local copies, waits for them, and re-layouts: 0.69 us -> none
    pallas_call x10 -> x12, Pallas kernels: 15.5 us -> 15.7 us  [call(): pl.pallas_call(kernel, out_shape=out_shape, in_specs=in_specs or [vmem] *...]
  transfers between devices with their start and end apart: 10 -> 10, of which waited for: 3 -> 4; matrix products, arithmetic and copies ran while one was open for 0% -> 0% of each run, Pallas kernels for 18% -> 20%
where the time goes in v3:
time: 62.1 us; the launch traced here: 62 us
  starting transfers between devices  25.8 us (42%)
  waiting for transfers between devices  19.7 us (32%)
  Pallas kernels  15.7 us (25%)
  between operations  0.73 us (1%)
    ppermute x10, starting transfers between devices, on_device(): send = lambda array, route: lax.ppermute(array, 'blk', route)  25.8 us
    ppermute x10, waiting for transfers between devices, on_device(): send = lambda array, route: lax.ppermute(array, 'blk', route)  19.7 us
    pallas_call x12, Pallas kernels, call(): pl.pallas_call(kernel, out_shape=out_shape, in_specs=in_specs or [vmem] *...  15.7 us
  transfers between devices with their start and end apart: 10, of which 4 were waited for; matrix products, arithmetic and copies ran while one was open for 0% of the time, Pallas kernels for 20%

profile of v3, /device:TPU:1, one launch (start us, length us, event | category | flops | bytes accessed | tf_op | source)
XLA Modules:
  0.0 62.0 jit_solution(7262878284518367087)
XLA Ops:
  0.6 1.9 %unit_early.1.after_ref.ue_ref = bf16[4112,128]{1,0:T(8,128)(2,1)S(1)} custom-call(f32[768,1024]{1,0:T(8,128)} %x_ref.3, s32[6,128]{1,0:T(8,128)} %bitcast.3), custom_call_target="tpu_custom_call" | custom-call | flops 1200000000 | bytes 1024 | tf_op jit(solution)/shard_map/unit_early/pallas_call | solution.py:25
  2.6 2.2 %collective-permute-start.2 = (bf16[4112,128]{1,0:T(8,128)(2,1)S(1)}, bf16[4112,128]{1,0:T(8,128)(2,1)S(1)}, u32[]{:S(2)}, u32[]{:S(2)}) collective-permute-start(bf16[4112,128]{1,0:T(8,128)(2,1)S(1)} %unit_early.1.after_ref.ue_ref), channel_id=1, source_target_pairs={{0,2},{1,3},{2,4},{3,5},{4,6},{5,7},{6,8},{7,9},{8,10},{9,11},{10,... | collective-permute-start | bytes 3158024 | tf_op jit(solution)/shard_map/ppermute | solution.py:303
  4.8 9.0 %collective-permute-start.3 = (bf16[4112,128]{1,0:T(8,128)(2,1)S(1)}, bf16[4112,128]{1,0:T(8,128)(2,1)S(1)}, u32[]{:S(2)}, u32[]{:S(2)}) collective-permute-start(bf16[4112,128]{1,0:T(8,128)(2,1)S(1)} %unit_early.1.after_ref.ue_ref), channel_id=1, source_target_pairs={{0,254},{1,255},{2,0},{3,1},{4,2},{5,3},{6,4},{7,5},{8,6},{9,7},{1... | collective-permute-start | bytes 3158024 | tf_op jit(solution)/shard_map/ppermute | solution.py:303
  13.8 1.4 %unit_late.1.ul_ref = bf16[2048,128]{1,0:T(8,128)(2,1)S(1)} custom-call(f32[768,1024]{1,0:T(8,128)} %x_ref.3, bf16[4112,128]{1,0:T(8,128)(2,1)S(1)} %unit_early.1.after_ref.ue_ref), custom_call_target="tpu_custom_call" | custom-call | flops 1200000000 | bytes 1024 | tf_op jit(solution)/shard_map/unit_late/pallas_call | solution.py:25
  15.2 1.0 %collective-permute-start.1 = (bf16[2048,128]{1,0:T(8,128)(2,1)S(1)}, bf16[2048,128]{1,0:T(8,128)(2,1)S(1)}, u32[]{:S(2)}, u32[]{:S(2)}) collective-permute-start(bf16[2048,128]{1,0:T(8,128)(2,1)S(1)} %unit_late.1.ul_ref), channel_id=1, source_target_pairs={{0,1},{1,0},{2,3},{3,2},{4,5},{5,4},{6,7},{7,6},{8,9},{9,8},{10,11... | collective-permute-start | bytes 1572872 | tf_op jit(solution)/shard_map/ppermute | solution.py:303
  16.2 0.1 collective-permute-start
  16.4 1.7 %own.1 = (f32[2,768]{1,0:T(2,128)S(1)}, bf16[2048,128]{1,0:T(8,128)(2,1)S(1)}) custom-call(bf16[4112,128]{1,0:T(8,128)(2,1)S(1)} %unit_early.1.after_ref.ue_ref, bf16[2048,128]{1,0:T(8,128)(2,1)S(1)} %unit_late.1.ul_ref), custom_call_target="tpu_custom_call" | custom-call | flops 12000000000 | bytes 1024 | tf_op jit(solution)/shard_map/own/pallas_call | solution.py:25
  18.0 1.7 %collective-permute-start.4 = (bf16[2048,128]{1,0:T(8,128)(2,1)S(1)}, bf16[2048,128]{1,0:T(8,128)(2,1)S(1)}, u32[]{:S(2)}, u32[]{:S(2)}) collective-permute-start(bf16[2048,128]{1,0:T(8,128)(2,1)S(1)} %get-tuple-element.26), channel_id=1, source_target_pairs={{0,254},{1,255},{2,0},{3,1},{4,2},{5,3},{6,4},{7,5},{8,6},{9,7},{1... | collective-permute-start | bytes 1572872 | tf_op jit(solution)/shard_map/ppermute | solution.py:303
  19.7 0.0 collective-permute-done.1.xl_ref
  19.7 0.0 collective-permute-start.6
  19.7 0.0 collective-permute-done.xe_ref
  19.8 1.6 %with_partner.1 = (f32[2,768]{1,0:T(2,128)S(1)}, f32[768,128]{1,0:T(8,128)S(1)}) custom-call(bf16[4112,128]{1,0:T(8,128)(2,1)S(1)} %unit_early.1.after_ref.ue_ref, bf16[2048,128]{1,0:T(8,128)(2,1)S(1)} %unit_late.1.ul_ref, bf16[4112,128]{1,0:T(8,128)(2,1)S(1)} %collective-permute-done.xe_ref, bf16[2048,128]{1,0:T(8,128)(2,1)S(1)} %collective-permute-done.1.xl_ref, ...), custom_call_target="tpu_custom_call" | custom-call | flops 12000000000 | bytes 1024 | tf_op jit(solution)/shard_map/with_partner/pallas_call | solution.py:25
  21.4 15.3 %collective-permute-done.2.pe_ref.p_ref = bf16[4112,128]{1,0:T(8,128)(2,1)S(1)} collective-permute-done((bf16[4112,128]{1,0:T(8,128)(2,1)S(1)}, bf16[4112,128]{1,0:T(8,128)(2,1)S(1)}, u32[]{:S(2)}, u32[]{:S(2)}) %collective-permute-start.2) | collective-permute-done | bytes 1052704 | tf_op jit(solution)/shard_map/ppermute | solution.py:303
  36.7 0.0 collective-permute-done.3.ne_ref.n_ref
  36.7 0.1 pick.1
  36.7 2.3 %collective-permute-start.5 = (bf16[4112,128]{1,0:T(8,128)(2,1)S(1)}, bf16[4112,128]{1,0:T(8,128)(2,1)S(1)}, u32[]{:S(2)}, u32[]{:S(2)}) collective-permute-start(bf16[4112,128]{1,0:T(8,128)(2,1)S(1)} %pick.1), channel_id=1, source_target_pairs={{0,1},{1,0},{2,3},{3,2},{4,5},{5,4},{6,7},{7,6},{8,9},{9,8},{10,11... | collective-permute-start | bytes 3158024 | tf_op jit(solution)/shard_map/ppermute | solution.py:303
  39.1 3.7 %early.1 = (f32[2,768]{1,0:T(2,128)S(1)}, f32[2,512]{1,0:T(2,128)S(1)}, f32[2,512]{1,0:T(2,128)S(1)}, f32[768,128]{1,0:T(8,128)S(1)}, f32[768,128]{1,0:T(8,128)S(1)}) custom-call(bf16[4112,128]{1,0:T(8,128)(2,1)S(1)} %unit_early.1.after_ref.ue_ref, bf16[2048,128]{1,0:T(8,128)(2,1)S(1)} %unit_late.1.ul_ref, ...), custom_call_target="tpu_custom_call" | custom-call | flops 30000001024 | bytes 1024 | tf_op jit(solution)/shard_map/early/pallas_call | solution.py:25
  42.8 0.0 collective-permute-done.5.fe_ref
  42.8 0.9 %early_f.1 = (f32[2,512]{1,0:T(2,128)S(1)}, f32[2,512]{1,0:T(2,128)S(1)}, f32[768,128]{1,0:T(8,128)S(1)}) custom-call(bf16[4112,128]{1,0:T(8,128)(2,1)S(1)} %collective-permute-done.5.fe_ref, bf16[4112,128]{1,0:T(8,128)(2,1)S(1)} %collective-permute-done.2.pe_ref.p_ref, bf16[4112,128]{1,0:T(8,128)(2,1)S(1)} %collective-permute-done.3.ne_ref.n_ref, ...), custom_call_target="tpu_custom_call" | custom-call | flops 6000000000 | bytes 1024 | tf_op jit(solution)/shard_map/early_f/pallas_call | solution.py:25
  43.8 3.2 %collective-permute-done.4.nl_ref.n_ref = bf16[2048,128]{1,0:T(8,128)(2,1)S(1)} collective-permute-done((bf16[2048,128]{1,0:T(8,128)(2,1)S(1)}, bf16[2048,128]{1,0:T(8,128)(2,1)S(1)}, u32[]{:S(2)}, u32[]{:S(2)}) %collective-permute-start.4) | collective-permute-done | bytes 524320 | tf_op jit(solution)/shard_map/ppermute | solution.py:303
  46.9 1.4 %late_n.1 = (f32[2,768]{1,0:T(2,128)S(1)}, f32[2,512]{1,0:T(2,128)S(1)}, f32[2,256]{1,0:T(2,128)S(1)}, f32[2,256,128]{2,1,0:T(8,128)S(1)}) custom-call(bf16[4112,128]{1,0:T(8,128)(2,1)S(1)} %unit_early.1.after_ref.ue_ref, bf16[2048,128]{1,0:T(8,128)(2,1)S(1)} %unit_late.1.ul_ref, bf16[4112,128]{1,0:T(8,128)(2,1)S(1)} %collective-permute-done.xe_ref, ...), custom_call_target="tpu_custom_call" | custom-call | flops 12000000000 | bytes 1024 | tf_op jit(solution)/shard_map/late_n/pallas_call | solution.py:25
  48.4 0.0 collective-permute-done.6.p_ref.pl_ref
  48.4 0.1 pick_late.1
  48.4 1.6 %collective-permute-start.7 = (bf16[2048,128]{1,0:T(8,128)(2,1)S(1)}, bf16[2048,128]{1,0:T(8,128)(2,1)S(1)}, u32[]{:S(2)}, u32[]{:S(2)}) collective-permute-start(bf16[2048,128]{1,0:T(8,128)(2,1)S(1)} %pick_late.1), channel_id=1, source_target_pairs={{0,1},{1,0},{2,3},{3,2},{4,5},{5,4},{6,7},{7,6},{8,9},{9,8},{10,11... | collective-permute-start | bytes 1572872 | tf_op jit(solution)/shard_map/ppermute | solution.py:303
  50.1 1.3 %late_p.1 = (f32[2,768]{1,0:T(2,128)S(1)}, f32[2,768]{1,0:T(2,128)S(1)}) custom-call(bf16[4112,128]{1,0:T(8,128)(2,1)S(1)} %collective-permute-done.xe_ref, bf16[2048,128]{1,0:T(8,128)(2,1)S(1)} %collective-permute-done.1.xl_ref, bf16[4112,128]{1,0:T(8,128)(2,1)S(1)} %collective-permute-done.2.pe_ref.p_ref, ...), custom_call_target="tpu_custom_call" | custom-call | flops 8400000000 | bytes 1024 | tf_op jit(solution)/shard_map/late_p/pallas_call | solution.py:25
  51.3 0.3 collective-permute-done.7.fl_ref
  51.6 1.0 %end.1 = (f32[2,768]{1,0:T(2,128)S(1)}, f32[2,768]{1,0:T(2,128)S(1)}) custom-call(bf16[4112,128]{1,0:T(8,128)(2,1)S(1)} %collective-permute-done.5.fe_ref, bf16[2048,128]{1,0:T(8,128)(2,1)S(1)} %collective-permute-done.7.fl_ref, bf16[4112,128]{1,0:T(8,128)(2,1)S(1)} %collective-permute-done.2.pe_ref.p_ref, ...), custom_call_target="tpu_custom_call" | custom-call | flops 7200000000 | bytes 1024 | tf_op jit(solution)/shard_map/end/pallas_call | solution.py:25
  52.6 0.1 collective-permute-start.8
  52.7 7.7 %collective-permute-start.9 = (f32[2,768]{1,0:T(2,128)S(1)}, f32[2,768]{1,0:T(2,128)S(1)}, u32[]{:S(2)}, u32[]{:S(2)}) collective-permute-start(f32[2,768]{1,0:T(2,128)S(1)} %get-tuple-element.45), channel_id=1, source_target_pairs={{0,254},{1,255},{2,0},{3,1},{4,2},{5,3},{6,4},{7,5},{8,6},{9,7},{1... | collective-permute-start | bytes 18440 | tf_op jit(solution)/shard_map/ppermute | solution.py:303
  60.4 0.9 %collective-permute-done.8.a_ref = f32[2,768]{1,0:T(2,128)S(1)} collective-permute-done((f32[2,768]{1,0:T(2,128)S(1)}, f32[2,768]{1,0:T(2,128)S(1)}, u32[]{:S(2)}, u32[]{:S(2)}) %collective-permute-start.8) | collective-permute-done | bytes 6176 | tf_op jit(solution)/shard_map/ppermute | solution.py:303
  61.3 0.0 collective-permute-done.9.b_ref
  61.3 0.6 last.1
Async XLA Ops:
  2.6 34.1 %collective-permute-start.2 = (bf16[4112,128]{1,0:T(8,128)(2,1)S(1)}, bf16[4112,128]{1,0:T(8,128)(2,1)S(1)}, u32[]{:S(2)}, u32[]{:S(2)}) collective-permute-start(bf16[4112,128]{1,0:T(8,128)(2,1)S(1)} %unit_early.1.after_ref.ue_ref), channel_id=1, source_target_pairs={{0,2},{1,3},{2,4},{3,5},{4,6},{5,7},{6,8},{7,9},{8,10},{9,11},{10,... | collective-permute-start | bytes 3158024 | tf_op jit(solution)/shard_map/ppermute | solution.py:303
  4.8 31.9 %collective-permute-start.3 = (bf16[4112,128]{1,0:T(8,128)(2,1)S(1)}, bf16[4112,128]{1,0:T(8,128)(2,1)S(1)}, u32[]{:S(2)}, u32[]{:S(2)}) collective-permute-start(bf16[4112,128]{1,0:T(8,128)(2,1)S(1)} %unit_early.1.after_ref.ue_ref), channel_id=1, source_target_pairs={{0,254},{1,255},{2,0},{3,1},{4,2},{5,3},{6,4},{7,5},{8,6},{9,7},{1... | collective-permute-start | bytes 3158024 | tf_op jit(solution)/shard_map/ppermute | solution.py:303
  15.2 4.5 %collective-permute-start.1 = (bf16[2048,128]{1,0:T(8,128)(2,1)S(1)}, bf16[2048,128]{1,0:T(8,128)(2,1)S(1)}, u32[]{:S(2)}, u32[]{:S(2)}) collective-permute-start(bf16[2048,128]{1,0:T(8,128)(2,1)S(1)} %unit_late.1.ul_ref), channel_id=1, source_target_pairs={{0,1},{1,0},{2,3},{3,2},{4,5},{5,4},{6,7},{7,6},{8,9},{9,8},{10,11... | collective-permute-start | bytes 1572872 | tf_op jit(solution)/shard_map/ppermute | solution.py:303
  16.2 3.5 %collective-permute-start = (bf16[4112,128]{1,0:T(8,128)(2,1)S(1)}, bf16[4112,128]{1,0:T(8,128)(2,1)S(1)}, u32[]{:S(2)}, u32[]{:S(2)}) collective-permute-start(bf16[4112,128]{1,0:T(8,128)(2,1)S(1)} %unit_early.1.after_ref.ue_ref), channel_id=1, source_target_pairs={{0,1},{1,0},{2,3},{3,2},{4,5},{5,4},{6,7},{7,6},{8,9},{9,8},{10,11... | collective-permute-start | bytes 3158024 | tf_op jit(solution)/shard_map/ppermute | solution.py:303
  18.0 28.9 %collective-permute-start.4 = (bf16[2048,128]{1,0:T(8,128)(2,1)S(1)}, bf16[2048,128]{1,0:T(8,128)(2,1)S(1)}, u32[]{:S(2)}, u32[]{:S(2)}) collective-permute-start(bf16[2048,128]{1,0:T(8,128)(2,1)S(1)} %get-tuple-element.26), channel_id=1, source_target_pairs={{0,254},{1,255},{2,0},{3,1},{4,2},{5,3},{6,4},{7,5},{8,6},{9,7},{1... | collective-permute-start | bytes 1572872 | tf_op jit(solution)/shard_map/ppermute | solution.py:303
  19.7 28.6 %collective-permute-start.6 = (bf16[2048,128]{1,0:T(8,128)(2,1)S(1)}, bf16[2048,128]{1,0:T(8,128)(2,1)S(1)}, u32[]{:S(2)}, u32[]{:S(2)}) collective-permute-start(bf16[2048,128]{1,0:T(8,128)(2,1)S(1)} %get-tuple-element.26), channel_id=1, source_target_pairs={{0,2},{1,3},{2,4},{3,5},{4,6},{5,7},{6,8},{7,9},{8,10},{9,11},{10,... | collective-permute-start | bytes 1572872 | tf_op jit(solution)/shard_map/ppermute | solution.py:303
  36.7 6.1 %collective-permute-start.5 = (bf16[4112,128]{1,0:T(8,128)(2,1)S(1)}, bf16[4112,128]{1,0:T(8,128)(2,1)S(1)}, u32[]{:S(2)}, u32[]{:S(2)}) collective-permute-start(bf16[4112,128]{1,0:T(8,128)(2,1)S(1)} %pick.1), channel_id=1, source_target_pairs={{0,1},{1,0},{2,3},{3,2},{4,5},{5,4},{6,7},{7,6},{8,9},{9,8},{10,11... | collective-permute-start | bytes 3158024 | tf_op jit(solution)/shard_map/ppermute | solution.py:303
  48.4 3.2 %collective-permute-start.7 = (bf16[2048,128]{1,0:T(8,128)(2,1)S(1)}, bf16[2048,128]{1,0:T(8,128)(2,1)S(1)}, u32[]{:S(2)}, u32[]{:S(2)}) collective-permute-start(bf16[2048,128]{1,0:T(8,128)(2,1)S(1)} %pick_late.1), channel_id=1, source_target_pairs={{0,1},{1,0},{2,3},{3,2},{4,5},{5,4},{6,7},{7,6},{8,9},{9,8},{10,11... | collective-permute-start | bytes 1572872 | tf_op jit(solution)/shard_map/ppermute | solution.py:303
  52.6 8.7 %collective-permute-start.8 = (f32[2,768]{1,0:T(2,128)S(1)}, f32[2,768]{1,0:T(2,128)S(1)}, u32[]{:S(2)}, u32[]{:S(2)}) collective-permute-start(f32[2,768]{1,0:T(2,128)S(1)} %get-tuple-element.44), channel_id=1, source_target_pairs={{0,2},{1,3},{2,4},{3,5},{4,6},{5,7},{6,8},{7,9},{8,10},{9,11},{10,... | collective-permute-start | bytes 18440 | tf_op jit(solution)/shard_map/ppermute | solution.py:303
  52.7 8.6 %collective-permute-start.9 = (f32[2,768]{1,0:T(2,128)S(1)}, f32[2,768]{1,0:T(2,128)S(1)}, u32[]{:S(2)}, u32[]{:S(2)}) collective-permute-start(f32[2,768]{1,0:T(2,128)S(1)} %get-tuple-element.45), channel_id=1, source_target_pairs={{0,254},{1,255},{2,0},{3,1},{4,2},{5,3},{6,4},{7,5},{8,6},{9,7},{1... | collective-permute-start | bytes 18440 | tf_op jit(solution)/shard_map/ppermute | solution.py:303

commit v4 on v3

--- a/solution.py
+++ b/solution.py
@@ -15,6 +15,7 @@
 EARLY = 512
 LATE = 256
 CHUNK = 512
+LONG = 8
 STEP = 256
 F32 = jnp.float32
 BF16 = jnp.bfloat16
@@ -138,11 +139,10 @@
         copy.start()
     for i in range(parts):
         copies[i].wait()
-        for q in range(i * part, (i + 1) * part, 64):
-            x = held[q : q + 64, :]
-            unit = (x * lax.rsqrt(jnp.sum(x * x, axis=1, keepdims=True) + 1e-06)).astype(BF16)
-            for k in range(x.shape[1] // LANES):
-                write(k, q, unit[:, k * LANES : (k + 1) * LANES])
+        x = held[i * part : (i + 1) * part, :]
+        unit = (x * lax.rsqrt(jnp.sum(x * x, axis=1, keepdims=True) + 1e-06)).astype(BF16)
+        for k in range(x.shape[1] // LANES):
+            write(k, i * part, unit[:, k * LANES : (k + 1) * LANES])
 
 
 def unit_early_kernel(x_ref, labels_hbm, out_ref, held, labels_ref, sems, labels_sem):
@@ -150,7 +150,7 @@
     labels_copy.start()
 
     def write(slab, row, unit):
-        out_ref[HEAD + slab * EARLY + row : HEAD + slab * EARLY + row + 64, :] = unit
+        out_ref[HEAD + slab * EARLY + row : HEAD + slab * EARLY + row + unit.shape[0], :] = unit
 
     normalise(x_ref, 0, held, sems, write)
     labels_copy.wait()
@@ -163,20 +163,20 @@
 
 def unit_late_kernel(x_ref, after_ref, out_ref, held, sems):
     def write(slab, row, unit):
-        out_ref[slab * LATE + row : slab * LATE + row + 64, :] = unit
+        out_ref[slab * LATE + row : slab * LATE + row + unit.shape[0], :] = unit
 
     normalise(x_ref, EARLY, held, sems, write)
 
 
-def own_kernel(ue_ref, ul_ref, own_ref, copy_ref):
-    copy_ref[...] = ul_ref[...]
+def own_kernel(ue_ref, ul_ref, own_ref):
     unit = jnp.concatenate([early_part(ue_ref), late_part(ul_ref)], axis=0)
     labels = label_row(ue_ref, EARLY + LATE)
     _, own = weigh(unit, label_column(ue_ref, EARLY + LATE), unit, labels, False, True, own=0)
     own_ref[...] = own
 
 
-def partner_kernel(ue_ref, ul_ref, xe_ref, xl_ref, own_in_ref, own_ref, x_labels_ref):
+def partner_kernel(ue_ref, ul_ref, xe_ref, xl_ref, own_in_ref, own_ref, x_labels_ref, copy_ref):
+    copy_ref[...] = ul_ref[...]
     unit = jnp.concatenate([early_part(ue_ref), late_part(ul_ref)], axis=0)
     labels, x_labels = label_row(ue_ref, EARLY + LATE), label_column(xe_ref, EARLY + LATE)
     x_labels_ref[...] = x_labels
@@ -189,23 +189,43 @@
     return lax.rem(lax.axis_index("blk"), 2) == 0
 
 
-def pick_kernel(p_ref, n_ref, after_ref, out_ref):
+def is_lower():
+    return lax.rem(lax.axis_index("blk"), LONG) < 2
+
+
+def is_upper():
+    return lax.rem(lax.axis_index("blk"), LONG) >= LONG - 2
+
+
+def copy_when(condition, source_ref, out_ref):
+    @pl.when(condition)
+    def _():
+        out_ref[...] = source_ref[...]
+
+
+def pick_early_kernel(p_ref, n_ref, after_ref, out_ref):
     even = is_even()
-
-    @pl.when(even)
-    def _():
-        out_ref[...] = n_ref[...]
-
-    @pl.when(jnp.logical_not(even))
-    def _():
-        out_ref[...] = p_ref[...]
+    copy_when(even, n_ref, out_ref)
+    copy_when(jnp.logical_not(even), p_ref, out_ref)
+
+
+def pick_late_kernel(p_ref, n_ref, w_ref, after_ref, out_ref):
+    even = is_even()
+    odd = jnp.logical_not(even)
+    copy_when(even & is_upper(), w_ref, out_ref)
+    copy_when(even & jnp.logical_not(is_upper()), n_ref, out_ref)
+    copy_when(odd & is_lower(), w_ref, out_ref)
+    copy_when(odd & jnp.logical_not(is_lower()), p_ref, out_ref)
+
+
+def labels_kernel(p_ref, after_ref, labels_ref):
+    labels_ref[...] = label_column(p_ref, EARLY + LATE)
 
 
 def early_kernel(
     ue_ref, ul_ref, xe_ref, xl_ref, pe_ref, ne_ref, x_labels_ref, own_in_ref,
-    own_ref, p_ref, n_ref, p_labels_ref, n_labels_ref,
+    own_ref, p_ref, n_ref, n_labels_ref,
 ):
-    p_labels_ref[...] = label_column(pe_ref, EARLY + LATE)
     n_labels = label_column(ne_ref, EARLY + LATE)
     n_labels_ref[...] = n_labels
     n, labels = early_part(ne_ref), n_labels[:EARLY]
@@ -224,22 +244,18 @@
     p_ref[...] = p1 + p2 + p3
 
 
-def early_f_kernel(fe_ref, pe_ref, ne_ref, p_in_ref, n_in_ref, p_ref, n_ref, f_labels_ref):
+def early_f_kernel(fe_ref, re_ref, p_in_ref, n_in_ref, p_ref, n_ref, f_labels_ref):
     even = is_even()
-    right = jnp.where(even, early_part(ne_ref), early_part(pe_ref))
-    labels = jnp.where(even, row_of(ne_ref, False), row_of(pe_ref, False))
     f_labels = label_column(fe_ref, EARLY + LATE)
     f_labels_ref[...] = f_labels
-    _, more = weigh(early_part(fe_ref), f_labels[:EARLY], right, labels, False, True)
+    _, more = weigh(early_part(fe_ref), f_labels[:EARLY], early_part(re_ref), row_of(re_ref, False), False, True)
     p_ref[...] = p_in_ref[...] + jnp.where(even, 0.0, more)
     n_ref[...] = n_in_ref[...] + jnp.where(even, more, 0.0)
 
 
-def late_n_kernel(
-    ue_ref, ul_ref, xe_ref, xl_ref, pe_ref, ne_ref, nl_ref, x_labels_ref, n_labels_ref, own_in_ref, p_in_ref,
-    own_ref, p_ref, n_ref, part_ref,
-):
-    n, labels = late_part(nl_ref), n_labels_ref[EARLY:]
+def add_late_n(n_ref, ue_ref, ul_ref, xe_ref, xl_ref, pe_ref, ne_ref, x_labels_ref, n_labels_ref, out):
+    own_ref, p_ref, late_ref, part_ref = out
+    n, labels = late_part(n_ref), n_labels_ref[EARLY:]
     n1, own1 = weigh(n, labels, early_part(ue_ref), row_of(ue_ref, False), True, True)
     n2, own2 = weigh(n, labels, late_part(ul_ref), row_of(ue_ref, True), True, True)
     n3, p1 = weigh(n, labels, early_part(pe_ref), row_of(pe_ref, False), True, True)
@@ -248,35 +264,85 @@
     labels = row_of(ne_ref, True)
     _, n4 = weigh(early_part(xe_ref), x_labels_ref[:EARLY], n, labels, False, True)
     _, n5 = weigh(late_part(xl_ref), x_labels_ref[EARLY:], n, labels, False, True)
-    own_ref[:, :EARLY] = own_in_ref[:, :EARLY] + own1
-    own_ref[:, EARLY:] = own_in_ref[:, EARLY:] + own2
-    p_ref[...] = p_in_ref[...] + p1
-    n_ref[...] = n4 + n5
-
-
-def late_p_kernel(
-    xe_ref, xl_ref, pe_ref, ne_ref, pl_ref, nl_ref, x_labels_ref, p_labels_ref, n_labels_ref,
-    p_in_ref, n_in_ref, n_late_ref, n_part_ref, p_ref, n_ref,
-):
-    p, labels = late_part(pl_ref), row_of(pe_ref, True)
+    own_ref[:, :EARLY] = own_ref[:, :EARLY] + own1
+    own_ref[:, EARLY:] = own_ref[:, EARLY:] + own2
+    p_ref[...] = p_ref[...] + p1
+    late_ref[...] = n4 + n5
+
+
+def add_late_p(p_ref, xe_ref, xl_ref, pe_ref, ne_ref, x_labels_ref, p_labels_ref, out):
+    n_ref, late_ref = out
+    p, labels = late_part(p_ref), row_of(pe_ref, True)
     _, p1 = weigh(early_part(xe_ref), x_labels_ref[:EARLY], p, labels, False, True)
     _, p2 = weigh(late_part(xl_ref), x_labels_ref[EARLY:], p, labels, False, True)
     p3, n1 = weigh(p, p_labels_ref[EARLY:], early_part(ne_ref), row_of(ne_ref, False), True, True)
-    n2, p4 = weigh(late_part(nl_ref), n_labels_ref[EARLY:], p, labels, True, True)
-    p_ref[:, :EARLY] = p_in_ref[...]
-    p_ref[:, EARLY:] = p1 + p2 + p4 + add(p3)
-    n_ref[:, :EARLY] = n_in_ref[...] + n1
-    n_ref[:, EARLY:] = n_late_ref[...] + add((n_part_ref[0], n_part_ref[1]), n2)
-
-
-def end_kernel(fe_ref, fl_ref, pe_ref, ne_ref, pl_ref, nl_ref, f_labels_ref, p_in_ref, n_in_ref, p_ref, n_ref):
+    n_ref[...] = n_ref[...] + n1
+    late_ref[...] = p1 + p2 + add(p3)
+
+
+def near_kernel(
+    pl_ref, nl_ref, ue_ref, ul_ref, xe_ref, xl_ref, ne_ref, pe_ref, x_labels_ref, p_labels_ref, n_labels_ref,
+    own_in_ref, p_in_ref, n_in_ref, own_ref, p_ref, n_ref, p_late_ref, n_late_ref, part_ref,
+):
+    own_ref[...] = own_in_ref[...]
+    p_ref[...] = p_in_ref[...]
+    n_ref[...] = n_in_ref[...]
+
+    @pl.when(jnp.logical_not(is_upper()))
+    def _():
+        add_late_n(
+            nl_ref, ue_ref, ul_ref, xe_ref, xl_ref, pe_ref, ne_ref, x_labels_ref, n_labels_ref,
+            (own_ref, p_ref, n_late_ref, part_ref),
+        )
+
+    @pl.when(jnp.logical_not(is_lower()))
+    def _():
+        add_late_p(pl_ref, xe_ref, xl_ref, pe_ref, ne_ref, x_labels_ref, p_labels_ref, (n_ref, p_late_ref))
+
+
+def far_kernel(
+    w_ref, nl_ref, pl_ref, ue_ref, ul_ref, xe_ref, xl_ref, ne_ref, pe_ref, x_labels_ref, p_labels_ref,
+    n_labels_ref, own_in_ref, p_in_ref, n_in_ref, p_late_in_ref, n_late_in_ref, part_in_ref,
+    own_ref, p_ref, n_ref, p_early, n_early, p_late, n_late, part,
+):
+    lower, upper = is_lower(), is_upper()
+    own_ref[...] = own_in_ref[...]
+    p_early[...] = p_in_ref[...]
+    n_early[...] = n_in_ref[...]
+
+    @pl.when(upper)
+    def _():
+        add_late_n(
+            w_ref, ue_ref, ul_ref, xe_ref, xl_ref, pe_ref, ne_ref, x_labels_ref, n_labels_ref,
+            (own_ref, p_early, n_late, part),
+        )
+
+    @pl.when(jnp.logical_not(upper))
+    def _():
+        n_late[...] = n_late_in_ref[...]
+        part[...] = part_in_ref[...]
+
+    @pl.when(lower)
+    def _():
+        add_late_p(w_ref, xe_ref, xl_ref, pe_ref, ne_ref, x_labels_ref, p_labels_ref, (n_early, p_late))
+
+    copy_when(jnp.logical_not(lower), p_late_in_ref, p_late)
+    w = late_part(w_ref)
+    n = jnp.where(upper, w, late_part(nl_ref))
+    p = jnp.where(lower, w, late_part(pl_ref))
+    n1, p1 = weigh(n, n_labels_ref[EARLY:], p, row_of(pe_ref, True), True, True)
+    p_ref[:, :EARLY] = p_early[...]
+    p_ref[:, EARLY:] = p_late[...] + p1
+    n_ref[:, :EARLY] = n_early[...]
+    n_ref[:, EARLY:] = n_late[...] + add((part[0], part[1]), n1)
+
+
+def end_kernel(fe_ref, fl_ref, re_ref, rl_ref, f_labels_ref, p_in_ref, n_in_ref, p_ref, n_ref):
     even = is_even()
-    right = jnp.where(even, early_part(ne_ref), early_part(pe_ref))
-    late = jnp.where(even, late_part(nl_ref), late_part(pl_ref))
-    labels = jnp.where(even, row_of(ne_ref, False), row_of(pe_ref, False))
-    late_labels = jnp.where(even, row_of(ne_ref, True), row_of(pe_ref, True))
+    labels, late_labels = row_of(re_ref, False), row_of(re_ref, True)
+    late = late_part(rl_ref)
     f, f_labels = late_part(fl_ref), f_labels_ref[EARLY:]
-    _, a = weigh(f, f_labels, right, labels, False, True)
+    _, a = weigh(f, f_labels, early_part(re_ref), labels, False, True)
     _, b = weigh(f, f_labels, late, late_labels, False, True)
     _, c = weigh(early_part(fe_ref), f_labels_ref[:EARLY], late, late_labels, False, True)
     more = jnp.concatenate([a, b + c], axis=1)
@@ -317,7 +383,7 @@
         scratch=[
             pltpu.VMEM((EARLY, depth), F32),
             pltpu.VMEM((n // LANES, LANES), jnp.int32),
-            pltpu.SemaphoreType.DMA((8,)),
+            pltpu.SemaphoreType.DMA((4,)),
             pltpu.SemaphoreType.DMA,
         ],
         limit=52,
@@ -329,46 +395,53 @@
         "unit_late",
         0.1,
         in_specs=[hbm, pl.BlockSpec(memory_space=pltpu.VMEM)],
-        scratch=[pltpu.VMEM((LATE, depth), F32), pltpu.SemaphoreType.DMA((4,))],
+        scratch=[pltpu.VMEM((LATE, depth), F32), pltpu.SemaphoreType.DMA((2,))],
         limit=52,
     )
     pe = send(ue, up)
     ne = send(ue, down)
     xe = send(lax.optimization_barrier((ue, ul))[0], swap)
     xl = send(ul, swap)
-    own, copy = call(own_kernel, (sums, late), (ue, ul), "own", 1)
-    late_p = send(copy, up)
-    late_n = send(copy, down)
+    own = call(own_kernel, sums, (ue, ul), "own", 1)
     column, late_sums, part = struct((n, LANES), F32), struct((2, LATE), F32), struct((2, LATE, LANES), F32)
-    own, x_labels = call(partner_kernel, (sums, column), (ue, ul, xe, xl, own), "with_partner", 1)
-
-    fe = send(call(pick_kernel, early, (pe, ne, own), "pick", 0.1), swap)
-    own, p, q, p_labels, q_labels = call(
+    own, x_labels, copy = call(partner_kernel, (sums, column, late), (ue, ul, xe, xl, own), "with_partner", 1)
+    upper = [i for i in range(size) if i % LONG >= LONG - 2]
+    far = [(i, (i + 2) % size) for i in upper] + [((i + 2) % size, i) for i in upper]
+    late_p = send(copy, [pair for pair in up if pair not in far])
+    late_n = send(copy, [pair for pair in down if pair not in far])
+    late_w = send(copy, far)
+
+    p_labels = call(labels_kernel, column, (pe, own), "labels", 0.1)
+    re = call(pick_early_kernel, early, (pe, ne, p_labels), "pick", 0.1)
+    fe = send(re, swap)
+    own, p, q, q_labels = call(
         early_kernel,
-        (sums, early_sums, early_sums, column, column),
+        (sums, early_sums, early_sums, column),
         (ue, ul, xe, xl, pe, ne, x_labels, own),
         "early",
         2.5,
     )
-    p, q, f_labels = call(
-        early_f_kernel, (early_sums, early_sums, column), (fe, pe, ne, p, q), "early_f", 0.5
-    )
-    own, p, q_late, q_part = call(
-        late_n_kernel,
-        (sums, early_sums, late_sums, part),
-        (ue, ul, xe, xl, pe, ne, late_n, x_labels, q_labels, own, p),
-        "late_n",
-        1,
-    )
-    fl = send(call(pick_kernel, late, (late_p, late_n, q_late), "pick_late", 0.1), swap)
-    p, q = call(
-        late_p_kernel,
-        (sums, sums),
-        (xe, xl, pe, ne, late_p, late_n, x_labels, p_labels, q_labels, p, q, q_late, q_part),
-        "late_p",
-        0.7,
-    )
-    p, q = call(end_kernel, (sums, sums), (fe, fl, pe, ne, late_p, late_n, f_labels, p, q), "end", 0.6)
+    p, q, f_labels = call(early_f_kernel, (early_sums, early_sums, column), (fe, re, p, q), "early_f", 0.5)
+    fixed = (ue, ul, xe, xl, ne, pe, x_labels, p_labels, q_labels)
+    own, p, q, p_late, q_late, q_part = call(
+        near_kernel,
+        (sums, early_sums, early_sums, late_sums, late_sums, part),
+        (late_p, late_n, *fixed, own, p, q),
+        "near",
+        1.7,
+    )
+    rl = call(pick_late_kernel, late, (late_p, late_n, late_w, q), "pick_late", 0.1)
+    fl = send(rl, swap)
+    vmem = lambda shape: pltpu.VMEM(shape.shape, shape.dtype)
+    own, p, q = call(
+        far_kernel,
+        (sums, sums, sums),
+        (late_w, late_n, late_p, *fixed, own, p, q, p_late, q_late, q_part),
+        "far",
+        0.2,
+        scratch=[vmem(early_sums), vmem(early_sums), vmem(late_sums), vmem(late_sums), vmem(part)],
+    )
+    p, q = call(end_kernel, (sums, sums), (fe, fl, re, rl, f_labels, p, q), "end", 0.6)
     from_lower = send(q, up)
     from_upper = send(p, down)
     shape = struct((n // LANES, LANES), F32)

time: 62.1 us -> 60.7 us (0.977)
  waiting for transfers between devices: 19.7 us -> 11.7 us
  starting transfers between devices: 25.8 us -> 32.1 us
    ppermute x10 -> x11, waiting for transfers between devices: 19.7 us -> 11.7 us  [on_device(): send = lambda array, route: lax.ppermute(array, 'blk', route)]
    ppermute x10 -> x11, starting transfers between devices: 25.8 us -> 32.1 us  [on_device(): send = lambda array, route: lax.ppermute(array, 'blk', route)]
    pallas_call x12 -> x13, Pallas kernels: 15.7 us -> 15.9 us  [call(): pl.pallas_call(kernel, out_shape=out_shape, in_specs=in_specs or [vmem] *...]
  transfers between devices with their start and end apart: 10 -> 11, of which waited for: 4 -> 4; matrix products, arithmetic and copies ran while one was open for 0% -> 0% of each run, Pallas kernels for 20% -> 21%
where the time goes in v4:
time: 60.7 us; the launch traced here: 60.5 us
  starting transfers between devices  32.1 us (53%)
  Pallas kernels  15.9 us (26%)
  waiting for transfers between devices  11.7 us (19%)
  between operations  0.79 us (1%)
    ppermute x11, starting transfers between devices, on_device(): send = lambda array, route: lax.ppermute(array, 'blk', route)  32.1 us
    pallas_call x13, Pallas kernels, call(): pl.pallas_call(kernel, out_shape=out_shape, in_specs=in_specs or [vmem] *...  15.9 us
    ppermute x11, waiting for transfers between devices, on_device(): send = lambda array, route: lax.ppermute(array, 'blk', route)  11.7 us
  transfers between devices with their start and end apart: 11, of which 4 were waited for; matrix products, arithmetic and copies ran while one was open for 0% of the time, Pallas kernels for 21%

profile of v4, /device:TPU:1, one launch (start us, length us, event | category | flops | bytes accessed | tf_op | source)
XLA Modules:
  0.0 60.5 jit_solution(2872941511636095329)
XLA Ops:
  0.6 1.7 %unit_early.1.after_ref.ue_ref = bf16[4112,128]{1,0:T(8,128)(2,1)S(1)} custom-call(f32[768,1024]{1,0:T(8,128)} %x_ref.3, s32[6,128]{1,0:T(8,128)} %bitcast.3), custom_call_target="tpu_custom_call" | custom-call | flops 1200000000 | bytes 1024 | tf_op jit(solution)/shard_map/unit_early/pallas_call | solution.py:26
  2.4 2.2 %collective-permute-start.6 = (bf16[4112,128]{1,0:T(8,128)(2,1)S(1)}, bf16[4112,128]{1,0:T(8,128)(2,1)S(1)}, u32[]{:S(2)}, u32[]{:S(2)}) collective-permute-start(bf16[4112,128]{1,0:T(8,128)(2,1)S(1)} %unit_early.1.after_ref.ue_ref), channel_id=1, source_target_pairs={{0,2},{1,3},{2,4},{3,5},{4,6},{5,7},{6,8},{7,9},{8,10},{9,11},{10,... | collective-permute-start | bytes 3158024 | tf_op jit(solution)/shard_map/ppermute | solution.py:369
  4.6 9.0 %collective-permute-start.5 = (bf16[4112,128]{1,0:T(8,128)(2,1)S(1)}, bf16[4112,128]{1,0:T(8,128)(2,1)S(1)}, u32[]{:S(2)}, u32[]{:S(2)}) collective-permute-start(bf16[4112,128]{1,0:T(8,128)(2,1)S(1)} %unit_early.1.after_ref.ue_ref), channel_id=1, source_target_pairs={{0,254},{1,255},{2,0},{3,1},{4,2},{5,3},{6,4},{7,5},{8,6},{9,7},{1... | collective-permute-start | bytes 3158024 | tf_op jit(solution)/shard_map/ppermute | solution.py:369
  13.6 1.3 %unit_late.1.ul_ref = bf16[2048,128]{1,0:T(8,128)(2,1)S(1)} custom-call(f32[768,1024]{1,0:T(8,128)} %x_ref.3, bf16[4112,128]{1,0:T(8,128)(2,1)S(1)} %unit_early.1.after_ref.ue_ref), custom_call_target="tpu_custom_call" | custom-call | flops 1200000000 | bytes 1024 | tf_op jit(solution)/shard_map/unit_late/pallas_call | solution.py:26
  14.9 1.0 %collective-permute-start.1 = (bf16[2048,128]{1,0:T(8,128)(2,1)S(1)}, bf16[2048,128]{1,0:T(8,128)(2,1)S(1)}, u32[]{:S(2)}, u32[]{:S(2)}) collective-permute-start(bf16[2048,128]{1,0:T(8,128)(2,1)S(1)} %unit_late.1.ul_ref), channel_id=1, source_target_pairs={{0,1},{1,0},{2,3},{3,2},{4,5},{5,4},{6,7},{7,6},{8,9},{9,8},{10,11... | collective-permute-start | bytes 1572872 | tf_op jit(solution)/shard_map/ppermute | solution.py:369
  16.0 0.1 collective-permute-start
  16.1 1.6 %own.1.own_in_ref = f32[2,768]{1,0:T(2,128)S(1)} custom-call(bf16[4112,128]{1,0:T(8,128)(2,1)S(1)} %unit_early.1.after_ref.ue_ref, bf16[2048,128]{1,0:T(8,128)(2,1)S(1)} %unit_late.1.ul_ref), custom_call_target="tpu_custom_call" | custom-call | flops 12000000000 | bytes 1024 | tf_op jit(solution)/shard_map/own/pallas_call | solution.py:26
  17.7 0.0 collective-permute-done.1.xl_ref
  17.7 1.3 %collective-permute-done.xe_ref = bf16[4112,128]{1,0:T(8,128)(2,1)S(1)} collective-permute-done((bf16[4112,128]{1,0:T(8,128)(2,1)S(1)}, bf16[4112,128]{1,0:T(8,128)(2,1)S(1)}, u32[]{:S(2)}, u32[]{:S(2)}) %collective-permute-start) | collective-permute-done | bytes 1052704 | tf_op jit(solution)/shard_map/ppermute | solution.py:369
  19.0 1.6 %with_partner.1 = (f32[2,768]{1,0:T(2,128)S(1)}, f32[768,128]{1,0:T(8,128)S(1)}, bf16[2048,128]{1,0:T(8,128)(2,1)S(1)}) custom-call(bf16[4112,128]{1,0:T(8,128)(2,1)S(1)} %unit_early.1.after_ref.ue_ref, bf16[2048,128]{1,0:T(8,128)(2,1)S(1)} %unit_late.1.ul_ref, bf16[4112,128]{1,0:T(8,128)(2,1)S(1)} %collective-permute-done.xe_ref, ...), custom_call_target="tpu_custom_call" | custom-call | flops 12000000000 | bytes 1024 | tf_op jit(solution)/shard_map/with_partner/pallas_call | solution.py:26
  20.7 1.3 %collective-permute-start.4 = (bf16[2048,128]{1,0:T(8,128)(2,1)S(1)}, bf16[2048,128]{1,0:T(8,128)(2,1)S(1)}, u32[]{:S(2)}, u32[]{:S(2)}) collective-permute-start(bf16[2048,128]{1,0:T(8,128)(2,1)S(1)} %get-tuple-element.27), channel_id=1, source_target_pairs={{0,2},{1,3},{2,4},{3,5},{4,6},{5,7},{8,10},{9,11},{10,12},{11,13},... | collective-permute-start | bytes 1572872 | tf_op jit(solution)/shard_map/ppermute | solution.py:369
  22.0 1.3 %collective-permute-start.3 = (bf16[2048,128]{1,0:T(8,128)(2,1)S(1)}, bf16[2048,128]{1,0:T(8,128)(2,1)S(1)}, u32[]{:S(2)}, u32[]{:S(2)}) collective-permute-start(bf16[2048,128]{1,0:T(8,128)(2,1)S(1)} %get-tuple-element.27), channel_id=1, source_target_pairs={{2,0},{3,1},{4,2},{5,3},{6,4},{7,5},{10,8},{11,9},{12,10},{13,11},... | collective-permute-start | bytes 1572872 | tf_op jit(solution)/shard_map/ppermute | solution.py:369
  23.3 6.3 %collective-permute-start.2 = (bf16[2048,128]{1,0:T(8,128)(2,1)S(1)}, bf16[2048,128]{1,0:T(8,128)(2,1)S(1)}, u32[]{:S(2)}, u32[]{:S(2)}) collective-permute-start(bf16[2048,128]{1,0:T(8,128)(2,1)S(1)} %get-tuple-element.27), channel_id=1, source_target_pairs={{6,8},{7,9},{14,16},{15,17},{22,24},{23,25},{30,32},{31,33},{38,40... | collective-permute-start | bytes 1572872 | tf_op jit(solution)/shard_map/ppermute | solution.py:369
  29.6 6.9 %collective-permute-done.6.p_ref.pe_ref = bf16[4112,128]{1,0:T(8,128)(2,1)S(1)} collective-permute-done((bf16[4112,128]{1,0:T(8,128)(2,1)S(1)}, bf16[4112,128]{1,0:T(8,128)(2,1)S(1)}, u32[]{:S(2)}, u32[]{:S(2)}) %collective-permute-start.6) | collective-permute-done | bytes 1052704 | tf_op jit(solution)/shard_map/ppermute | solution.py:369
  36.5 0.2 labels.1.after_ref.p_labels_ref
  36.7 0.0 collective-permute-done.5.ne_ref.n_ref
  36.7 0.1 pick.1.re_ref
  36.8 2.1 %collective-permute-start.7 = (bf16[4112,128]{1,0:T(8,128)(2,1)S(1)}, bf16[4112,128]{1,0:T(8,128)(2,1)S(1)}, u32[]{:S(2)}, u32[]{:S(2)}) collective-permute-start(bf16[4112,128]{1,0:T(8,128)(2,1)S(1)} %pick.1.re_ref), channel_id=1, source_target_pairs={{0,1},{1,0},{2,3},{3,2},{4,5},{5,4},{6,7},{7,6},{8,9},{9,8},{10,11... | collective-permute-start | bytes 3158024 | tf_op jit(solution)/shard_map/ppermute | solution.py:369
  38.9 3.6 %early.1 = (f32[2,768]{1,0:T(2,128)S(1)}, f32[2,512]{1,0:T(2,128)S(1)}, f32[2,512]{1,0:T(2,128)S(1)}, f32[768,128]{1,0:T(8,128)S(1)}) custom-call(bf16[4112,128]{1,0:T(8,128)(2,1)S(1)} %unit_early.1.after_ref.ue_ref, bf16[2048,128]{1,0:T(8,128)(2,1)S(1)} %unit_late.1.ul_ref, bf16[4112,128]{1,0:T(8,128)(2,1)S(1)} %collective-permute-done.xe_ref, ...), custom_call_target="tpu_custom_call" | custom-call | flops 30000001024 | bytes 1024 | tf_op jit(solution)/shard_map/early/pallas_call | solution.py:26
  42.6 0.0 collective-permute-done.7.fe_ref
  42.6 0.9 %early_f.1 = (f32[2,512]{1,0:T(2,128)S(1)}, f32[2,512]{1,0:T(2,128)S(1)}, f32[768,128]{1,0:T(8,128)S(1)}) custom-call(bf16[4112,128]{1,0:T(8,128)(2,1)S(1)} %collective-permute-done.7.fe_ref, bf16[4112,128]{1,0:T(8,128)(2,1)S(1)} %pick.1.re_ref, f32[2,512]{1,0:T(2,128)S(1)} %get-tuple-element.32.p_in_ref, f32[2,512]{1,0:T(2,128)S(1)} %get-tuple-element.33.n_in_ref), custom_call_target="tpu_custom_call" | custom-call | flops 6000000000 | bytes 1024 | tf_op jit(solution)/shard_map/early_f/pallas_call | solution.py:26
  43.5 0.0 collective-permute-done.4.pl_ref.p_ref
  43.5 0.0 collective-permute-done.3.nl_ref.n_ref
  43.5 1.6 %near.1 = (f32[2,768]{1,0:T(2,128)S(1)}, f32[2,512]{1,0:T(2,128)S(1)}, f32[2,512]{1,0:T(2,128)S(1)}, f32[2,256]{1,0:T(2,128)S(1)}, f32[2,256]{1,0:T(2,128)S(1)}, /*index=5*/f32[2,256,128]{2,1,0:T(8,128)S(1)}) custom-call(bf16[2048,128]{1,0:T(8,128)(2,1)S(1)} %collective-permute-done.4.pl_ref.p_ref, ...), custom_call_target="tpu_custom_call" | custom-call | flops 20400001024 | bytes 1024 | tf_op jit(solution)/shard_map/near/pallas_call | solution.py:26
  45.1 2.5 %collective-permute-done.2.w_ref = bf16[2048,128]{1,0:T(8,128)(2,1)S(1)} collective-permute-done((bf16[2048,128]{1,0:T(8,128)(2,1)S(1)}, bf16[2048,128]{1,0:T(8,128)(2,1)S(1)}, u32[]{:S(2)}, u32[]{:S(2)}) %collective-permute-start.2) | collective-permute-done | bytes 524320 | tf_op jit(solution)/shard_map/ppermute | solution.py:369
  47.7 1.3 %collective-permute-start.8 = (bf16[2048,128]{1,0:T(8,128)(2,1)S(1)}, bf16[2048,128]{1,0:T(8,128)(2,1)S(1)}, u32[]{:S(2)}, u32[]{:S(2)}) collective-permute-start(bf16[2048,128]{1,0:T(8,128)(2,1)S(1)} %pick_late.1.rl_ref), channel_id=1, source_target_pairs={{0,1},{1,0},{2,3},{3,2},{4,5},{5,4},{6,7},{7,6},{8,9},{9,8},{10,11... | collective-permute-start | bytes 1572872 | tf_op jit(solution)/shard_map/ppermute | solution.py:369
  49.1 1.6 %far.1 = (f32[2,768]{1,0:T(2,128)S(1)}, f32[2,768]{1,0:T(2,128)S(1)}, f32[2,768]{1,0:T(2,128)S(1)}) custom-call(bf16[2048,128]{1,0:T(8,128)(2,1)S(1)} %collective-permute-done.2.w_ref, bf16[2048,128]{1,0:T(8,128)(2,1)S(1)} %collective-permute-done.3.nl_ref.n_ref, bf16[2048,128]{1,0:T(8,128)(2,1)S(1)} %collective-permute-done.4.pl_ref.p_ref, ...), custom_call_target="tpu_custom_call" | custom-call | flops 2400000000 | bytes 1024 | tf_op jit(solution)/shard_map/far/pallas_call | solution.py:26
  50.6 0.0 collective-permute-done.8.fl_ref
  50.6 0.9 %end.1 = (f32[2,768]{1,0:T(2,128)S(1)}, f32[2,768]{1,0:T(2,128)S(1)}) custom-call(bf16[4112,128]{1,0:T(8,128)(2,1)S(1)} %collective-permute-done.7.fe_ref, bf16[2048,128]{1,0:T(8,128)(2,1)S(1)} %collective-permute-done.8.fl_ref, bf16[4112,128]{1,0:T(8,128)(2,1)S(1)} %pick.1.re_ref, bf16[2048,128]{1,0:T(8,128)(2,1)S(1)} %pick_late.1.rl_ref, ...), custom_call_target="tpu_custom_call" | custom-call | flops 7200000000 | bytes 1024 | tf_op jit(solution)/shard_map/end/pallas_call | solution.py:26
  51.5 0.1 collective-permute-start.9
  51.6 7.3 %collective-permute-start.10 = (f32[2,768]{1,0:T(2,128)S(1)}, f32[2,768]{1,0:T(2,128)S(1)}, u32[]{:S(2)}, u32[]{:S(2)}) collective-permute-start(f32[2,768]{1,0:T(2,128)S(1)} %get-tuple-element.47), channel_id=1, source_target_pairs={{0,254},{1,255},{2,0},{3,1},{4,2},{5,3},{6,4},{7,5},{8,6},{9,7},{1... | collective-permute-start | bytes 18440 | tf_op jit(solution)/shard_map/ppermute | solution.py:369
  59.0 0.9 %collective-permute-done.9.a_ref = f32[2,768]{1,0:T(2,128)S(1)} collective-permute-done((f32[2,768]{1,0:T(2,128)S(1)}, f32[2,768]{1,0:T(2,128)S(1)}, u32[]{:S(2)}, u32[]{:S(2)}) %collective-permute-start.9) | collective-permute-done | bytes 6176 | tf_op jit(solution)/shard_map/ppermute | solution.py:369
  59.9 0.0 collective-permute-done.10.b_ref
  59.9 0.6 %last.1 = (f32[6,128]{1,0:T(8,128)}, f32[6,128]{1,0:T(8,128)}) custom-call(f32[2,768]{1,0:T(2,128)S(1)} %get-tuple-element.42.own_ref, f32[2,768]{1,0:T(2,128)S(1)} %collective-permute-done.9.a_ref, f32[2,768]{1,0:T(2,128)S(1)} %collective-permute-done.10.b_ref), custom_call_target="tpu_custom_call" | custom-call | flops 120000000 | bytes 1024 | tf_op jit(solution)/shard_map/last/pallas_call | solution.py:26
  (1 shorter events, 0.0 us)
Async XLA Ops:
  2.4 34.1 %collective-permute-start.6 = (bf16[4112,128]{1,0:T(8,128)(2,1)S(1)}, bf16[4112,128]{1,0:T(8,128)(2,1)S(1)}, u32[]{:S(2)}, u32[]{:S(2)}) collective-permute-start(bf16[4112,128]{1,0:T(8,128)(2,1)S(1)} %unit_early.1.after_ref.ue_ref), channel_id=1, source_target_pairs={{0,2},{1,3},{2,4},{3,5},{4,6},{5,7},{6,8},{7,9},{8,10},{9,11},{10,... | collective-permute-start | bytes 3158024 | tf_op jit(solution)/shard_map/ppermute | solution.py:369
  4.6 32.1 %collective-permute-start.5 = (bf16[4112,128]{1,0:T(8,128)(2,1)S(1)}, bf16[4112,128]{1,0:T(8,128)(2,1)S(1)}, u32[]{:S(2)}, u32[]{:S(2)}) collective-permute-start(bf16[4112,128]{1,0:T(8,128)(2,1)S(1)} %unit_early.1.after_ref.ue_ref), channel_id=1, source_target_pairs={{0,254},{1,255},{2,0},{3,1},{4,2},{5,3},{6,4},{7,5},{8,6},{9,7},{1... | collective-permute-start | bytes 3158024 | tf_op jit(solution)/shard_map/ppermute | solution.py:369
  14.9 2.8 %collective-permute-start.1 = (bf16[2048,128]{1,0:T(8,128)(2,1)S(1)}, bf16[2048,128]{1,0:T(8,128)(2,1)S(1)}, u32[]{:S(2)}, u32[]{:S(2)}) collective-permute-start(bf16[2048,128]{1,0:T(8,128)(2,1)S(1)} %unit_late.1.ul_ref), channel_id=1, source_target_pairs={{0,1},{1,0},{2,3},{3,2},{4,5},{5,4},{6,7},{7,6},{8,9},{9,8},{10,11... | collective-permute-start | bytes 1572872 | tf_op jit(solution)/shard_map/ppermute | solution.py:369
  16.0 3.0 %collective-permute-start = (bf16[4112,128]{1,0:T(8,128)(2,1)S(1)}, bf16[4112,128]{1,0:T(8,128)(2,1)S(1)}, u32[]{:S(2)}, u32[]{:S(2)}) collective-permute-start(bf16[4112,128]{1,0:T(8,128)(2,1)S(1)} %unit_early.1.after_ref.ue_ref), channel_id=1, source_target_pairs={{0,1},{1,0},{2,3},{3,2},{4,5},{5,4},{6,7},{7,6},{8,9},{9,8},{10,11... | collective-permute-start | bytes 3158024 | tf_op jit(solution)/shard_map/ppermute | solution.py:369
  20.7 22.9 %collective-permute-start.4 = (bf16[2048,128]{1,0:T(8,128)(2,1)S(1)}, bf16[2048,128]{1,0:T(8,128)(2,1)S(1)}, u32[]{:S(2)}, u32[]{:S(2)}) collective-permute-start(bf16[2048,128]{1,0:T(8,128)(2,1)S(1)} %get-tuple-element.27), channel_id=1, source_target_pairs={{0,2},{1,3},{2,4},{3,5},{4,6},{5,7},{8,10},{9,11},{10,12},{11,13},... | collective-permute-start | bytes 1572872 | tf_op jit(solution)/shard_map/ppermute | solution.py:369
  22.0 21.6 %collective-permute-start.3 = (bf16[2048,128]{1,0:T(8,128)(2,1)S(1)}, bf16[2048,128]{1,0:T(8,128)(2,1)S(1)}, u32[]{:S(2)}, u32[]{:S(2)}) collective-permute-start(bf16[2048,128]{1,0:T(8,128)(2,1)S(1)} %get-tuple-element.27), channel_id=1, source_target_pairs={{2,0},{3,1},{4,2},{5,3},{6,4},{7,5},{10,8},{11,9},{12,10},{13,11},... | collective-permute-start | bytes 1572872 | tf_op jit(solution)/shard_map/ppermute | solution.py:369
  23.3 24.4 %collective-permute-start.2 = (bf16[2048,128]{1,0:T(8,128)(2,1)S(1)}, bf16[2048,128]{1,0:T(8,128)(2,1)S(1)}, u32[]{:S(2)}, u32[]{:S(2)}) collective-permute-start(bf16[2048,128]{1,0:T(8,128)(2,1)S(1)} %get-tuple-element.27), channel_id=1, source_target_pairs={{6,8},{7,9},{14,16},{15,17},{22,24},{23,25},{30,32},{31,33},{38,40... | collective-permute-start | bytes 1572872 | tf_op jit(solution)/shard_map/ppermute | solution.py:369
  36.8 5.8 %collective-permute-start.7 = (bf16[4112,128]{1,0:T(8,128)(2,1)S(1)}, bf16[4112,128]{1,0:T(8,128)(2,1)S(1)}, u32[]{:S(2)}, u32[]{:S(2)}) collective-permute-start(bf16[4112,128]{1,0:T(8,128)(2,1)S(1)} %pick.1.re_ref), channel_id=1, source_target_pairs={{0,1},{1,0},{2,3},{3,2},{4,5},{5,4},{6,7},{7,6},{8,9},{9,8},{10,11... | collective-permute-start | bytes 3158024 | tf_op jit(solution)/shard_map/ppermute | solution.py:369
  47.7 2.9 %collective-permute-start.8 = (bf16[2048,128]{1,0:T(8,128)(2,1)S(1)}, bf16[2048,128]{1,0:T(8,128)(2,1)S(1)}, u32[]{:S(2)}, u32[]{:S(2)}) collective-permute-start(bf16[2048,128]{1,0:T(8,128)(2,1)S(1)} %pick_late.1.rl_ref), channel_id=1, source_target_pairs={{0,1},{1,0},{2,3},{3,2},{4,5},{5,4},{6,7},{7,6},{8,9},{9,8},{10,11... | collective-permute-start | bytes 1572872 | tf_op jit(solution)/shard_map/ppermute | solution.py:369
  51.5 8.4 %collective-permute-start.9 = (f32[2,768]{1,0:T(2,128)S(1)}, f32[2,768]{1,0:T(2,128)S(1)}, u32[]{:S(2)}, u32[]{:S(2)}) collective-permute-start(f32[2,768]{1,0:T(2,128)S(1)} %get-tuple-element.46), channel_id=1, source_target_pairs={{0,2},{1,3},{2,4},{3,5},{4,6},{5,7},{6,8},{7,9},{8,10},{9,11},{10,... | collective-permute-start | bytes 18440 | tf_op jit(solution)/shard_map/ppermute | solution.py:369
  51.6 8.3 %collective-permute-start.10 = (f32[2,768]{1,0:T(2,128)S(1)}, f32[2,768]{1,0:T(2,128)S(1)}, u32[]{:S(2)}, u32[]{:S(2)}) collective-permute-start(f32[2,768]{1,0:T(2,128)S(1)} %get-tuple-element.47), channel_id=1, source_target_pairs={{0,254},{1,255},{2,0},{3,1},{4,2},{5,3},{6,4},{7,5},{8,6},{9,7},{1... | collective-permute-start | bytes 18440 | tf_op jit(solution)/shard_map/ppermute | solution.py:369

commit v5 on v4

--- a/solution.py
+++ b/solution.py
@@ -253,99 +253,103 @@
     n_ref[...] = n_in_ref[...] + jnp.where(even, more, 0.0)
 
 
-def add_late_n(n_ref, ue_ref, ul_ref, xe_ref, xl_ref, pe_ref, ne_ref, x_labels_ref, n_labels_ref, out):
-    own_ref, p_ref, late_ref, part_ref = out
+def with_late_n(n_ref, ue_ref, ul_ref, xe_ref, xl_ref, pe_ref, ne_ref, n_labels_ref):
     n, labels = late_part(n_ref), n_labels_ref[EARLY:]
     n1, own1 = weigh(n, labels, early_part(ue_ref), row_of(ue_ref, False), True, True)
     n2, own2 = weigh(n, labels, late_part(ul_ref), row_of(ue_ref, True), True, True)
     n3, p1 = weigh(n, labels, early_part(pe_ref), row_of(pe_ref, False), True, True)
-    for k in range(2):
-        part_ref[k] = n1[k] + n2[k] + n3[k]
-    labels = row_of(ne_ref, True)
-    _, n4 = weigh(early_part(xe_ref), x_labels_ref[:EARLY], n, labels, False, True)
-    _, n5 = weigh(late_part(xl_ref), x_labels_ref[EARLY:], n, labels, False, True)
-    own_ref[:, :EARLY] = own_ref[:, :EARLY] + own1
-    own_ref[:, EARLY:] = own_ref[:, EARLY:] + own2
-    p_ref[...] = p_ref[...] + p1
-    late_ref[...] = n4 + n5
-
-
-def add_late_p(p_ref, xe_ref, xl_ref, pe_ref, ne_ref, x_labels_ref, p_labels_ref, out):
-    n_ref, late_ref = out
-    p, labels = late_part(p_ref), row_of(pe_ref, True)
-    _, p1 = weigh(early_part(xe_ref), x_labels_ref[:EARLY], p, labels, False, True)
-    _, p2 = weigh(late_part(xl_ref), x_labels_ref[EARLY:], p, labels, False, True)
-    p3, n1 = weigh(p, p_labels_ref[EARLY:], early_part(ne_ref), row_of(ne_ref, False), True, True)
-    n_ref[...] = n_ref[...] + n1
-    late_ref[...] = p1 + p2 + add(p3)
+    n4, _ = weigh(n, labels, early_part(xe_ref), row_of(xe_ref, False), True, False)
+    n5, _ = weigh(n, labels, late_part(xl_ref), row_of(xe_ref, True), True, False)
+    return (n1, n2, n3, n4, n5), own1, own2, p1
+
+
+def with_late_p(p_ref, xe_ref, xl_ref, pe_ref, ne_ref, p_labels_ref):
+    p, labels = late_part(p_ref), p_labels_ref[EARLY:]
+    p1, n1 = weigh(p, labels, early_part(ne_ref), row_of(ne_ref, False), True, True)
+    p2, _ = weigh(p, labels, early_part(xe_ref), row_of(xe_ref, False), True, False)
+    p3, _ = weigh(p, labels, late_part(xl_ref), row_of(xe_ref, True), True, False)
+    return (p1, p2, p3), n1
 
 
 def near_kernel(
-    pl_ref, nl_ref, ue_ref, ul_ref, xe_ref, xl_ref, ne_ref, pe_ref, x_labels_ref, p_labels_ref, n_labels_ref,
-    own_in_ref, p_in_ref, n_in_ref, own_ref, p_ref, n_ref, p_late_ref, n_late_ref, part_ref,
+    pl_ref, nl_ref, ue_ref, ul_ref, xe_ref, xl_ref, ne_ref, pe_ref, p_labels_ref, n_labels_ref,
+    own_in_ref, p_in_ref, n_in_ref, own_ref, p_ref, n_ref, p_late_ref, n_late_ref,
 ):
-    own_ref[...] = own_in_ref[...]
-    p_ref[...] = p_in_ref[...]
-    n_ref[...] = n_in_ref[...]
-
-    @pl.when(jnp.logical_not(is_upper()))
-    def _():
-        add_late_n(
-            nl_ref, ue_ref, ul_ref, xe_ref, xl_ref, pe_ref, ne_ref, x_labels_ref, n_labels_ref,
-            (own_ref, p_ref, n_late_ref, part_ref),
-        )
-
-    @pl.when(jnp.logical_not(is_lower()))
-    def _():
-        add_late_p(pl_ref, xe_ref, xl_ref, pe_ref, ne_ref, x_labels_ref, p_labels_ref, (n_ref, p_late_ref))
+    upper, lower = is_upper(), is_lower()
+    copy_when(upper, own_in_ref, own_ref)
+    copy_when(upper, p_in_ref, p_ref)
+    copy_when(lower, n_in_ref, n_ref)
+
+    @pl.when(jnp.logical_not(upper))
+    def _():
+        n, own1, own2, p1 = with_late_n(nl_ref, ue_ref, ul_ref, xe_ref, xl_ref, pe_ref, ne_ref, n_labels_ref)
+        own_ref[:, :EARLY] = own_in_ref[:, :EARLY] + own1
+        own_ref[:, EARLY:] = own_in_ref[:, EARLY:] + own2
+        p_ref[...] = p_in_ref[...] + p1
+        n_late_ref[...] = add(*n)
+
+    @pl.when(jnp.logical_not(lower))
+    def _():
+        p, n1 = with_late_p(pl_ref, xe_ref, xl_ref, pe_ref, ne_ref, p_labels_ref)
+        n_ref[...] = n_in_ref[...] + n1
+        p_late_ref[...] = add(*p)
 
 
 def far_kernel(
-    w_ref, nl_ref, pl_ref, ue_ref, ul_ref, xe_ref, xl_ref, ne_ref, pe_ref, x_labels_ref, p_labels_ref,
-    n_labels_ref, own_in_ref, p_in_ref, n_in_ref, p_late_in_ref, n_late_in_ref, part_in_ref,
-    own_ref, p_ref, n_ref, p_early, n_early, p_late, n_late, part,
+    w_ref, nl_ref, pl_ref, ue_ref, ul_ref, xe_ref, xl_ref, ne_ref, pe_ref, p_labels_ref, n_labels_ref,
+    own_in_ref, p_in_ref, n_in_ref, p_late_ref, n_late_ref, fe_ref, re_ref, rl_ref, f_labels_ref,
+    own_ref, p_ref, n_ref,
 ):
-    lower, upper = is_lower(), is_upper()
-    own_ref[...] = own_in_ref[...]
-    p_early[...] = p_in_ref[...]
-    n_early[...] = n_in_ref[...]
+    upper, lower = is_upper(), is_lower()
 
     @pl.when(upper)
     def _():
-        add_late_n(
-            w_ref, ue_ref, ul_ref, xe_ref, xl_ref, pe_ref, ne_ref, x_labels_ref, n_labels_ref,
-            (own_ref, p_early, n_late, part),
-        )
+        n, own1, own2, p1 = with_late_n(w_ref, ue_ref, ul_ref, xe_ref, xl_ref, pe_ref, ne_ref, n_labels_ref)
+        labels = n_labels_ref[EARLY:]
+        n6, p2 = weigh(late_part(w_ref), labels, late_part(pl_ref), row_of(pe_ref, True), True, True)
+        own_ref[:, :EARLY] = own_in_ref[:, :EARLY] + own1
+        own_ref[:, EARLY:] = own_in_ref[:, EARLY:] + own2
+        p_ref[:, :EARLY] = p_in_ref[...] + p1
+        p_ref[:, EARLY:] = p_late_ref[...] + p2
+        n_ref[:, :EARLY] = n_in_ref[...]
+        n_ref[:, EARLY:] = add(*n, n6)
 
     @pl.when(jnp.logical_not(upper))
     def _():
-        n_late[...] = n_late_in_ref[...]
-        part[...] = part_in_ref[...]
+        own_ref[...] = own_in_ref[...]
+        p_ref[:, :EARLY] = p_in_ref[...]
 
     @pl.when(lower)
     def _():
-        add_late_p(w_ref, xe_ref, xl_ref, pe_ref, ne_ref, x_labels_ref, p_labels_ref, (n_early, p_late))
-
-    copy_when(jnp.logical_not(lower), p_late_in_ref, p_late)
-    w = late_part(w_ref)
-    n = jnp.where(upper, w, late_part(nl_ref))
-    p = jnp.where(lower, w, late_part(pl_ref))
-    n1, p1 = weigh(n, n_labels_ref[EARLY:], p, row_of(pe_ref, True), True, True)
-    p_ref[:, :EARLY] = p_early[...]
-    p_ref[:, EARLY:] = p_late[...] + p1
-    n_ref[:, :EARLY] = n_early[...]
-    n_ref[:, EARLY:] = n_late[...] + add((part[0], part[1]), n1)
-
-
-def end_kernel(fe_ref, fl_ref, re_ref, rl_ref, f_labels_ref, p_in_ref, n_in_ref, p_ref, n_ref):
+        p, n1 = with_late_p(w_ref, xe_ref, xl_ref, pe_ref, ne_ref, p_labels_ref)
+        labels = p_labels_ref[EARLY:]
+        p4, n2 = weigh(late_part(w_ref), labels, late_part(nl_ref), row_of(ne_ref, True), True, True)
+        p_ref[:, EARLY:] = add(*p, p4)
+        n_ref[:, :EARLY] = n_in_ref[...] + n1
+        n_ref[:, EARLY:] = n_late_ref[...] + n2
+
+    @pl.when(jnp.logical_not(lower | upper))
+    def _():
+        labels = p_labels_ref[EARLY:]
+        p1, n1 = weigh(late_part(pl_ref), labels, late_part(nl_ref), row_of(ne_ref, True), True, True)
+        p_ref[:, EARLY:] = p_late_ref[...] + add(p1)
+        n_ref[:, :EARLY] = n_in_ref[...]
+        n_ref[:, EARLY:] = n_late_ref[...] + n1
+
+    _, more = weigh(
+        early_part(fe_ref), f_labels_ref[:EARLY], late_part(rl_ref), row_of(re_ref, True), False, True
+    )
     even = is_even()
-    labels, late_labels = row_of(re_ref, False), row_of(re_ref, True)
-    late = late_part(rl_ref)
-    f, f_labels = late_part(fl_ref), f_labels_ref[EARLY:]
-    _, a = weigh(f, f_labels, early_part(re_ref), labels, False, True)
-    _, b = weigh(f, f_labels, late, late_labels, False, True)
-    _, c = weigh(early_part(fe_ref), f_labels_ref[:EARLY], late, late_labels, False, True)
-    more = jnp.concatenate([a, b + c], axis=1)
+    p_ref[:, EARLY:] = p_ref[:, EARLY:] + jnp.where(even, 0.0, more)
+    n_ref[:, EARLY:] = n_ref[:, EARLY:] + jnp.where(even, more, 0.0)
+
+
+def end_kernel(fl_ref, re_ref, rl_ref, f_labels_ref, p_in_ref, n_in_ref, p_ref, n_ref):
+    even = is_even()
+    f, labels = late_part(fl_ref), f_labels_ref[EARLY:]
+    _, a = weigh(f, labels, early_part(re_ref), row_of(re_ref, False), False, True)
+    _, b = weigh(f, labels, late_part(rl_ref), row_of(re_ref, True), False, True)
+    more = jnp.concatenate([a, b], axis=1)
     p_ref[...] = p_in_ref[...] + jnp.where(even, 0.0, more)
     n_ref[...] = n_in_ref[...] + jnp.where(even, more, 0.0)
 
@@ -353,7 +357,7 @@
 def last_kernel(own_ref, a_ref, b_ref, agreement_ref, log_ref):
     sums = own_ref[...] + a_ref[...] + b_ref[...]
     agreement = sums[1:2] / sums[0:1]
-    log_weight = jnp.log(sums[0:1]) - 1.0 / TAU
+    log_weight = jnp.log(sums[0:1] * math.exp(-1.0 / TAU))
     for k in range(agreement_ref.shape[0]):
         agreement_ref[k : k + 1, :] = agreement[:, k * LANES : (k + 1) * LANES]
         log_ref[k : k + 1, :] = log_weight[:, k * LANES : (k + 1) * LANES]
@@ -383,7 +387,7 @@
         scratch=[
             pltpu.VMEM((EARLY, depth), F32),
             pltpu.VMEM((n // LANES, LANES), jnp.int32),
-            pltpu.SemaphoreType.DMA((4,)),
+            pltpu.SemaphoreType.DMA((2,)),
             pltpu.SemaphoreType.DMA,
         ],
         limit=52,
@@ -403,7 +407,7 @@
     xe = send(lax.optimization_barrier((ue, ul))[0], swap)
     xl = send(ul, swap)
     own = call(own_kernel, sums, (ue, ul), "own", 1)
-    column, late_sums, part = struct((n, LANES), F32), struct((2, LATE), F32), struct((2, LATE, LANES), F32)
+    column, late_sums = struct((n, LANES), F32), struct((2, LATE), F32)
     own, x_labels, copy = call(partner_kernel, (sums, column, late), (ue, ul, xe, xl, own), "with_partner", 1)
     upper = [i for i in range(size) if i % LONG >= LONG - 2]
     far = [(i, (i + 2) % size) for i in upper] + [((i + 2) % size, i) for i in upper]
@@ -422,26 +426,24 @@
         2.5,
     )
     p, q, f_labels = call(early_f_kernel, (early_sums, early_sums, column), (fe, re, p, q), "early_f", 0.5)
-    fixed = (ue, ul, xe, xl, ne, pe, x_labels, p_labels, q_labels)
-    own, p, q, p_late, q_late, q_part = call(
+    fixed = (ue, ul, xe, xl, ne, pe, p_labels, q_labels)
+    own, p, q, p_late, q_late = call(
         near_kernel,
-        (sums, early_sums, early_sums, late_sums, late_sums, part),
+        (sums, early_sums, early_sums, late_sums, late_sums),
         (late_p, late_n, *fixed, own, p, q),
         "near",
         1.7,
     )
     rl = call(pick_late_kernel, late, (late_p, late_n, late_w, q), "pick_late", 0.1)
     fl = send(rl, swap)
-    vmem = lambda shape: pltpu.VMEM(shape.shape, shape.dtype)
     own, p, q = call(
         far_kernel,
         (sums, sums, sums),
-        (late_w, late_n, late_p, *fixed, own, p, q, p_late, q_late, q_part),
+        (late_w, late_n, late_p, *fixed, own, p, q, p_late, q_late, fe, re, rl, f_labels),
         "far",
         0.2,
-        scratch=[vmem(early_sums), vmem(early_sums), vmem(late_sums), vmem(late_sums), vmem(part)],
-    )
-    p, q = call(end_kernel, (sums, sums), (fe, fl, re, rl, f_labels, p, q), "end", 0.6)
+    )
+    p, q = call(end_kernel, (sums, sums), (fl, re, rl, f_labels, p, q), "end", 0.6)
     from_lower = send(q, up)
     from_upper = send(p, down)
     shape = struct((n // LANES, LANES), F32)

time: 60.7 us -> 60.8 us (level)
  no operation moved by 1% of the time
where the time goes in v5:
time: 60.8 us; the launch traced here: 60.6 us
  starting transfers between devices  32.3 us (53%)
  Pallas kernels  16 us (26%)
  waiting for transfers between devices  11.5 us (19%)
  between operations  0.8 us (1%)
    ppermute x11, starting transfers between devices, on_device(): send = lambda array, route: lax.ppermute(array, 'blk', route)  32.3 us
    pallas_call x13, Pallas kernels, call(): pl.pallas_call(kernel, out_shape=out_shape, in_specs=in_specs or [vmem] *...  16 us
    ppermute x11, waiting for transfers between devices, on_device(): send = lambda array, route: lax.ppermute(array, 'blk', route)  11.5 us
  transfers between devices with their start and end apart: 11, of which 4 were waited for; matrix products, arithmetic and copies ran while one was open for 0% of the time, Pallas kernels for 21%

profile of v5, /device:TPU:1, one launch (start us, length us, event | category | flops | bytes accessed | tf_op | source)
XLA Modules:
  0.0 60.6 jit_solution(2624820798200841880)
XLA Ops:
  0.6 1.8 %unit_early.1.after_ref.ue_ref = bf16[4112,128]{1,0:T(8,128)(2,1)S(1)} custom-call(f32[768,1024]{1,0:T(8,128)} %x_ref.3, s32[6,128]{1,0:T(8,128)} %bitcast.3), custom_call_target="tpu_custom_call" | custom-call | flops 1200000000 | bytes 1024 | tf_op jit(solution)/shard_map/unit_early/pallas_call | solution.py:26
  2.4 2.2 %collective-permute-start.6 = (bf16[4112,128]{1,0:T(8,128)(2,1)S(1)}, bf16[4112,128]{1,0:T(8,128)(2,1)S(1)}, u32[]{:S(2)}, u32[]{:S(2)}) collective-permute-start(bf16[4112,128]{1,0:T(8,128)(2,1)S(1)} %unit_early.1.after_ref.ue_ref), channel_id=1, source_target_pairs={{0,2},{1,3},{2,4},{3,5},{4,6},{5,7},{6,8},{7,9},{8,10},{9,11},{10,... | collective-permute-start | bytes 3158024 | tf_op jit(solution)/shard_map/ppermute | solution.py:373
  4.6 9.0 %collective-permute-start.5 = (bf16[4112,128]{1,0:T(8,128)(2,1)S(1)}, bf16[4112,128]{1,0:T(8,128)(2,1)S(1)}, u32[]{:S(2)}, u32[]{:S(2)}) collective-permute-start(bf16[4112,128]{1,0:T(8,128)(2,1)S(1)} %unit_early.1.after_ref.ue_ref), channel_id=1, source_target_pairs={{0,254},{1,255},{2,0},{3,1},{4,2},{5,3},{6,4},{7,5},{8,6},{9,7},{1... | collective-permute-start | bytes 3158024 | tf_op jit(solution)/shard_map/ppermute | solution.py:373
  13.6 1.3 %unit_late.1.ul_ref = bf16[2048,128]{1,0:T(8,128)(2,1)S(1)} custom-call(f32[768,1024]{1,0:T(8,128)} %x_ref.3, bf16[4112,128]{1,0:T(8,128)(2,1)S(1)} %unit_early.1.after_ref.ue_ref), custom_call_target="tpu_custom_call" | custom-call | flops 1200000000 | bytes 1024 | tf_op jit(solution)/shard_map/unit_late/pallas_call | solution.py:26
  15.0 1.0 %collective-permute-start.1 = (bf16[2048,128]{1,0:T(8,128)(2,1)S(1)}, bf16[2048,128]{1,0:T(8,128)(2,1)S(1)}, u32[]{:S(2)}, u32[]{:S(2)}) collective-permute-start(bf16[2048,128]{1,0:T(8,128)(2,1)S(1)} %unit_late.1.ul_ref), channel_id=1, source_target_pairs={{0,1},{1,0},{2,3},{3,2},{4,5},{5,4},{6,7},{7,6},{8,9},{9,8},{10,11... | collective-permute-start | bytes 1572872 | tf_op jit(solution)/shard_map/ppermute | solution.py:373
  16.0 0.1 collective-permute-start
  16.1 1.6 %own.1.own_in_ref = f32[2,768]{1,0:T(2,128)S(1)} custom-call(bf16[4112,128]{1,0:T(8,128)(2,1)S(1)} %unit_early.1.after_ref.ue_ref, bf16[2048,128]{1,0:T(8,128)(2,1)S(1)} %unit_late.1.ul_ref), custom_call_target="tpu_custom_call" | custom-call | flops 12000000000 | bytes 1024 | tf_op jit(solution)/shard_map/own/pallas_call | solution.py:26
  17.8 0.0 collective-permute-done.1.xl_ref
  17.8 1.3 %collective-permute-done.xe_ref = bf16[4112,128]{1,0:T(8,128)(2,1)S(1)} collective-permute-done((bf16[4112,128]{1,0:T(8,128)(2,1)S(1)}, bf16[4112,128]{1,0:T(8,128)(2,1)S(1)}, u32[]{:S(2)}, u32[]{:S(2)}) %collective-permute-start) | collective-permute-done | bytes 1052704 | tf_op jit(solution)/shard_map/ppermute | solution.py:373
  19.1 1.7 %with_partner.1 = (f32[2,768]{1,0:T(2,128)S(1)}, f32[768,128]{1,0:T(8,128)S(1)}, bf16[2048,128]{1,0:T(8,128)(2,1)S(1)}) custom-call(bf16[4112,128]{1,0:T(8,128)(2,1)S(1)} %unit_early.1.after_ref.ue_ref, bf16[2048,128]{1,0:T(8,128)(2,1)S(1)} %unit_late.1.ul_ref, bf16[4112,128]{1,0:T(8,128)(2,1)S(1)} %collective-permute-done.xe_ref, ...), custom_call_target="tpu_custom_call" | custom-call | flops 12000000000 | bytes 1024 | tf_op jit(solution)/shard_map/with_partner/pallas_call | solution.py:26
  20.7 1.3 %collective-permute-start.4 = (bf16[2048,128]{1,0:T(8,128)(2,1)S(1)}, bf16[2048,128]{1,0:T(8,128)(2,1)S(1)}, u32[]{:S(2)}, u32[]{:S(2)}) collective-permute-start(bf16[2048,128]{1,0:T(8,128)(2,1)S(1)} %get-tuple-element.26), channel_id=1, source_target_pairs={{0,2},{1,3},{2,4},{3,5},{4,6},{5,7},{8,10},{9,11},{10,12},{11,13},... | collective-permute-start | bytes 1572872 | tf_op jit(solution)/shard_map/ppermute | solution.py:373
  22.1 1.3 %collective-permute-start.3 = (bf16[2048,128]{1,0:T(8,128)(2,1)S(1)}, bf16[2048,128]{1,0:T(8,128)(2,1)S(1)}, u32[]{:S(2)}, u32[]{:S(2)}) collective-permute-start(bf16[2048,128]{1,0:T(8,128)(2,1)S(1)} %get-tuple-element.26), channel_id=1, source_target_pairs={{2,0},{3,1},{4,2},{5,3},{6,4},{7,5},{10,8},{11,9},{12,10},{13,11},... | collective-permute-start | bytes 1572872 | tf_op jit(solution)/shard_map/ppermute | solution.py:373
  23.4 6.3 %collective-permute-start.2 = (bf16[2048,128]{1,0:T(8,128)(2,1)S(1)}, bf16[2048,128]{1,0:T(8,128)(2,1)S(1)}, u32[]{:S(2)}, u32[]{:S(2)}) collective-permute-start(bf16[2048,128]{1,0:T(8,128)(2,1)S(1)} %get-tuple-element.26), channel_id=1, source_target_pairs={{6,8},{7,9},{14,16},{15,17},{22,24},{23,25},{30,32},{31,33},{38,40... | collective-permute-start | bytes 1572872 | tf_op jit(solution)/shard_map/ppermute | solution.py:373
  29.6 6.9 %collective-permute-done.6.p_ref.pe_ref = bf16[4112,128]{1,0:T(8,128)(2,1)S(1)} collective-permute-done((bf16[4112,128]{1,0:T(8,128)(2,1)S(1)}, bf16[4112,128]{1,0:T(8,128)(2,1)S(1)}, u32[]{:S(2)}, u32[]{:S(2)}) %collective-permute-start.6) | collective-permute-done | bytes 1052704 | tf_op jit(solution)/shard_map/ppermute | solution.py:373
  36.5 0.2 labels.1.after_ref.p_labels_ref
  36.7 0.0 collective-permute-done.5.ne_ref.n_ref
  36.8 0.1 pick.1.re_ref
  36.8 2.1 %collective-permute-start.7 = (bf16[4112,128]{1,0:T(8,128)(2,1)S(1)}, bf16[4112,128]{1,0:T(8,128)(2,1)S(1)}, u32[]{:S(2)}, u32[]{:S(2)}) collective-permute-start(bf16[4112,128]{1,0:T(8,128)(2,1)S(1)} %pick.1.re_ref), channel_id=1, source_target_pairs={{0,1},{1,0},{2,3},{3,2},{4,5},{5,4},{6,7},{7,6},{8,9},{9,8},{10,11... | collective-permute-start | bytes 3158024 | tf_op jit(solution)/shard_map/ppermute | solution.py:373
  39.0 3.7 %early.1 = (f32[2,768]{1,0:T(2,128)S(1)}, f32[2,512]{1,0:T(2,128)S(1)}, f32[2,512]{1,0:T(2,128)S(1)}, f32[768,128]{1,0:T(8,128)S(1)}) custom-call(bf16[4112,128]{1,0:T(8,128)(2,1)S(1)} %unit_early.1.after_ref.ue_ref, bf16[2048,128]{1,0:T(8,128)(2,1)S(1)} %unit_late.1.ul_ref, bf16[4112,128]{1,0:T(8,128)(2,1)S(1)} %collective-permute-done.xe_ref, ...), custom_call_target="tpu_custom_call" | custom-call | flops 30000001024 | bytes 1024 | tf_op jit(solution)/shard_map/early/pallas_call | solution.py:26
  42.7 0.0 collective-permute-done.7.fe_ref
  42.7 0.9 %early_f.1 = (f32[2,512]{1,0:T(2,128)S(1)}, f32[2,512]{1,0:T(2,128)S(1)}, f32[768,128]{1,0:T(8,128)S(1)}) custom-call(bf16[4112,128]{1,0:T(8,128)(2,1)S(1)} %collective-permute-done.7.fe_ref, bf16[4112,128]{1,0:T(8,128)(2,1)S(1)} %pick.1.re_ref, f32[2,512]{1,0:T(2,128)S(1)} %get-tuple-element.31.p_in_ref, f32[2,512]{1,0:T(2,128)S(1)} %get-tuple-element.32.n_in_ref), custom_call_target="tpu_custom_call" | custom-call | flops 6000000000 | bytes 1024 | tf_op jit(solution)/shard_map/early_f/pallas_call | solution.py:26
  43.6 0.0 collective-permute-done.4.pl_ref.p_ref
  43.6 0.0 collective-permute-done.3.nl_ref.n_ref
  43.6 1.7 %near.1 = (f32[2,768]{1,0:T(2,128)S(1)}, f32[2,512]{1,0:T(2,128)S(1)}, f32[2,512]{1,0:T(2,128)S(1)}, f32[2,256]{1,0:T(2,128)S(1)}, f32[2,256]{1,0:T(2,128)S(1)}) custom-call(bf16[2048,128]{1,0:T(8,128)(2,1)S(1)} %collective-permute-done.4.pl_ref.p_ref, bf16[2048,128]{1,0:T(8,128)(2,1)S(1)} %collective-permute-done.3.nl_ref.n_ref, ...), custom_call_target="tpu_custom_call" | custom-call | flops 20400001024 | bytes 1024 | tf_op jit(solution)/shard_map/near/pallas_call | solution.py:26
  45.3 2.4 %collective-permute-done.2.w_ref = bf16[2048,128]{1,0:T(8,128)(2,1)S(1)} collective-permute-done((bf16[2048,128]{1,0:T(8,128)(2,1)S(1)}, bf16[2048,128]{1,0:T(8,128)(2,1)S(1)}, u32[]{:S(2)}, u32[]{:S(2)}) %collective-permute-start.2) | collective-permute-done | bytes 524320 | tf_op jit(solution)/shard_map/ppermute | solution.py:373
  47.8 1.3 %collective-permute-start.8 = (bf16[2048,128]{1,0:T(8,128)(2,1)S(1)}, bf16[2048,128]{1,0:T(8,128)(2,1)S(1)}, u32[]{:S(2)}, u32[]{:S(2)}) collective-permute-start(bf16[2048,128]{1,0:T(8,128)(2,1)S(1)} %pick_late.1.rl_ref), channel_id=1, source_target_pairs={{0,1},{1,0},{2,3},{3,2},{4,5},{5,4},{6,7},{7,6},{8,9},{9,8},{10,11... | collective-permute-start | bytes 1572872 | tf_op jit(solution)/shard_map/ppermute | solution.py:373
  49.1 1.7 %far.1 = (f32[2,768]{1,0:T(2,128)S(1)}, f32[2,768]{1,0:T(2,128)S(1)}, f32[2,768]{1,0:T(2,128)S(1)}) custom-call(bf16[2048,128]{1,0:T(8,128)(2,1)S(1)} %collective-permute-done.2.w_ref, bf16[2048,128]{1,0:T(8,128)(2,1)S(1)} %collective-permute-done.3.nl_ref.n_ref, bf16[2048,128]{1,0:T(8,128)(2,1)S(1)} %collective-permute-done.4.pl_ref.p_ref, ...), custom_call_target="tpu_custom_call" | custom-call | flops 2400000000 | bytes 1024 | tf_op jit(solution)/shard_map/far/pallas_call | solution.py:26
  50.8 0.0 collective-permute-done.8.fl_ref
  50.8 0.7 %end.1 = (f32[2,768]{1,0:T(2,128)S(1)}, f32[2,768]{1,0:T(2,128)S(1)}) custom-call(bf16[2048,128]{1,0:T(8,128)(2,1)S(1)} %collective-permute-done.8.fl_ref, bf16[4112,128]{1,0:T(8,128)(2,1)S(1)} %pick.1.re_ref, bf16[2048,128]{1,0:T(8,128)(2,1)S(1)} %pick_late.1.rl_ref, f32[768,128]{1,0:T(8,128)S(1)} %get-tuple-element.40.f_labels_ref, ...), custom_call_target="tpu_custom_call" | custom-call | flops 7200000000 | bytes 1024 | tf_op jit(solution)/shard_map/end/pallas_call | solution.py:26
  51.5 0.1 collective-permute-start.9
  51.6 7.5 %collective-permute-start.10 = (f32[2,768]{1,0:T(2,128)S(1)}, f32[2,768]{1,0:T(2,128)S(1)}, u32[]{:S(2)}, u32[]{:S(2)}) collective-permute-start(f32[2,768]{1,0:T(2,128)S(1)} %get-tuple-element.45), channel_id=1, source_target_pairs={{0,254},{1,255},{2,0},{3,1},{4,2},{5,3},{6,4},{7,5},{8,6},{9,7},{1... | collective-permute-start | bytes 18440 | tf_op jit(solution)/shard_map/ppermute | solution.py:373
  59.1 0.9 %collective-permute-done.9.a_ref = f32[2,768]{1,0:T(2,128)S(1)} collective-permute-done((f32[2,768]{1,0:T(2,128)S(1)}, f32[2,768]{1,0:T(2,128)S(1)}, u32[]{:S(2)}, u32[]{:S(2)}) %collective-permute-start.9) | collective-permute-done | bytes 6176 | tf_op jit(solution)/shard_map/ppermute | solution.py:373
  60.0 0.0 collective-permute-done.10.b_ref
  60.0 0.6 %last.1 = (f32[6,128]{1,0:T(8,128)}, f32[6,128]{1,0:T(8,128)}) custom-call(f32[2,768]{1,0:T(2,128)S(1)} %get-tuple-element.41.own_ref, f32[2,768]{1,0:T(2,128)S(1)} %collective-permute-done.9.a_ref, f32[2,768]{1,0:T(2,128)S(1)} %collective-permute-done.10.b_ref), custom_call_target="tpu_custom_call" | custom-call | flops 120000000 | bytes 1024 | tf_op jit(solution)/shard_map/last/pallas_call | solution.py:26
  (1 shorter events, 0.0 us)
Async XLA Ops:
  2.4 34.1 %collective-permute-start.6 = (bf16[4112,128]{1,0:T(8,128)(2,1)S(1)}, bf16[4112,128]{1,0:T(8,128)(2,1)S(1)}, u32[]{:S(2)}, u32[]{:S(2)}) collective-permute-start(bf16[4112,128]{1,0:T(8,128)(2,1)S(1)} %unit_early.1.after_ref.ue_ref), channel_id=1, source_target_pairs={{0,2},{1,3},{2,4},{3,5},{4,6},{5,7},{6,8},{7,9},{8,10},{9,11},{10,... | collective-permute-start | bytes 3158024 | tf_op jit(solution)/shard_map/ppermute | solution.py:373
  4.6 32.1 %collective-permute-start.5 = (bf16[4112,128]{1,0:T(8,128)(2,1)S(1)}, bf16[4112,128]{1,0:T(8,128)(2,1)S(1)}, u32[]{:S(2)}, u32[]{:S(2)}) collective-permute-start(bf16[4112,128]{1,0:T(8,128)(2,1)S(1)} %unit_early.1.after_ref.ue_ref), channel_id=1, source_target_pairs={{0,254},{1,255},{2,0},{3,1},{4,2},{5,3},{6,4},{7,5},{8,6},{9,7},{1... | collective-permute-start | bytes 3158024 | tf_op jit(solution)/shard_map/ppermute | solution.py:373
  15.0 2.8 %collective-permute-start.1 = (bf16[2048,128]{1,0:T(8,128)(2,1)S(1)}, bf16[2048,128]{1,0:T(8,128)(2,1)S(1)}, u32[]{:S(2)}, u32[]{:S(2)}) collective-permute-start(bf16[2048,128]{1,0:T(8,128)(2,1)S(1)} %unit_late.1.ul_ref), channel_id=1, source_target_pairs={{0,1},{1,0},{2,3},{3,2},{4,5},{5,4},{6,7},{7,6},{8,9},{9,8},{10,11... | collective-permute-start | bytes 1572872 | tf_op jit(solution)/shard_map/ppermute | solution.py:373
  16.0 3.0 %collective-permute-start = (bf16[4112,128]{1,0:T(8,128)(2,1)S(1)}, bf16[4112,128]{1,0:T(8,128)(2,1)S(1)}, u32[]{:S(2)}, u32[]{:S(2)}) collective-permute-start(bf16[4112,128]{1,0:T(8,128)(2,1)S(1)} %unit_early.1.after_ref.ue_ref), channel_id=1, source_target_pairs={{0,1},{1,0},{2,3},{3,2},{4,5},{5,4},{6,7},{7,6},{8,9},{9,8},{10,11... | collective-permute-start | bytes 3158024 | tf_op jit(solution)/shard_map/ppermute | solution.py:373
  20.7 22.9 %collective-permute-start.4 = (bf16[2048,128]{1,0:T(8,128)(2,1)S(1)}, bf16[2048,128]{1,0:T(8,128)(2,1)S(1)}, u32[]{:S(2)}, u32[]{:S(2)}) collective-permute-start(bf16[2048,128]{1,0:T(8,128)(2,1)S(1)} %get-tuple-element.26), channel_id=1, source_target_pairs={{0,2},{1,3},{2,4},{3,5},{4,6},{5,7},{8,10},{9,11},{10,12},{11,13},... | collective-permute-start | bytes 1572872 | tf_op jit(solution)/shard_map/ppermute | solution.py:373
  22.1 21.6 %collective-permute-start.3 = (bf16[2048,128]{1,0:T(8,128)(2,1)S(1)}, bf16[2048,128]{1,0:T(8,128)(2,1)S(1)}, u32[]{:S(2)}, u32[]{:S(2)}) collective-permute-start(bf16[2048,128]{1,0:T(8,128)(2,1)S(1)} %get-tuple-element.26), channel_id=1, source_target_pairs={{2,0},{3,1},{4,2},{5,3},{6,4},{7,5},{10,8},{11,9},{12,10},{13,11},... | collective-permute-start | bytes 1572872 | tf_op jit(solution)/shard_map/ppermute | solution.py:373
  23.4 24.4 %collective-permute-start.2 = (bf16[2048,128]{1,0:T(8,128)(2,1)S(1)}, bf16[2048,128]{1,0:T(8,128)(2,1)S(1)}, u32[]{:S(2)}, u32[]{:S(2)}) collective-permute-start(bf16[2048,128]{1,0:T(8,128)(2,1)S(1)} %get-tuple-element.26), channel_id=1, source_target_pairs={{6,8},{7,9},{14,16},{15,17},{22,24},{23,25},{30,32},{31,33},{38,40... | collective-permute-start | bytes 1572872 | tf_op jit(solution)/shard_map/ppermute | solution.py:373
  36.8 5.8 %collective-permute-start.7 = (bf16[4112,128]{1,0:T(8,128)(2,1)S(1)}, bf16[4112,128]{1,0:T(8,128)(2,1)S(1)}, u32[]{:S(2)}, u32[]{:S(2)}) collective-permute-start(bf16[4112,128]{1,0:T(8,128)(2,1)S(1)} %pick.1.re_ref), channel_id=1, source_target_pairs={{0,1},{1,0},{2,3},{3,2},{4,5},{5,4},{6,7},{7,6},{8,9},{9,8},{10,11... | collective-permute-start | bytes 3158024 | tf_op jit(solution)/shard_map/ppermute | solution.py:373
  47.8 3.0 %collective-permute-start.8 = (bf16[2048,128]{1,0:T(8,128)(2,1)S(1)}, bf16[2048,128]{1,0:T(8,128)(2,1)S(1)}, u32[]{:S(2)}, u32[]{:S(2)}) collective-permute-start(bf16[2048,128]{1,0:T(8,128)(2,1)S(1)} %pick_late.1.rl_ref), channel_id=1, source_target_pairs={{0,1},{1,0},{2,3},{3,2},{4,5},{5,4},{6,7},{7,6},{8,9},{9,8},{10,11... | collective-permute-start | bytes 1572872 | tf_op jit(solution)/shard_map/ppermute | solution.py:373
  51.5 8.5 %collective-permute-start.9 = (f32[2,768]{1,0:T(2,128)S(1)}, f32[2,768]{1,0:T(2,128)S(1)}, u32[]{:S(2)}, u32[]{:S(2)}) collective-permute-start(f32[2,768]{1,0:T(2,128)S(1)} %get-tuple-element.44), channel_id=1, source_target_pairs={{0,2},{1,3},{2,4},{3,5},{4,6},{5,7},{6,8},{7,9},{8,10},{9,11},{10,... | collective-permute-start | bytes 18440 | tf_op jit(solution)/shard_map/ppermute | solution.py:373
  51.6 8.5 %collective-permute-start.10 = (f32[2,768]{1,0:T(2,128)S(1)}, f32[2,768]{1,0:T(2,128)S(1)}, u32[]{:S(2)}, u32[]{:S(2)}) collective-permute-start(f32[2,768]{1,0:T(2,128)S(1)} %get-tuple-element.45), channel_id=1, source_target_pairs={{0,254},{1,255},{2,0},{3,1},{4,2},{5,3},{6,4},{7,5},{8,6},{9,7},{1... | collective-permute-start | bytes 18440 | tf_op jit(solution)/shard_map/ppermute | solution.py:373

commit v6 on v5

--- a/solution.py
+++ b/solution.py
@@ -336,26 +336,48 @@
         n_ref[:, :EARLY] = n_in_ref[...]
         n_ref[:, EARLY:] = n_late_ref[...] + n1
 
-    _, more = weigh(
-        early_part(fe_ref), f_labels_ref[:EARLY], late_part(rl_ref), row_of(re_ref, True), False, True
-    )
-    even = is_even()
-    p_ref[:, EARLY:] = p_ref[:, EARLY:] + jnp.where(even, 0.0, more)
-    n_ref[:, EARLY:] = n_ref[:, EARLY:] + jnp.where(even, more, 0.0)
-
-
-def end_kernel(fl_ref, re_ref, rl_ref, f_labels_ref, p_in_ref, n_in_ref, p_ref, n_ref):
-    even = is_even()
+    @pl.when(is_even())
+    def _():
+        n_ref[:, EARLY:] = n_ref[:, EARLY:] + early_f_late(fe_ref, re_ref, rl_ref, f_labels_ref)
+
+
+def early_f_late(fe_ref, re_ref, rl_ref, f_labels_ref):
+    late = late_part(rl_ref)
+    return weigh(early_part(fe_ref), f_labels_ref[:EARLY], late, row_of(re_ref, True), False, True)[1]
+
+
+def late_f(fl_ref, re_ref, rl_ref, f_labels_ref):
     f, labels = late_part(fl_ref), f_labels_ref[EARLY:]
     _, a = weigh(f, labels, early_part(re_ref), row_of(re_ref, False), False, True)
     _, b = weigh(f, labels, late_part(rl_ref), row_of(re_ref, True), False, True)
-    more = jnp.concatenate([a, b], axis=1)
-    p_ref[...] = p_in_ref[...] + jnp.where(even, 0.0, more)
-    n_ref[...] = n_in_ref[...] + jnp.where(even, more, 0.0)
-
-
-def last_kernel(own_ref, a_ref, b_ref, agreement_ref, log_ref):
-    sums = own_ref[...] + a_ref[...] + b_ref[...]
+    return a, b
+
+
+def end_n_kernel(fl_ref, re_ref, rl_ref, f_labels_ref, n_in_ref, n_ref):
+    copy_when(jnp.logical_not(is_even()), n_in_ref, n_ref)
+
+    @pl.when(is_even())
+    def _():
+        a, b = late_f(fl_ref, re_ref, rl_ref, f_labels_ref)
+        n_ref[...] = n_in_ref[...] + jnp.concatenate([a, b], axis=1)
+
+
+def end_p_kernel(fe_ref, fl_ref, re_ref, rl_ref, f_labels_ref, p_in_ref, after_ref, p_ref):
+    copy_when(is_even(), p_in_ref, p_ref)
+
+    @pl.when(jnp.logical_not(is_even()))
+    def _():
+        a, b = late_f(fl_ref, re_ref, rl_ref, f_labels_ref)
+        c = early_f_late(fe_ref, re_ref, rl_ref, f_labels_ref)
+        p_ref[...] = p_in_ref[...] + jnp.concatenate([a, b + c], axis=1)
+
+
+def sum_kernel(own_ref, more_ref, out_ref):
+    out_ref[...] = own_ref[...] + more_ref[...]
+
+
+def last_kernel(own_ref, more_ref, agreement_ref, log_ref):
+    sums = own_ref[...] + more_ref[...]
     agreement = sums[1:2] / sums[0:1]
     log_weight = jnp.log(sums[0:1] * math.exp(-1.0 / TAU))
     for k in range(agreement_ref.shape[0]):
@@ -443,11 +465,13 @@
         "far",
         0.2,
     )
-    p, q = call(end_kernel, (sums, sums), (fl, re, rl, f_labels, p, q), "end", 0.6)
+    q = call(end_n_kernel, sums, (fl, re, rl, f_labels, q), "end_n", 0.3)
     from_lower = send(q, up)
+    p = call(end_p_kernel, sums, (fe, fl, re, rl, f_labels, p, q), "end_p", 0.3)
     from_upper = send(p, down)
+    own = call(sum_kernel, sums, (own, from_lower), "sum", 0.001)
     shape = struct((n // LANES, LANES), F32)
-    agreement, log_weight = call(last_kernel, (shape, shape), (own, from_lower, from_upper), "last", 0.01)
+    agreement, log_weight = call(last_kernel, (shape, shape), (own, from_upper), "last", 0.01)
     return agreement.reshape(n), log_weight.reshape(n)
 
 

time: 60.8 us -> 60.5 us (level)
    pallas_call x13 -> x15, Pallas kernels: 16 us -> 15.8 us  [call(): pl.pallas_call(kernel, out_shape=out_shape, in_specs=in_specs or [vmem] *...]
  transfers between devices with their start and end apart: 11 -> 11, of which waited for: 4 -> 5; matrix products, arithmetic and copies ran while one was open for 0% -> 0% of each run, Pallas kernels for 21% -> 22%
where the time goes in v6:
time: 60.5 us; the launch traced here: 60.3 us
  starting transfers between devices  32 us (53%)
  Pallas kernels  15.8 us (26%)
  waiting for transfers between devices  11.7 us (19%)
  between operations  0.79 us (1%)
    ppermute x11, starting transfers between devices, on_device(): send = lambda array, route: lax.ppermute(array, 'blk', route)  32 us
    pallas_call x15, Pallas kernels, call(): pl.pallas_call(kernel, out_shape=out_shape, in_specs=in_specs or [vmem] *...  15.8 us
    ppermute x11, waiting for transfers between devices, on_device(): send = lambda array, route: lax.ppermute(array, 'blk', route)  11.7 us
  transfers between devices with their start and end apart: 11, of which 5 were waited for; matrix products, arithmetic and copies ran while one was open for 0% of the time, Pallas kernels for 22%

profile of v6, /device:TPU:1, one launch (start us, length us, event | category | flops | bytes accessed | tf_op | source)
XLA Modules:
  0.0 60.3 jit_solution(17772860114277356732)
XLA Ops:
  0.6 1.8 %unit_early.1.after_ref.ue_ref = bf16[4112,128]{1,0:T(8,128)(2,1)S(1)} custom-call(f32[768,1024]{1,0:T(8,128)} %x_ref.3, s32[6,128]{1,0:T(8,128)} %bitcast.3), custom_call_target="tpu_custom_call" | custom-call | flops 1200000000 | bytes 1024 | tf_op jit(solution)/shard_map/unit_early/pallas_call | solution.py:26
  2.4 2.2 %collective-permute-start.6 = (bf16[4112,128]{1,0:T(8,128)(2,1)S(1)}, bf16[4112,128]{1,0:T(8,128)(2,1)S(1)}, u32[]{:S(2)}, u32[]{:S(2)}) collective-permute-start(bf16[4112,128]{1,0:T(8,128)(2,1)S(1)} %unit_early.1.after_ref.ue_ref), channel_id=1, source_target_pairs={{0,2},{1,3},{2,4},{3,5},{4,6},{5,7},{6,8},{7,9},{8,10},{9,11},{10,... | collective-permute-start | bytes 3158024 | tf_op jit(solution)/shard_map/ppermute | solution.py:395
  4.6 9.0 %collective-permute-start.5 = (bf16[4112,128]{1,0:T(8,128)(2,1)S(1)}, bf16[4112,128]{1,0:T(8,128)(2,1)S(1)}, u32[]{:S(2)}, u32[]{:S(2)}) collective-permute-start(bf16[4112,128]{1,0:T(8,128)(2,1)S(1)} %unit_early.1.after_ref.ue_ref), channel_id=1, source_target_pairs={{0,254},{1,255},{2,0},{3,1},{4,2},{5,3},{6,4},{7,5},{8,6},{9,7},{1... | collective-permute-start | bytes 3158024 | tf_op jit(solution)/shard_map/ppermute | solution.py:395
  13.6 1.3 %unit_late.1.ul_ref = bf16[2048,128]{1,0:T(8,128)(2,1)S(1)} custom-call(f32[768,1024]{1,0:T(8,128)} %x_ref.3, bf16[4112,128]{1,0:T(8,128)(2,1)S(1)} %unit_early.1.after_ref.ue_ref), custom_call_target="tpu_custom_call" | custom-call | flops 1200000000 | bytes 1024 | tf_op jit(solution)/shard_map/unit_late/pallas_call | solution.py:26
  15.0 1.0 %collective-permute-start.1 = (bf16[2048,128]{1,0:T(8,128)(2,1)S(1)}, bf16[2048,128]{1,0:T(8,128)(2,1)S(1)}, u32[]{:S(2)}, u32[]{:S(2)}) collective-permute-start(bf16[2048,128]{1,0:T(8,128)(2,1)S(1)} %unit_late.1.ul_ref), channel_id=1, source_target_pairs={{0,1},{1,0},{2,3},{3,2},{4,5},{5,4},{6,7},{7,6},{8,9},{9,8},{10,11... | collective-permute-start | bytes 1572872 | tf_op jit(solution)/shard_map/ppermute | solution.py:395
  16.0 0.1 collective-permute-start
  16.1 1.6 %own.1.own_in_ref = f32[2,768]{1,0:T(2,128)S(1)} custom-call(bf16[4112,128]{1,0:T(8,128)(2,1)S(1)} %unit_early.1.after_ref.ue_ref, bf16[2048,128]{1,0:T(8,128)(2,1)S(1)} %unit_late.1.ul_ref), custom_call_target="tpu_custom_call" | custom-call | flops 12000000000 | bytes 1024 | tf_op jit(solution)/shard_map/own/pallas_call | solution.py:26
  17.8 0.0 collective-permute-done.1.xl_ref
  17.8 1.3 %collective-permute-done.xe_ref = bf16[4112,128]{1,0:T(8,128)(2,1)S(1)} collective-permute-done((bf16[4112,128]{1,0:T(8,128)(2,1)S(1)}, bf16[4112,128]{1,0:T(8,128)(2,1)S(1)}, u32[]{:S(2)}, u32[]{:S(2)}) %collective-permute-start) | collective-permute-done | bytes 1052704 | tf_op jit(solution)/shard_map/ppermute | solution.py:395
  19.1 1.7 %with_partner.1 = (f32[2,768]{1,0:T(2,128)S(1)}, f32[768,128]{1,0:T(8,128)S(1)}, bf16[2048,128]{1,0:T(8,128)(2,1)S(1)}) custom-call(bf16[4112,128]{1,0:T(8,128)(2,1)S(1)} %unit_early.1.after_ref.ue_ref, bf16[2048,128]{1,0:T(8,128)(2,1)S(1)} %unit_late.1.ul_ref, bf16[4112,128]{1,0:T(8,128)(2,1)S(1)} %collective-permute-done.xe_ref, ...), custom_call_target="tpu_custom_call" | custom-call | flops 12000000000 | bytes 1024 | tf_op jit(solution)/shard_map/with_partner/pallas_call | solution.py:26
  20.7 1.3 %collective-permute-start.4 = (bf16[2048,128]{1,0:T(8,128)(2,1)S(1)}, bf16[2048,128]{1,0:T(8,128)(2,1)S(1)}, u32[]{:S(2)}, u32[]{:S(2)}) collective-permute-start(bf16[2048,128]{1,0:T(8,128)(2,1)S(1)} %get-tuple-element.24), channel_id=1, source_target_pairs={{0,2},{1,3},{2,4},{3,5},{4,6},{5,7},{8,10},{9,11},{10,12},{11,13},... | collective-permute-start | bytes 1572872 | tf_op jit(solution)/shard_map/ppermute | solution.py:395
  22.1 1.3 %collective-permute-start.3 = (bf16[2048,128]{1,0:T(8,128)(2,1)S(1)}, bf16[2048,128]{1,0:T(8,128)(2,1)S(1)}, u32[]{:S(2)}, u32[]{:S(2)}) collective-permute-start(bf16[2048,128]{1,0:T(8,128)(2,1)S(1)} %get-tuple-element.24), channel_id=1, source_target_pairs={{2,0},{3,1},{4,2},{5,3},{6,4},{7,5},{10,8},{11,9},{12,10},{13,11},... | collective-permute-start | bytes 1572872 | tf_op jit(solution)/shard_map/ppermute | solution.py:395
  23.4 6.3 %collective-permute-start.2 = (bf16[2048,128]{1,0:T(8,128)(2,1)S(1)}, bf16[2048,128]{1,0:T(8,128)(2,1)S(1)}, u32[]{:S(2)}, u32[]{:S(2)}) collective-permute-start(bf16[2048,128]{1,0:T(8,128)(2,1)S(1)} %get-tuple-element.24), channel_id=1, source_target_pairs={{6,8},{7,9},{14,16},{15,17},{22,24},{23,25},{30,32},{31,33},{38,40... | collective-permute-start | bytes 1572872 | tf_op jit(solution)/shard_map/ppermute | solution.py:395
  29.6 6.9 %collective-permute-done.6.p_ref.pe_ref = bf16[4112,128]{1,0:T(8,128)(2,1)S(1)} collective-permute-done((bf16[4112,128]{1,0:T(8,128)(2,1)S(1)}, bf16[4112,128]{1,0:T(8,128)(2,1)S(1)}, u32[]{:S(2)}, u32[]{:S(2)}) %collective-permute-start.6) | collective-permute-done | bytes 1052704 | tf_op jit(solution)/shard_map/ppermute | solution.py:395
  36.5 0.2 labels.1.after_ref.p_labels_ref
  36.7 0.0 collective-permute-done.5.ne_ref.n_ref
  36.8 0.1 pick.1.re_ref
  36.8 2.1 %collective-permute-start.7 = (bf16[4112,128]{1,0:T(8,128)(2,1)S(1)}, bf16[4112,128]{1,0:T(8,128)(2,1)S(1)}, u32[]{:S(2)}, u32[]{:S(2)}) collective-permute-start(bf16[4112,128]{1,0:T(8,128)(2,1)S(1)} %pick.1.re_ref), channel_id=1, source_target_pairs={{0,1},{1,0},{2,3},{3,2},{4,5},{5,4},{6,7},{7,6},{8,9},{9,8},{10,11... | collective-permute-start | bytes 3158024 | tf_op jit(solution)/shard_map/ppermute | solution.py:395
  39.0 3.7 %early.1 = (f32[2,768]{1,0:T(2,128)S(1)}, f32[2,512]{1,0:T(2,128)S(1)}, f32[2,512]{1,0:T(2,128)S(1)}, f32[768,128]{1,0:T(8,128)S(1)}) custom-call(bf16[4112,128]{1,0:T(8,128)(2,1)S(1)} %unit_early.1.after_ref.ue_ref, bf16[2048,128]{1,0:T(8,128)(2,1)S(1)} %unit_late.1.ul_ref, bf16[4112,128]{1,0:T(8,128)(2,1)S(1)} %collective-permute-done.xe_ref, ...), custom_call_target="tpu_custom_call" | custom-call | flops 30000001024 | bytes 1024 | tf_op jit(solution)/shard_map/early/pallas_call | solution.py:26
  42.7 0.0 collective-permute-done.7.fe_ref
  42.7 0.9 %early_f.1 = (f32[2,512]{1,0:T(2,128)S(1)}, f32[2,512]{1,0:T(2,128)S(1)}, f32[768,128]{1,0:T(8,128)S(1)}) custom-call(bf16[4112,128]{1,0:T(8,128)(2,1)S(1)} %collective-permute-done.7.fe_ref, bf16[4112,128]{1,0:T(8,128)(2,1)S(1)} %pick.1.re_ref, f32[2,512]{1,0:T(2,128)S(1)} %get-tuple-element.29.p_in_ref, f32[2,512]{1,0:T(2,128)S(1)} %get-tuple-element.30.n_in_ref), custom_call_target="tpu_custom_call" | custom-call | flops 6000000000 | bytes 1024 | tf_op jit(solution)/shard_map/early_f/pallas_call | solution.py:26
  43.6 0.0 collective-permute-done.4.pl_ref.p_ref
  43.6 0.0 collective-permute-done.3.nl_ref.n_ref
  43.6 1.7 %near.1 = (f32[2,768]{1,0:T(2,128)S(1)}, f32[2,512]{1,0:T(2,128)S(1)}, f32[2,512]{1,0:T(2,128)S(1)}, f32[2,256]{1,0:T(2,128)S(1)}, f32[2,256]{1,0:T(2,128)S(1)}) custom-call(bf16[2048,128]{1,0:T(8,128)(2,1)S(1)} %collective-permute-done.4.pl_ref.p_ref, bf16[2048,128]{1,0:T(8,128)(2,1)S(1)} %collective-permute-done.3.nl_ref.n_ref, ...), custom_call_target="tpu_custom_call" | custom-call | flops 20400001024 | bytes 1024 | tf_op jit(solution)/shard_map/near/pallas_call | solution.py:26
  45.3 2.4 %collective-permute-done.2.w_ref = bf16[2048,128]{1,0:T(8,128)(2,1)S(1)} collective-permute-done((bf16[2048,128]{1,0:T(8,128)(2,1)S(1)}, bf16[2048,128]{1,0:T(8,128)(2,1)S(1)}, u32[]{:S(2)}, u32[]{:S(2)}) %collective-permute-start.2) | collective-permute-done | bytes 524320 | tf_op jit(solution)/shard_map/ppermute | solution.py:395
  47.8 1.3 %collective-permute-start.8 = (bf16[2048,128]{1,0:T(8,128)(2,1)S(1)}, bf16[2048,128]{1,0:T(8,128)(2,1)S(1)}, u32[]{:S(2)}, u32[]{:S(2)}) collective-permute-start(bf16[2048,128]{1,0:T(8,128)(2,1)S(1)} %pick_late.1.rl_ref), channel_id=1, source_target_pairs={{0,1},{1,0},{2,3},{3,2},{4,5},{5,4},{6,7},{7,6},{8,9},{9,8},{10,11... | collective-permute-start | bytes 1572872 | tf_op jit(solution)/shard_map/ppermute | solution.py:395
  49.1 1.2 %far.1 = (f32[2,768]{1,0:T(2,128)S(1)}, f32[2,768]{1,0:T(2,128)S(1)}, f32[2,768]{1,0:T(2,128)S(1)}) custom-call(bf16[2048,128]{1,0:T(8,128)(2,1)S(1)} %collective-permute-done.2.w_ref, bf16[2048,128]{1,0:T(8,128)(2,1)S(1)} %collective-permute-done.3.nl_ref.n_ref, bf16[2048,128]{1,0:T(8,128)(2,1)S(1)} %collective-permute-done.4.pl_ref.p_ref, ...), custom_call_target="tpu_custom_call" | custom-call | flops 2400000000 | bytes 1024 | tf_op jit(solution)/shard_map/far/pallas_call | solution.py:26
  50.3 0.3 collective-permute-done.8.fl_ref
  50.6 0.0 collective-permute-start.9
  50.6 0.9 %end_p.1 = f32[2,768]{1,0:T(2,128)S(1)} custom-call(bf16[4112,128]{1,0:T(8,128)(2,1)S(1)} %collective-permute-done.7.fe_ref, bf16[2048,128]{1,0:T(8,128)(2,1)S(1)} %collective-permute-done.8.fl_ref, bf16[4112,128]{1,0:T(8,128)(2,1)S(1)} %pick.1.re_ref, bf16[2048,128]{1,0:T(8,128)(2,1)S(1)} %pick_late.1.rl_ref, ...), custom_call_target="tpu_custom_call" | custom-call | flops 3600000000 | bytes 1024 | tf_op jit(solution)/shard_map/end_p/pallas_call | solution.py:26
  51.6 7.3 %collective-permute-start.10 = (f32[2,768]{1,0:T(2,128)S(1)}, f32[2,768]{1,0:T(2,128)S(1)}, u32[]{:S(2)}, u32[]{:S(2)}) collective-permute-start(f32[2,768]{1,0:T(2,128)S(1)} %end_p.1), channel_id=1, source_target_pairs={{0,254},{1,255},{2,0},{3,1},{4,2},{5,3},{6,4},{7,5},{8,6},{9,7},{1... | collective-permute-start | bytes 18440 | tf_op jit(solution)/shard_map/ppermute | solution.py:395
  58.9 0.0 collective-permute-done.9.more_ref
  58.9 0.8 %collective-permute-done.10.more_ref = f32[2,768]{1,0:T(2,128)S(1)} collective-permute-done((f32[2,768]{1,0:T(2,128)S(1)}, f32[2,768]{1,0:T(2,128)S(1)}, u32[]{:S(2)}, u32[]{:S(2)}) %collective-permute-start.10) | collective-permute-done | bytes 6176 | tf_op jit(solution)/shard_map/ppermute | solution.py:395
  59.7 0.6 %last.1 = (f32[6,128]{1,0:T(8,128)}, f32[6,128]{1,0:T(8,128)}) custom-call(f32[2,768]{1,0:T(2,128)S(1)} %sum.1.own_ref, f32[2,768]{1,0:T(2,128)S(1)} %collective-permute-done.10.more_ref), custom_call_target="tpu_custom_call" | custom-call | flops 120000000 | bytes 1024 | tf_op jit(solution)/shard_map/last/pallas_call | solution.py:26
  (3 shorter events, 0.0 us)
Async XLA Ops:
  2.4 34.1 %collective-permute-start.6 = (bf16[4112,128]{1,0:T(8,128)(2,1)S(1)}, bf16[4112,128]{1,0:T(8,128)(2,1)S(1)}, u32[]{:S(2)}, u32[]{:S(2)}) collective-permute-start(bf16[4112,128]{1,0:T(8,128)(2,1)S(1)} %unit_early.1.after_ref.ue_ref), channel_id=1, source_target_pairs={{0,2},{1,3},{2,4},{3,5},{4,6},{5,7},{6,8},{7,9},{8,10},{9,11},{10,... | collective-permute-start | bytes 3158024 | tf_op jit(solution)/shard_map/ppermute | solution.py:395
  4.6 32.1 %collective-permute-start.5 = (bf16[4112,128]{1,0:T(8,128)(2,1)S(1)}, bf16[4112,128]{1,0:T(8,128)(2,1)S(1)}, u32[]{:S(2)}, u32[]{:S(2)}) collective-permute-start(bf16[4112,128]{1,0:T(8,128)(2,1)S(1)} %unit_early.1.after_ref.ue_ref), channel_id=1, source_target_pairs={{0,254},{1,255},{2,0},{3,1},{4,2},{5,3},{6,4},{7,5},{8,6},{9,7},{1... | collective-permute-start | bytes 3158024 | tf_op jit(solution)/shard_map/ppermute | solution.py:395
  15.0 2.8 %collective-permute-start.1 = (bf16[2048,128]{1,0:T(8,128)(2,1)S(1)}, bf16[2048,128]{1,0:T(8,128)(2,1)S(1)}, u32[]{:S(2)}, u32[]{:S(2)}) collective-permute-start(bf16[2048,128]{1,0:T(8,128)(2,1)S(1)} %unit_late.1.ul_ref), channel_id=1, source_target_pairs={{0,1},{1,0},{2,3},{3,2},{4,5},{5,4},{6,7},{7,6},{8,9},{9,8},{10,11... | collective-permute-start | bytes 1572872 | tf_op jit(solution)/shard_map/ppermute | solution.py:395
  16.0 3.0 %collective-permute-start = (bf16[4112,128]{1,0:T(8,128)(2,1)S(1)}, bf16[4112,128]{1,0:T(8,128)(2,1)S(1)}, u32[]{:S(2)}, u32[]{:S(2)}) collective-permute-start(bf16[4112,128]{1,0:T(8,128)(2,1)S(1)} %unit_early.1.after_ref.ue_ref), channel_id=1, source_target_pairs={{0,1},{1,0},{2,3},{3,2},{4,5},{5,4},{6,7},{7,6},{8,9},{9,8},{10,11... | collective-permute-start | bytes 3158024 | tf_op jit(solution)/shard_map/ppermute | solution.py:395
  20.7 22.9 %collective-permute-start.4 = (bf16[2048,128]{1,0:T(8,128)(2,1)S(1)}, bf16[2048,128]{1,0:T(8,128)(2,1)S(1)}, u32[]{:S(2)}, u32[]{:S(2)}) collective-permute-start(bf16[2048,128]{1,0:T(8,128)(2,1)S(1)} %get-tuple-element.24), channel_id=1, source_target_pairs={{0,2},{1,3},{2,4},{3,5},{4,6},{5,7},{8,10},{9,11},{10,12},{11,13},... | collective-permute-start | bytes 1572872 | tf_op jit(solution)/shard_map/ppermute | solution.py:395
  22.1 21.6 %collective-permute-start.3 = (bf16[2048,128]{1,0:T(8,128)(2,1)S(1)}, bf16[2048,128]{1,0:T(8,128)(2,1)S(1)}, u32[]{:S(2)}, u32[]{:S(2)}) collective-permute-start(bf16[2048,128]{1,0:T(8,128)(2,1)S(1)} %get-tuple-element.24), channel_id=1, source_target_pairs={{2,0},{3,1},{4,2},{5,3},{6,4},{7,5},{10,8},{11,9},{12,10},{13,11},... | collective-permute-start | bytes 1572872 | tf_op jit(solution)/shard_map/ppermute | solution.py:395
  23.4 24.4 %collective-permute-start.2 = (bf16[2048,128]{1,0:T(8,128)(2,1)S(1)}, bf16[2048,128]{1,0:T(8,128)(2,1)S(1)}, u32[]{:S(2)}, u32[]{:S(2)}) collective-permute-start(bf16[2048,128]{1,0:T(8,128)(2,1)S(1)} %get-tuple-element.24), channel_id=1, source_target_pairs={{6,8},{7,9},{14,16},{15,17},{22,24},{23,25},{30,32},{31,33},{38,40... | collective-permute-start | bytes 1572872 | tf_op jit(solution)/shard_map/ppermute | solution.py:395
  36.8 5.8 %collective-permute-start.7 = (bf16[4112,128]{1,0:T(8,128)(2,1)S(1)}, bf16[4112,128]{1,0:T(8,128)(2,1)S(1)}, u32[]{:S(2)}, u32[]{:S(2)}) collective-permute-start(bf16[4112,128]{1,0:T(8,128)(2,1)S(1)} %pick.1.re_ref), channel_id=1, source_target_pairs={{0,1},{1,0},{2,3},{3,2},{4,5},{5,4},{6,7},{7,6},{8,9},{9,8},{10,11... | collective-permute-start | bytes 3158024 | tf_op jit(solution)/shard_map/ppermute | solution.py:395
  47.8 2.9 %collective-permute-start.8 = (bf16[2048,128]{1,0:T(8,128)(2,1)S(1)}, bf16[2048,128]{1,0:T(8,128)(2,1)S(1)}, u32[]{:S(2)}, u32[]{:S(2)}) collective-permute-start(bf16[2048,128]{1,0:T(8,128)(2,1)S(1)} %pick_late.1.rl_ref), channel_id=1, source_target_pairs={{0,1},{1,0},{2,3},{3,2},{4,5},{5,4},{6,7},{7,6},{8,9},{9,8},{10,11... | collective-permute-start | bytes 1572872 | tf_op jit(solution)/shard_map/ppermute | solution.py:395
  50.6 8.3 %collective-permute-start.9 = (f32[2,768]{1,0:T(2,128)S(1)}, f32[2,768]{1,0:T(2,128)S(1)}, u32[]{:S(2)}, u32[]{:S(2)}) collective-permute-start(f32[2,768]{1,0:T(2,128)S(1)} %end_n.1.after_ref), channel_id=1, source_target_pairs={{0,2},{1,3},{2,4},{3,5},{4,6},{5,7},{6,8},{7,9},{8,10},{9,11},{10,... | collective-permute-start | bytes 18440 | tf_op jit(solution)/shard_map/ppermute | solution.py:395
  51.6 8.1 %collective-permute-start.10 = (f32[2,768]{1,0:T(2,128)S(1)}, f32[2,768]{1,0:T(2,128)S(1)}, u32[]{:S(2)}, u32[]{:S(2)}) collective-permute-start(f32[2,768]{1,0:T(2,128)S(1)} %end_p.1), channel_id=1, source_target_pairs={{0,254},{1,255},{2,0},{3,1},{4,2},{5,3},{6,4},{7,5},{8,6},{9,7},{1... | collective-permute-start | bytes 18440 | tf_op jit(solution)/shard_map/ppermute | solution.py:395

commit v7 on v6

--- a/solution.py
+++ b/solution.py
@@ -409,7 +409,7 @@
         scratch=[
             pltpu.VMEM((EARLY, depth), F32),
             pltpu.VMEM((n // LANES, LANES), jnp.int32),
-            pltpu.SemaphoreType.DMA((2,)),
+            pltpu.SemaphoreType.DMA((4,)),
             pltpu.SemaphoreType.DMA,
         ],
         limit=52,

time: 60.5 us -> 60.5 us (level)
  no operation moved by 1% of the time
where the time goes in v7:
time: 60.5 us; the launch traced here: 60.3 us
  starting transfers between devices  32 us (53%)
  Pallas kernels  15.8 us (26%)
  waiting for transfers between devices  11.7 us (19%)
  between operations  0.79 us (1%)
    ppermute x11, starting transfers between devices, on_device(): send = lambda array, route: lax.ppermute(array, 'blk', route)  32 us
    pallas_call x15, Pallas kernels, call(): pl.pallas_call(kernel, out_shape=out_shape, in_specs=in_specs or [vmem] *...  15.8 us
    ppermute x11, waiting for transfers between devices, on_device(): send = lambda array, route: lax.ppermute(array, 'blk', route)  11.7 us
  transfers between devices with their start and end apart: 11, of which 5 were waited for; matrix products, arithmetic and copies ran while one was open for 0% of the time, Pallas kernels for 22%

profile of v7, /device:TPU:1, one launch (start us, length us, event | category | flops | bytes accessed | tf_op | source)
XLA Modules:
  0.0 60.3 jit_solution(11656147366396494574)
XLA Ops:
  0.6 1.7 %unit_early.1.after_ref.ue_ref = bf16[4112,128]{1,0:T(8,128)(2,1)S(1)} custom-call(f32[768,1024]{1,0:T(8,128)} %x_ref.3, s32[6,128]{1,0:T(8,128)} %bitcast.3), custom_call_target="tpu_custom_call" | custom-call | flops 1200000000 | bytes 1024 | tf_op jit(solution)/shard_map/unit_early/pallas_call | solution.py:26
  2.4 2.2 %collective-permute-start.6 = (bf16[4112,128]{1,0:T(8,128)(2,1)S(1)}, bf16[4112,128]{1,0:T(8,128)(2,1)S(1)}, u32[]{:S(2)}, u32[]{:S(2)}) collective-permute-start(bf16[4112,128]{1,0:T(8,128)(2,1)S(1)} %unit_early.1.after_ref.ue_ref), channel_id=1, source_target_pairs={{0,2},{1,3},{2,4},{3,5},{4,6},{5,7},{6,8},{7,9},{8,10},{9,11},{10,... | collective-permute-start | bytes 3158024 | tf_op jit(solution)/shard_map/ppermute | solution.py:395
  4.6 9.0 %collective-permute-start.5 = (bf16[4112,128]{1,0:T(8,128)(2,1)S(1)}, bf16[4112,128]{1,0:T(8,128)(2,1)S(1)}, u32[]{:S(2)}, u32[]{:S(2)}) collective-permute-start(bf16[4112,128]{1,0:T(8,128)(2,1)S(1)} %unit_early.1.after_ref.ue_ref), channel_id=1, source_target_pairs={{0,254},{1,255},{2,0},{3,1},{4,2},{5,3},{6,4},{7,5},{8,6},{9,7},{1... | collective-permute-start | bytes 3158024 | tf_op jit(solution)/shard_map/ppermute | solution.py:395
  13.6 1.3 %unit_late.1.ul_ref = bf16[2048,128]{1,0:T(8,128)(2,1)S(1)} custom-call(f32[768,1024]{1,0:T(8,128)} %x_ref.3, bf16[4112,128]{1,0:T(8,128)(2,1)S(1)} %unit_early.1.after_ref.ue_ref), custom_call_target="tpu_custom_call" | custom-call | flops 1200000000 | bytes 1024 | tf_op jit(solution)/shard_map/unit_late/pallas_call | solution.py:26
  14.9 1.0 %collective-permute-start.1 = (bf16[2048,128]{1,0:T(8,128)(2,1)S(1)}, bf16[2048,128]{1,0:T(8,128)(2,1)S(1)}, u32[]{:S(2)}, u32[]{:S(2)}) collective-permute-start(bf16[2048,128]{1,0:T(8,128)(2,1)S(1)} %unit_late.1.ul_ref), channel_id=1, source_target_pairs={{0,1},{1,0},{2,3},{3,2},{4,5},{5,4},{6,7},{7,6},{8,9},{9,8},{10,11... | collective-permute-start | bytes 1572872 | tf_op jit(solution)/shard_map/ppermute | solution.py:395
  16.0 0.1 collective-permute-start
  16.1 1.6 %own.1.own_in_ref = f32[2,768]{1,0:T(2,128)S(1)} custom-call(bf16[4112,128]{1,0:T(8,128)(2,1)S(1)} %unit_early.1.after_ref.ue_ref, bf16[2048,128]{1,0:T(8,128)(2,1)S(1)} %unit_late.1.ul_ref), custom_call_target="tpu_custom_call" | custom-call | flops 12000000000 | bytes 1024 | tf_op jit(solution)/shard_map/own/pallas_call | solution.py:26
  17.7 0.0 collective-permute-done.1.xl_ref
  17.7 1.3 %collective-permute-done.xe_ref = bf16[4112,128]{1,0:T(8,128)(2,1)S(1)} collective-permute-done((bf16[4112,128]{1,0:T(8,128)(2,1)S(1)}, bf16[4112,128]{1,0:T(8,128)(2,1)S(1)}, u32[]{:S(2)}, u32[]{:S(2)}) %collective-permute-start) | collective-permute-done | bytes 1052704 | tf_op jit(solution)/shard_map/ppermute | solution.py:395
  19.0 1.7 %with_partner.1 = (f32[2,768]{1,0:T(2,128)S(1)}, f32[768,128]{1,0:T(8,128)S(1)}, bf16[2048,128]{1,0:T(8,128)(2,1)S(1)}) custom-call(bf16[4112,128]{1,0:T(8,128)(2,1)S(1)} %unit_early.1.after_ref.ue_ref, bf16[2048,128]{1,0:T(8,128)(2,1)S(1)} %unit_late.1.ul_ref, bf16[4112,128]{1,0:T(8,128)(2,1)S(1)} %collective-permute-done.xe_ref, ...), custom_call_target="tpu_custom_call" | custom-call | flops 12000000000 | bytes 1024 | tf_op jit(solution)/shard_map/with_partner/pallas_call | solution.py:26
  20.7 1.3 %collective-permute-start.4 = (bf16[2048,128]{1,0:T(8,128)(2,1)S(1)}, bf16[2048,128]{1,0:T(8,128)(2,1)S(1)}, u32[]{:S(2)}, u32[]{:S(2)}) collective-permute-start(bf16[2048,128]{1,0:T(8,128)(2,1)S(1)} %get-tuple-element.24), channel_id=1, source_target_pairs={{0,2},{1,3},{2,4},{3,5},{4,6},{5,7},{8,10},{9,11},{10,12},{11,13},... | collective-permute-start | bytes 1572872 | tf_op jit(solution)/shard_map/ppermute | solution.py:395
  22.0 1.3 %collective-permute-start.3 = (bf16[2048,128]{1,0:T(8,128)(2,1)S(1)}, bf16[2048,128]{1,0:T(8,128)(2,1)S(1)}, u32[]{:S(2)}, u32[]{:S(2)}) collective-permute-start(bf16[2048,128]{1,0:T(8,128)(2,1)S(1)} %get-tuple-element.24), channel_id=1, source_target_pairs={{2,0},{3,1},{4,2},{5,3},{6,4},{7,5},{10,8},{11,9},{12,10},{13,11},... | collective-permute-start | bytes 1572872 | tf_op jit(solution)/shard_map/ppermute | solution.py:395
  23.3 6.3 %collective-permute-start.2 = (bf16[2048,128]{1,0:T(8,128)(2,1)S(1)}, bf16[2048,128]{1,0:T(8,128)(2,1)S(1)}, u32[]{:S(2)}, u32[]{:S(2)}) collective-permute-start(bf16[2048,128]{1,0:T(8,128)(2,1)S(1)} %get-tuple-element.24), channel_id=1, source_target_pairs={{6,8},{7,9},{14,16},{15,17},{22,24},{23,25},{30,32},{31,33},{38,40... | collective-permute-start | bytes 1572872 | tf_op jit(solution)/shard_map/ppermute | solution.py:395
  29.6 6.9 %collective-permute-done.6.p_ref.pe_ref = bf16[4112,128]{1,0:T(8,128)(2,1)S(1)} collective-permute-done((bf16[4112,128]{1,0:T(8,128)(2,1)S(1)}, bf16[4112,128]{1,0:T(8,128)(2,1)S(1)}, u32[]{:S(2)}, u32[]{:S(2)}) %collective-permute-start.6) | collective-permute-done | bytes 1052704 | tf_op jit(solution)/shard_map/ppermute | solution.py:395
  36.5 0.2 labels.1.after_ref.p_labels_ref
  36.7 0.0 collective-permute-done.5.ne_ref.n_ref
  36.7 0.1 pick.1.re_ref
  36.8 2.1 %collective-permute-start.7 = (bf16[4112,128]{1,0:T(8,128)(2,1)S(1)}, bf16[4112,128]{1,0:T(8,128)(2,1)S(1)}, u32[]{:S(2)}, u32[]{:S(2)}) collective-permute-start(bf16[4112,128]{1,0:T(8,128)(2,1)S(1)} %pick.1.re_ref), channel_id=1, source_target_pairs={{0,1},{1,0},{2,3},{3,2},{4,5},{5,4},{6,7},{7,6},{8,9},{9,8},{10,11... | collective-permute-start | bytes 3158024 | tf_op jit(solution)/shard_map/ppermute | solution.py:395
  38.9 3.7 %early.1 = (f32[2,768]{1,0:T(2,128)S(1)}, f32[2,512]{1,0:T(2,128)S(1)}, f32[2,512]{1,0:T(2,128)S(1)}, f32[768,128]{1,0:T(8,128)S(1)}) custom-call(bf16[4112,128]{1,0:T(8,128)(2,1)S(1)} %unit_early.1.after_ref.ue_ref, bf16[2048,128]{1,0:T(8,128)(2,1)S(1)} %unit_late.1.ul_ref, bf16[4112,128]{1,0:T(8,128)(2,1)S(1)} %collective-permute-done.xe_ref, ...), custom_call_target="tpu_custom_call" | custom-call | flops 30000001024 | bytes 1024 | tf_op jit(solution)/shard_map/early/pallas_call | solution.py:26
  42.6 0.0 collective-permute-done.7.fe_ref
  42.6 0.9 %early_f.1 = (f32[2,512]{1,0:T(2,128)S(1)}, f32[2,512]{1,0:T(2,128)S(1)}, f32[768,128]{1,0:T(8,128)S(1)}) custom-call(bf16[4112,128]{1,0:T(8,128)(2,1)S(1)} %collective-permute-done.7.fe_ref, bf16[4112,128]{1,0:T(8,128)(2,1)S(1)} %pick.1.re_ref, f32[2,512]{1,0:T(2,128)S(1)} %get-tuple-element.29.p_in_ref, f32[2,512]{1,0:T(2,128)S(1)} %get-tuple-element.30.n_in_ref), custom_call_target="tpu_custom_call" | custom-call | flops 6000000000 | bytes 1024 | tf_op jit(solution)/shard_map/early_f/pallas_call | solution.py:26
  43.6 0.0 collective-permute-done.4.pl_ref.p_ref
  43.6 0.0 collective-permute-done.3.nl_ref.n_ref
  43.6 1.7 %near.1 = (f32[2,768]{1,0:T(2,128)S(1)}, f32[2,512]{1,0:T(2,128)S(1)}, f32[2,512]{1,0:T(2,128)S(1)}, f32[2,256]{1,0:T(2,128)S(1)}, f32[2,256]{1,0:T(2,128)S(1)}) custom-call(bf16[2048,128]{1,0:T(8,128)(2,1)S(1)} %collective-permute-done.4.pl_ref.p_ref, bf16[2048,128]{1,0:T(8,128)(2,1)S(1)} %collective-permute-done.3.nl_ref.n_ref, ...), custom_call_target="tpu_custom_call" | custom-call | flops 20400001024 | bytes 1024 | tf_op jit(solution)/shard_map/near/pallas_call | solution.py:26
  45.3 2.4 %collective-permute-done.2.w_ref = bf16[2048,128]{1,0:T(8,128)(2,1)S(1)} collective-permute-done((bf16[2048,128]{1,0:T(8,128)(2,1)S(1)}, bf16[2048,128]{1,0:T(8,128)(2,1)S(1)}, u32[]{:S(2)}, u32[]{:S(2)}) %collective-permute-start.2) | collective-permute-done | bytes 524320 | tf_op jit(solution)/shard_map/ppermute | solution.py:395
  47.7 1.3 %collective-permute-start.8 = (bf16[2048,128]{1,0:T(8,128)(2,1)S(1)}, bf16[2048,128]{1,0:T(8,128)(2,1)S(1)}, u32[]{:S(2)}, u32[]{:S(2)}) collective-permute-start(bf16[2048,128]{1,0:T(8,128)(2,1)S(1)} %pick_late.1.rl_ref), channel_id=1, source_target_pairs={{0,1},{1,0},{2,3},{3,2},{4,5},{5,4},{6,7},{7,6},{8,9},{9,8},{10,11... | collective-permute-start | bytes 1572872 | tf_op jit(solution)/shard_map/ppermute | solution.py:395
  49.1 1.2 %far.1 = (f32[2,768]{1,0:T(2,128)S(1)}, f32[2,768]{1,0:T(2,128)S(1)}, f32[2,768]{1,0:T(2,128)S(1)}) custom-call(bf16[2048,128]{1,0:T(8,128)(2,1)S(1)} %collective-permute-done.2.w_ref, bf16[2048,128]{1,0:T(8,128)(2,1)S(1)} %collective-permute-done.3.nl_ref.n_ref, bf16[2048,128]{1,0:T(8,128)(2,1)S(1)} %collective-permute-done.4.pl_ref.p_ref, ...), custom_call_target="tpu_custom_call" | custom-call | flops 2400000000 | bytes 1024 | tf_op jit(solution)/shard_map/far/pallas_call | solution.py:26
  50.3 0.3 collective-permute-done.8.fl_ref
  50.6 0.0 collective-permute-start.9
  50.6 0.9 %end_p.1 = f32[2,768]{1,0:T(2,128)S(1)} custom-call(bf16[4112,128]{1,0:T(8,128)(2,1)S(1)} %collective-permute-done.7.fe_ref, bf16[2048,128]{1,0:T(8,128)(2,1)S(1)} %collective-permute-done.8.fl_ref, bf16[4112,128]{1,0:T(8,128)(2,1)S(1)} %pick.1.re_ref, bf16[2048,128]{1,0:T(8,128)(2,1)S(1)} %pick_late.1.rl_ref, ...), custom_call_target="tpu_custom_call" | custom-call | flops 3600000000 | bytes 1024 | tf_op jit(solution)/shard_map/end_p/pallas_call | solution.py:26
  51.5 7.3 %collective-permute-start.10 = (f32[2,768]{1,0:T(2,128)S(1)}, f32[2,768]{1,0:T(2,128)S(1)}, u32[]{:S(2)}, u32[]{:S(2)}) collective-permute-start(f32[2,768]{1,0:T(2,128)S(1)} %end_p.1), channel_id=1, source_target_pairs={{0,254},{1,255},{2,0},{3,1},{4,2},{5,3},{6,4},{7,5},{8,6},{9,7},{1... | collective-permute-start | bytes 18440 | tf_op jit(solution)/shard_map/ppermute | solution.py:395
  58.9 0.0 collective-permute-done.9.more_ref
  58.9 0.8 %collective-permute-done.10.more_ref = f32[2,768]{1,0:T(2,128)S(1)} collective-permute-done((f32[2,768]{1,0:T(2,128)S(1)}, f32[2,768]{1,0:T(2,128)S(1)}, u32[]{:S(2)}, u32[]{:S(2)}) %collective-permute-start.10) | collective-permute-done | bytes 6176 | tf_op jit(solution)/shard_map/ppermute | solution.py:395
  59.6 0.6 %last.1 = (f32[6,128]{1,0:T(8,128)}, f32[6,128]{1,0:T(8,128)}) custom-call(f32[2,768]{1,0:T(2,128)S(1)} %sum.1.own_ref, f32[2,768]{1,0:T(2,128)S(1)} %collective-permute-done.10.more_ref), custom_call_target="tpu_custom_call" | custom-call | flops 120000000 | bytes 1024 | tf_op jit(solution)/shard_map/last/pallas_call | solution.py:26
  (3 shorter events, 0.0 us)
Async XLA Ops:
  2.4 34.1 %collective-permute-start.6 = (bf16[4112,128]{1,0:T(8,128)(2,1)S(1)}, bf16[4112,128]{1,0:T(8,128)(2,1)S(1)}, u32[]{:S(2)}, u32[]{:S(2)}) collective-permute-start(bf16[4112,128]{1,0:T(8,128)(2,1)S(1)} %unit_early.1.after_ref.ue_ref), channel_id=1, source_target_pairs={{0,2},{1,3},{2,4},{3,5},{4,6},{5,7},{6,8},{7,9},{8,10},{9,11},{10,... | collective-permute-start | bytes 3158024 | tf_op jit(solution)/shard_map/ppermute | solution.py:395
  4.6 32.1 %collective-permute-start.5 = (bf16[4112,128]{1,0:T(8,128)(2,1)S(1)}, bf16[4112,128]{1,0:T(8,128)(2,1)S(1)}, u32[]{:S(2)}, u32[]{:S(2)}) collective-permute-start(bf16[4112,128]{1,0:T(8,128)(2,1)S(1)} %unit_early.1.after_ref.ue_ref), channel_id=1, source_target_pairs={{0,254},{1,255},{2,0},{3,1},{4,2},{5,3},{6,4},{7,5},{8,6},{9,7},{1... | collective-permute-start | bytes 3158024 | tf_op jit(solution)/shard_map/ppermute | solution.py:395
  14.9 2.8 %collective-permute-start.1 = (bf16[2048,128]{1,0:T(8,128)(2,1)S(1)}, bf16[2048,128]{1,0:T(8,128)(2,1)S(1)}, u32[]{:S(2)}, u32[]{:S(2)}) collective-permute-start(bf16[2048,128]{1,0:T(8,128)(2,1)S(1)} %unit_late.1.ul_ref), channel_id=1, source_target_pairs={{0,1},{1,0},{2,3},{3,2},{4,5},{5,4},{6,7},{7,6},{8,9},{9,8},{10,11... | collective-permute-start | bytes 1572872 | tf_op jit(solution)/shard_map/ppermute | solution.py:395
  16.0 3.0 %collective-permute-start = (bf16[4112,128]{1,0:T(8,128)(2,1)S(1)}, bf16[4112,128]{1,0:T(8,128)(2,1)S(1)}, u32[]{:S(2)}, u32[]{:S(2)}) collective-permute-start(bf16[4112,128]{1,0:T(8,128)(2,1)S(1)} %unit_early.1.after_ref.ue_ref), channel_id=1, source_target_pairs={{0,1},{1,0},{2,3},{3,2},{4,5},{5,4},{6,7},{7,6},{8,9},{9,8},{10,11... | collective-permute-start | bytes 3158024 | tf_op jit(solution)/shard_map/ppermute | solution.py:395
  20.7 22.9 %collective-permute-start.4 = (bf16[2048,128]{1,0:T(8,128)(2,1)S(1)}, bf16[2048,128]{1,0:T(8,128)(2,1)S(1)}, u32[]{:S(2)}, u32[]{:S(2)}) collective-permute-start(bf16[2048,128]{1,0:T(8,128)(2,1)S(1)} %get-tuple-element.24), channel_id=1, source_target_pairs={{0,2},{1,3},{2,4},{3,5},{4,6},{5,7},{8,10},{9,11},{10,12},{11,13},... | collective-permute-start | bytes 1572872 | tf_op jit(solution)/shard_map/ppermute | solution.py:395
  22.0 21.6 %collective-permute-start.3 = (bf16[2048,128]{1,0:T(8,128)(2,1)S(1)}, bf16[2048,128]{1,0:T(8,128)(2,1)S(1)}, u32[]{:S(2)}, u32[]{:S(2)}) collective-permute-start(bf16[2048,128]{1,0:T(8,128)(2,1)S(1)} %get-tuple-element.24), channel_id=1, source_target_pairs={{2,0},{3,1},{4,2},{5,3},{6,4},{7,5},{10,8},{11,9},{12,10},{13,11},... | collective-permute-start | bytes 1572872 | tf_op jit(solution)/shard_map/ppermute | solution.py:395
  23.3 24.4 %collective-permute-start.2 = (bf16[2048,128]{1,0:T(8,128)(2,1)S(1)}, bf16[2048,128]{1,0:T(8,128)(2,1)S(1)}, u32[]{:S(2)}, u32[]{:S(2)}) collective-permute-start(bf16[2048,128]{1,0:T(8,128)(2,1)S(1)} %get-tuple-element.24), channel_id=1, source_target_pairs={{6,8},{7,9},{14,16},{15,17},{22,24},{23,25},{30,32},{31,33},{38,40... | collective-permute-start | bytes 1572872 | tf_op jit(solution)/shard_map/ppermute | solution.py:395
  36.8 5.8 %collective-permute-start.7 = (bf16[4112,128]{1,0:T(8,128)(2,1)S(1)}, bf16[4112,128]{1,0:T(8,128)(2,1)S(1)}, u32[]{:S(2)}, u32[]{:S(2)}) collective-permute-start(bf16[4112,128]{1,0:T(8,128)(2,1)S(1)} %pick.1.re_ref), channel_id=1, source_target_pairs={{0,1},{1,0},{2,3},{3,2},{4,5},{5,4},{6,7},{7,6},{8,9},{9,8},{10,11... | collective-permute-start | bytes 3158024 | tf_op jit(solution)/shard_map/ppermute | solution.py:395
  47.7 2.9 %collective-permute-start.8 = (bf16[2048,128]{1,0:T(8,128)(2,1)S(1)}, bf16[2048,128]{1,0:T(8,128)(2,1)S(1)}, u32[]{:S(2)}, u32[]{:S(2)}) collective-permute-start(bf16[2048,128]{1,0:T(8,128)(2,1)S(1)} %pick_late.1.rl_ref), channel_id=1, source_target_pairs={{0,1},{1,0},{2,3},{3,2},{4,5},{5,4},{6,7},{7,6},{8,9},{9,8},{10,11... | collective-permute-start | bytes 1572872 | tf_op jit(solution)/shard_map/ppermute | solution.py:395
  50.6 8.3 %collective-permute-start.9 = (f32[2,768]{1,0:T(2,128)S(1)}, f32[2,768]{1,0:T(2,128)S(1)}, u32[]{:S(2)}, u32[]{:S(2)}) collective-permute-start(f32[2,768]{1,0:T(2,128)S(1)} %end_n.1.after_ref), channel_id=1, source_target_pairs={{0,2},{1,3},{2,4},{3,5},{4,6},{5,7},{6,8},{7,9},{8,10},{9,11},{10,... | collective-permute-start | bytes 18440 | tf_op jit(solution)/shard_map/ppermute | solution.py:395
  51.5 8.1 %collective-permute-start.10 = (f32[2,768]{1,0:T(2,128)S(1)}, f32[2,768]{1,0:T(2,128)S(1)}, u32[]{:S(2)}, u32[]{:S(2)}) collective-permute-start(f32[2,768]{1,0:T(2,128)S(1)} %end_p.1), channel_id=1, source_target_pairs={{0,254},{1,255},{2,0},{3,1},{4,2},{5,3},{6,4},{7,5},{8,6},{9,7},{1... | collective-permute-start | bytes 18440 | tf_op jit(solution)/shard_map/ppermute | solution.py:395

commit v8 on v7

--- a/solution.py
+++ b/solution.py
@@ -126,7 +126,7 @@
     return row[:, EARLY:] if late else row[:, :EARLY]
 
 
-def normalise(x_ref, first, held, sems, write):
+def normalise(x_ref, first, held, sems, write, meanwhile=None):
     rows, parts = held.shape[0], sems.shape[0]
     part = rows // parts
     copies = [
@@ -137,6 +137,8 @@
     ]
     for copy in copies:
         copy.start()
+    if meanwhile is not None:
+        meanwhile()
     for i in range(parts):
         copies[i].wait()
         x = held[i * part : (i + 1) * part, :]
@@ -152,13 +154,15 @@
     def write(slab, row, unit):
         out_ref[HEAD + slab * EARLY + row : HEAD + slab * EARLY + row + unit.shape[0], :] = unit
 
-    normalise(x_ref, 0, held, sems, write)
-    labels_copy.wait()
-    labels = labels_ref[...]
-    low = lax.rem(labels, 256)
-    blank = jnp.zeros((HEAD - 2 * labels.shape[0], LANES), F32)
-    head = jnp.concatenate([(labels - low).astype(F32), low.astype(F32), blank], axis=0)
-    out_ref[0:HEAD, :] = head.astype(BF16)
+    def write_labels():
+        labels_copy.wait()
+        labels = labels_ref[...]
+        low = lax.rem(labels, 256)
+        blank = jnp.zeros((HEAD - 2 * labels.shape[0], LANES), F32)
+        head = jnp.concatenate([(labels - low).astype(F32), low.astype(F32), blank], axis=0)
+        out_ref[0:HEAD, :] = head.astype(BF16)
+
+    normalise(x_ref, 0, held, sems, write, write_labels)
 
 
 def unit_late_kernel(x_ref, after_ref, out_ref, held, sems):

time: 60.5 us -> 60.5 us (level)
  no operation moved by 1% of the time
where the time goes in v8:
time: 60.5 us; the launch traced here: 60.3 us
  starting transfers between devices  32 us (53%)
  Pallas kernels  15.8 us (26%)
  waiting for transfers between devices  11.7 us (19%)
  between operations  0.79 us (1%)
    ppermute x11, starting transfers between devices, on_device(): send = lambda array, route: lax.ppermute(array, 'blk', route)  32 us
    pallas_call x15, Pallas kernels, call(): pl.pallas_call(kernel, out_shape=out_shape, in_specs=in_specs or [vmem] *...  15.8 us
    ppermute x11, waiting for transfers between devices, on_device(): send = lambda array, route: lax.ppermute(array, 'blk', route)  11.7 us
  transfers between devices with their start and end apart: 11, of which 5 were waited for; matrix products, arithmetic and copies ran while one was open for 0% of the time, Pallas kernels for 22%

profile of v8, /device:TPU:1, one launch (start us, length us, event | category | flops | bytes accessed | tf_op | source)
XLA Modules:
  0.0 60.3 jit_solution(13592166442378764235)
XLA Ops:
  0.6 1.7 %unit_early.1.after_ref.ue_ref = bf16[4112,128]{1,0:T(8,128)(2,1)S(1)} custom-call(f32[768,1024]{1,0:T(8,128)} %x_ref.3, s32[6,128]{1,0:T(8,128)} %bitcast.3), custom_call_target="tpu_custom_call" | custom-call | flops 1200000000 | bytes 1024 | tf_op jit(solution)/shard_map/unit_early/pallas_call | solution.py:26
  2.4 2.2 %collective-permute-start.6 = (bf16[4112,128]{1,0:T(8,128)(2,1)S(1)}, bf16[4112,128]{1,0:T(8,128)(2,1)S(1)}, u32[]{:S(2)}, u32[]{:S(2)}) collective-permute-start(bf16[4112,128]{1,0:T(8,128)(2,1)S(1)} %unit_early.1.after_ref.ue_ref), channel_id=1, source_target_pairs={{0,2},{1,3},{2,4},{3,5},{4,6},{5,7},{6,8},{7,9},{8,10},{9,11},{10,... | collective-permute-start | bytes 3158024 | tf_op jit(solution)/shard_map/ppermute | solution.py:399
  4.6 9.0 %collective-permute-start.5 = (bf16[4112,128]{1,0:T(8,128)(2,1)S(1)}, bf16[4112,128]{1,0:T(8,128)(2,1)S(1)}, u32[]{:S(2)}, u32[]{:S(2)}) collective-permute-start(bf16[4112,128]{1,0:T(8,128)(2,1)S(1)} %unit_early.1.after_ref.ue_ref), channel_id=1, source_target_pairs={{0,254},{1,255},{2,0},{3,1},{4,2},{5,3},{6,4},{7,5},{8,6},{9,7},{1... | collective-permute-start | bytes 3158024 | tf_op jit(solution)/shard_map/ppermute | solution.py:399
  13.6 1.3 %unit_late.1.ul_ref = bf16[2048,128]{1,0:T(8,128)(2,1)S(1)} custom-call(f32[768,1024]{1,0:T(8,128)} %x_ref.3, bf16[4112,128]{1,0:T(8,128)(2,1)S(1)} %unit_early.1.after_ref.ue_ref), custom_call_target="tpu_custom_call" | custom-call | flops 1200000000 | bytes 1024 | tf_op jit(solution)/shard_map/unit_late/pallas_call | solution.py:26
  14.9 1.0 %collective-permute-start.1 = (bf16[2048,128]{1,0:T(8,128)(2,1)S(1)}, bf16[2048,128]{1,0:T(8,128)(2,1)S(1)}, u32[]{:S(2)}, u32[]{:S(2)}) collective-permute-start(bf16[2048,128]{1,0:T(8,128)(2,1)S(1)} %unit_late.1.ul_ref), channel_id=1, source_target_pairs={{0,1},{1,0},{2,3},{3,2},{4,5},{5,4},{6,7},{7,6},{8,9},{9,8},{10,11... | collective-permute-start | bytes 1572872 | tf_op jit(solution)/shard_map/ppermute | solution.py:399
  16.0 0.1 collective-permute-start
  16.1 1.6 %own.1.own_in_ref = f32[2,768]{1,0:T(2,128)S(1)} custom-call(bf16[4112,128]{1,0:T(8,128)(2,1)S(1)} %unit_early.1.after_ref.ue_ref, bf16[2048,128]{1,0:T(8,128)(2,1)S(1)} %unit_late.1.ul_ref), custom_call_target="tpu_custom_call" | custom-call | flops 12000000000 | bytes 1024 | tf_op jit(solution)/shard_map/own/pallas_call | solution.py:26
  17.7 0.0 collective-permute-done.1.xl_ref
  17.7 1.3 %collective-permute-done.xe_ref = bf16[4112,128]{1,0:T(8,128)(2,1)S(1)} collective-permute-done((bf16[4112,128]{1,0:T(8,128)(2,1)S(1)}, bf16[4112,128]{1,0:T(8,128)(2,1)S(1)}, u32[]{:S(2)}, u32[]{:S(2)}) %collective-permute-start) | collective-permute-done | bytes 1052704 | tf_op jit(solution)/shard_map/ppermute | solution.py:399
  19.0 1.7 %with_partner.1 = (f32[2,768]{1,0:T(2,128)S(1)}, f32[768,128]{1,0:T(8,128)S(1)}, bf16[2048,128]{1,0:T(8,128)(2,1)S(1)}) custom-call(bf16[4112,128]{1,0:T(8,128)(2,1)S(1)} %unit_early.1.after_ref.ue_ref, bf16[2048,128]{1,0:T(8,128)(2,1)S(1)} %unit_late.1.ul_ref, bf16[4112,128]{1,0:T(8,128)(2,1)S(1)} %collective-permute-done.xe_ref, ...), custom_call_target="tpu_custom_call" | custom-call | flops 12000000000 | bytes 1024 | tf_op jit(solution)/shard_map/with_partner/pallas_call | solution.py:26
  20.7 1.3 %collective-permute-start.4 = (bf16[2048,128]{1,0:T(8,128)(2,1)S(1)}, bf16[2048,128]{1,0:T(8,128)(2,1)S(1)}, u32[]{:S(2)}, u32[]{:S(2)}) collective-permute-start(bf16[2048,128]{1,0:T(8,128)(2,1)S(1)} %get-tuple-element.24), channel_id=1, source_target_pairs={{0,2},{1,3},{2,4},{3,5},{4,6},{5,7},{8,10},{9,11},{10,12},{11,13},... | collective-permute-start | bytes 1572872 | tf_op jit(solution)/shard_map/ppermute | solution.py:399
  22.0 1.3 %collective-permute-start.3 = (bf16[2048,128]{1,0:T(8,128)(2,1)S(1)}, bf16[2048,128]{1,0:T(8,128)(2,1)S(1)}, u32[]{:S(2)}, u32[]{:S(2)}) collective-permute-start(bf16[2048,128]{1,0:T(8,128)(2,1)S(1)} %get-tuple-element.24), channel_id=1, source_target_pairs={{2,0},{3,1},{4,2},{5,3},{6,4},{7,5},{10,8},{11,9},{12,10},{13,11},... | collective-permute-start | bytes 1572872 | tf_op jit(solution)/shard_map/ppermute | solution.py:399
  23.3 6.2 %collective-permute-start.2 = (bf16[2048,128]{1,0:T(8,128)(2,1)S(1)}, bf16[2048,128]{1,0:T(8,128)(2,1)S(1)}, u32[]{:S(2)}, u32[]{:S(2)}) collective-permute-start(bf16[2048,128]{1,0:T(8,128)(2,1)S(1)} %get-tuple-element.24), channel_id=1, source_target_pairs={{6,8},{7,9},{14,16},{15,17},{22,24},{23,25},{30,32},{31,33},{38,40... | collective-permute-start | bytes 1572872 | tf_op jit(solution)/shard_map/ppermute | solution.py:399
  29.6 6.9 %collective-permute-done.6.p_ref.pe_ref = bf16[4112,128]{1,0:T(8,128)(2,1)S(1)} collective-permute-done((bf16[4112,128]{1,0:T(8,128)(2,1)S(1)}, bf16[4112,128]{1,0:T(8,128)(2,1)S(1)}, u32[]{:S(2)}, u32[]{:S(2)}) %collective-permute-start.6) | collective-permute-done | bytes 1052704 | tf_op jit(solution)/shard_map/ppermute | solution.py:399
  36.5 0.2 labels.1.after_ref.p_labels_ref
  36.7 0.0 collective-permute-done.5.ne_ref.n_ref
  36.7 0.1 pick.1.re_ref
  36.8 2.1 %collective-permute-start.7 = (bf16[4112,128]{1,0:T(8,128)(2,1)S(1)}, bf16[4112,128]{1,0:T(8,128)(2,1)S(1)}, u32[]{:S(2)}, u32[]{:S(2)}) collective-permute-start(bf16[4112,128]{1,0:T(8,128)(2,1)S(1)} %pick.1.re_ref), channel_id=1, source_target_pairs={{0,1},{1,0},{2,3},{3,2},{4,5},{5,4},{6,7},{7,6},{8,9},{9,8},{10,11... | collective-permute-start | bytes 3158024 | tf_op jit(solution)/shard_map/ppermute | solution.py:399
  38.9 3.7 %early.1 = (f32[2,768]{1,0:T(2,128)S(1)}, f32[2,512]{1,0:T(2,128)S(1)}, f32[2,512]{1,0:T(2,128)S(1)}, f32[768,128]{1,0:T(8,128)S(1)}) custom-call(bf16[4112,128]{1,0:T(8,128)(2,1)S(1)} %unit_early.1.after_ref.ue_ref, bf16[2048,128]{1,0:T(8,128)(2,1)S(1)} %unit_late.1.ul_ref, bf16[4112,128]{1,0:T(8,128)(2,1)S(1)} %collective-permute-done.xe_ref, ...), custom_call_target="tpu_custom_call" | custom-call | flops 30000001024 | bytes 1024 | tf_op jit(solution)/shard_map/early/pallas_call | solution.py:26
  42.6 0.0 collective-permute-done.7.fe_ref
  42.6 0.9 %early_f.1 = (f32[2,512]{1,0:T(2,128)S(1)}, f32[2,512]{1,0:T(2,128)S(1)}, f32[768,128]{1,0:T(8,128)S(1)}) custom-call(bf16[4112,128]{1,0:T(8,128)(2,1)S(1)} %collective-permute-done.7.fe_ref, bf16[4112,128]{1,0:T(8,128)(2,1)S(1)} %pick.1.re_ref, f32[2,512]{1,0:T(2,128)S(1)} %get-tuple-element.29.p_in_ref, f32[2,512]{1,0:T(2,128)S(1)} %get-tuple-element.30.n_in_ref), custom_call_target="tpu_custom_call" | custom-call | flops 6000000000 | bytes 1024 | tf_op jit(solution)/shard_map/early_f/pallas_call | solution.py:26
  43.6 0.0 collective-permute-done.4.pl_ref.p_ref
  43.6 0.0 collective-permute-done.3.nl_ref.n_ref
  43.6 1.7 %near.1 = (f32[2,768]{1,0:T(2,128)S(1)}, f32[2,512]{1,0:T(2,128)S(1)}, f32[2,512]{1,0:T(2,128)S(1)}, f32[2,256]{1,0:T(2,128)S(1)}, f32[2,256]{1,0:T(2,128)S(1)}) custom-call(bf16[2048,128]{1,0:T(8,128)(2,1)S(1)} %collective-permute-done.4.pl_ref.p_ref, bf16[2048,128]{1,0:T(8,128)(2,1)S(1)} %collective-permute-done.3.nl_ref.n_ref, ...), custom_call_target="tpu_custom_call" | custom-call | flops 20400001024 | bytes 1024 | tf_op jit(solution)/shard_map/near/pallas_call | solution.py:26
  45.3 2.4 %collective-permute-done.2.w_ref = bf16[2048,128]{1,0:T(8,128)(2,1)S(1)} collective-permute-done((bf16[2048,128]{1,0:T(8,128)(2,1)S(1)}, bf16[2048,128]{1,0:T(8,128)(2,1)S(1)}, u32[]{:S(2)}, u32[]{:S(2)}) %collective-permute-start.2) | collective-permute-done | bytes 524320 | tf_op jit(solution)/shard_map/ppermute | solution.py:399
  47.7 1.3 %collective-permute-start.8 = (bf16[2048,128]{1,0:T(8,128)(2,1)S(1)}, bf16[2048,128]{1,0:T(8,128)(2,1)S(1)}, u32[]{:S(2)}, u32[]{:S(2)}) collective-permute-start(bf16[2048,128]{1,0:T(8,128)(2,1)S(1)} %pick_late.1.rl_ref), channel_id=1, source_target_pairs={{0,1},{1,0},{2,3},{3,2},{4,5},{5,4},{6,7},{7,6},{8,9},{9,8},{10,11... | collective-permute-start | bytes 1572872 | tf_op jit(solution)/shard_map/ppermute | solution.py:399
  49.1 1.2 %far.1 = (f32[2,768]{1,0:T(2,128)S(1)}, f32[2,768]{1,0:T(2,128)S(1)}, f32[2,768]{1,0:T(2,128)S(1)}) custom-call(bf16[2048,128]{1,0:T(8,128)(2,1)S(1)} %collective-permute-done.2.w_ref, bf16[2048,128]{1,0:T(8,128)(2,1)S(1)} %collective-permute-done.3.nl_ref.n_ref, bf16[2048,128]{1,0:T(8,128)(2,1)S(1)} %collective-permute-done.4.pl_ref.p_ref, ...), custom_call_target="tpu_custom_call" | custom-call | flops 2400000000 | bytes 1024 | tf_op jit(solution)/shard_map/far/pallas_call | solution.py:26
  50.3 0.3 collective-permute-done.8.fl_ref
  50.6 0.0 collective-permute-start.9
  50.6 0.9 %end_p.1 = f32[2,768]{1,0:T(2,128)S(1)} custom-call(bf16[4112,128]{1,0:T(8,128)(2,1)S(1)} %collective-permute-done.7.fe_ref, bf16[2048,128]{1,0:T(8,128)(2,1)S(1)} %collective-permute-done.8.fl_ref, bf16[4112,128]{1,0:T(8,128)(2,1)S(1)} %pick.1.re_ref, bf16[2048,128]{1,0:T(8,128)(2,1)S(1)} %pick_late.1.rl_ref, ...), custom_call_target="tpu_custom_call" | custom-call | flops 3600000000 | bytes 1024 | tf_op jit(solution)/shard_map/end_p/pallas_call | solution.py:26
  51.5 7.3 %collective-permute-start.10 = (f32[2,768]{1,0:T(2,128)S(1)}, f32[2,768]{1,0:T(2,128)S(1)}, u32[]{:S(2)}, u32[]{:S(2)}) collective-permute-start(f32[2,768]{1,0:T(2,128)S(1)} %end_p.1), channel_id=1, source_target_pairs={{0,254},{1,255},{2,0},{3,1},{4,2},{5,3},{6,4},{7,5},{8,6},{9,7},{1... | collective-permute-start | bytes 18440 | tf_op jit(solution)/shard_map/ppermute | solution.py:399
  58.9 0.0 collective-permute-done.9.more_ref
  58.9 0.8 %collective-permute-done.10.more_ref = f32[2,768]{1,0:T(2,128)S(1)} collective-permute-done((f32[2,768]{1,0:T(2,128)S(1)}, f32[2,768]{1,0:T(2,128)S(1)}, u32[]{:S(2)}, u32[]{:S(2)}) %collective-permute-start.10) | collective-permute-done | bytes 6176 | tf_op jit(solution)/shard_map/ppermute | solution.py:399
  59.7 0.6 %last.1 = (f32[6,128]{1,0:T(8,128)}, f32[6,128]{1,0:T(8,128)}) custom-call(f32[2,768]{1,0:T(2,128)S(1)} %sum.1.own_ref, f32[2,768]{1,0:T(2,128)S(1)} %collective-permute-done.10.more_ref), custom_call_target="tpu_custom_call" | custom-call | flops 120000000 | bytes 1024 | tf_op jit(solution)/shard_map/last/pallas_call | solution.py:26
  (3 shorter events, 0.0 us)
Async XLA Ops:
  2.4 34.1 %collective-permute-start.6 = (bf16[4112,128]{1,0:T(8,128)(2,1)S(1)}, bf16[4112,128]{1,0:T(8,128)(2,1)S(1)}, u32[]{:S(2)}, u32[]{:S(2)}) collective-permute-start(bf16[4112,128]{1,0:T(8,128)(2,1)S(1)} %unit_early.1.after_ref.ue_ref), channel_id=1, source_target_pairs={{0,2},{1,3},{2,4},{3,5},{4,6},{5,7},{6,8},{7,9},{8,10},{9,11},{10,... | collective-permute-start | bytes 3158024 | tf_op jit(solution)/shard_map/ppermute | solution.py:399
  4.6 32.1 %collective-permute-start.5 = (bf16[4112,128]{1,0:T(8,128)(2,1)S(1)}, bf16[4112,128]{1,0:T(8,128)(2,1)S(1)}, u32[]{:S(2)}, u32[]{:S(2)}) collective-permute-start(bf16[4112,128]{1,0:T(8,128)(2,1)S(1)} %unit_early.1.after_ref.ue_ref), channel_id=1, source_target_pairs={{0,254},{1,255},{2,0},{3,1},{4,2},{5,3},{6,4},{7,5},{8,6},{9,7},{1... | collective-permute-start | bytes 3158024 | tf_op jit(solution)/shard_map/ppermute | solution.py:399
  14.9 2.8 %collective-permute-start.1 = (bf16[2048,128]{1,0:T(8,128)(2,1)S(1)}, bf16[2048,128]{1,0:T(8,128)(2,1)S(1)}, u32[]{:S(2)}, u32[]{:S(2)}) collective-permute-start(bf16[2048,128]{1,0:T(8,128)(2,1)S(1)} %unit_late.1.ul_ref), channel_id=1, source_target_pairs={{0,1},{1,0},{2,3},{3,2},{4,5},{5,4},{6,7},{7,6},{8,9},{9,8},{10,11... | collective-permute-start | bytes 1572872 | tf_op jit(solution)/shard_map/ppermute | solution.py:399
  16.0 3.0 %collective-permute-start = (bf16[4112,128]{1,0:T(8,128)(2,1)S(1)}, bf16[4112,128]{1,0:T(8,128)(2,1)S(1)}, u32[]{:S(2)}, u32[]{:S(2)}) collective-permute-start(bf16[4112,128]{1,0:T(8,128)(2,1)S(1)} %unit_early.1.after_ref.ue_ref), channel_id=1, source_target_pairs={{0,1},{1,0},{2,3},{3,2},{4,5},{5,4},{6,7},{7,6},{8,9},{9,8},{10,11... | collective-permute-start | bytes 3158024 | tf_op jit(solution)/shard_map/ppermute | solution.py:399
  20.7 22.9 %collective-permute-start.4 = (bf16[2048,128]{1,0:T(8,128)(2,1)S(1)}, bf16[2048,128]{1,0:T(8,128)(2,1)S(1)}, u32[]{:S(2)}, u32[]{:S(2)}) collective-permute-start(bf16[2048,128]{1,0:T(8,128)(2,1)S(1)} %get-tuple-element.24), channel_id=1, source_target_pairs={{0,2},{1,3},{2,4},{3,5},{4,6},{5,7},{8,10},{9,11},{10,12},{11,13},... | collective-permute-start | bytes 1572872 | tf_op jit(solution)/shard_map/ppermute | solution.py:399
  22.0 21.6 %collective-permute-start.3 = (bf16[2048,128]{1,0:T(8,128)(2,1)S(1)}, bf16[2048,128]{1,0:T(8,128)(2,1)S(1)}, u32[]{:S(2)}, u32[]{:S(2)}) collective-permute-start(bf16[2048,128]{1,0:T(8,128)(2,1)S(1)} %get-tuple-element.24), channel_id=1, source_target_pairs={{2,0},{3,1},{4,2},{5,3},{6,4},{7,5},{10,8},{11,9},{12,10},{13,11},... | collective-permute-start | bytes 1572872 | tf_op jit(solution)/shard_map/ppermute | solution.py:399
  23.3 24.4 %collective-permute-start.2 = (bf16[2048,128]{1,0:T(8,128)(2,1)S(1)}, bf16[2048,128]{1,0:T(8,128)(2,1)S(1)}, u32[]{:S(2)}, u32[]{:S(2)}) collective-permute-start(bf16[2048,128]{1,0:T(8,128)(2,1)S(1)} %get-tuple-element.24), channel_id=1, source_target_pairs={{6,8},{7,9},{14,16},{15,17},{22,24},{23,25},{30,32},{31,33},{38,40... | collective-permute-start | bytes 1572872 | tf_op jit(solution)/shard_map/ppermute | solution.py:399
  36.8 5.8 %collective-permute-start.7 = (bf16[4112,128]{1,0:T(8,128)(2,1)S(1)}, bf16[4112,128]{1,0:T(8,128)(2,1)S(1)}, u32[]{:S(2)}, u32[]{:S(2)}) collective-permute-start(bf16[4112,128]{1,0:T(8,128)(2,1)S(1)} %pick.1.re_ref), channel_id=1, source_target_pairs={{0,1},{1,0},{2,3},{3,2},{4,5},{5,4},{6,7},{7,6},{8,9},{9,8},{10,11... | collective-permute-start | bytes 3158024 | tf_op jit(solution)/shard_map/ppermute | solution.py:399
  47.7 2.9 %collective-permute-start.8 = (bf16[2048,128]{1,0:T(8,128)(2,1)S(1)}, bf16[2048,128]{1,0:T(8,128)(2,1)S(1)}, u32[]{:S(2)}, u32[]{:S(2)}) collective-permute-start(bf16[2048,128]{1,0:T(8,128)(2,1)S(1)} %pick_late.1.rl_ref), channel_id=1, source_target_pairs={{0,1},{1,0},{2,3},{3,2},{4,5},{5,4},{6,7},{7,6},{8,9},{9,8},{10,11... | collective-permute-start | bytes 1572872 | tf_op jit(solution)/shard_map/ppermute | solution.py:399
  50.6 8.3 %collective-permute-start.9 = (f32[2,768]{1,0:T(2,128)S(1)}, f32[2,768]{1,0:T(2,128)S(1)}, u32[]{:S(2)}, u32[]{:S(2)}) collective-permute-start(f32[2,768]{1,0:T(2,128)S(1)} %end_n.1.after_ref), channel_id=1, source_target_pairs={{0,2},{1,3},{2,4},{3,5},{4,6},{5,7},{6,8},{7,9},{8,10},{9,11},{10,... | collective-permute-start | bytes 18440 | tf_op jit(solution)/shard_map/ppermute | solution.py:399
  51.5 8.1 %collective-permute-start.10 = (f32[2,768]{1,0:T(2,128)S(1)}, f32[2,768]{1,0:T(2,128)S(1)}, u32[]{:S(2)}, u32[]{:S(2)}) collective-permute-start(f32[2,768]{1,0:T(2,128)S(1)} %end_p.1), channel_id=1, source_target_pairs={{0,254},{1,255},{2,0},{3,1},{4,2},{5,3},{6,4},{7,5},{8,6},{9,7},{1... | collective-permute-start | bytes 18440 | tf_op jit(solution)/shard_map/ppermute | solution.py:399
